TPU v7x, 128 devices: a whole 4x4x4 slice. The times are simulated.
128 devices in a mesh: dp: 16 (over z, x), heads: 8 (over y, core).
Axes of the slice: x: 4, y: 4, z: 4, core: 2. Of those that a mesh axis runs over, the one named last changes fastest.
Arguments:
- tokens_in: bfloat16 [16384, 2048], P(('dp', 'heads')), may hold values from -6 to 6
- cotangent: bfloat16 [16384, 2048], P(('dp', 'heads')), may hold values from -7.2 to 7.2
- seg_starts: int32 [16, 4], P('dp'), may hold values from 0 to 1023, as said below
- gains: float32 [5120], replicated, may hold values from 0.47 to 2.61
- w_q_down: bfloat16 [2048, 1024], replicated, may hold values from -0.125 to 0.125
- w_key: bfloat16 [2048, 256], replicated, may hold values from -0.125 to 0.125
- w_value: bfloat16 [2048, 256], replicated, may hold values from -0.125 to 0.125
- w_q_up: bfloat16 [1024, 4096], P(None, 'heads'), may hold values from -0.1875 to 0.1875
- w_out: bfloat16 [2048, 4096], P(None, 'heads'), may hold values from -0.625 to 0.625
- w_gate: bfloat16 [2048, 5632], P(None, 'heads'), may hold values from -0.125 to 0.125
- w_up: bfloat16 [2048, 5632], P(None, 'heads'), may hold values from -0.125 to 0.125
- w_down: bfloat16 [2048, 5632], P(None, 'heads'), may hold values from -0.078125 to 0.078125
- mom_gains: float32 [5120], P(('dp', 'heads')), may hold values from -460.8 to 460.8
- mom_q_down: float32 [2048, 1024], P(('dp', 'heads')), may hold values from -368.64 to 368.64
- mom_key: float32 [2048, 256], P(('dp', 'heads')), may hold values from -829.44 to 829.44
- mom_value: float32 [2048, 256], P(('dp', 'heads')), may hold values from -921.6 to 921.6
- mom_q_up: float32 [1024, 4096], P('dp', 'heads'), may hold values from -184.32 to 184.32
- mom_out: float32 [2048, 4096], P('dp', 'heads'), may hold values from -92.16 to 92.16
- mom_gate: float32 [2048, 5632], P('dp', 'heads'), may hold values from -276.48 to 276.48
- mom_up: float32 [2048, 5632], P('dp', 'heads'), may hold values from -322.56 to 322.56
- mom_down: float32 [2048, 5632], P('dp', 'heads'), may hold values from -552.96 to 552.96
Outputs:
- layer_out: bfloat16 [16384, 2048], P(('dp', 'heads'))
- input_grad: float32 [16384, 2048], P(('dp', 'heads'))
- gains_grad: float32 [5120], P(('dp', 'heads'))
- q_down_grad: float32 [2048, 1024], P(('dp', 'heads'))
- key_w_grad: float32 [2048, 256], P(('dp', 'heads'))
- value_w_grad: float32 [2048, 256], P(('dp', 'heads'))
- q_up_grad: float32 [1024, 4096], P('dp', 'heads')
- out_w_grad: float32 [2048, 4096], P('dp', 'heads')
- gate_w_grad: float32 [2048, 5632], P('dp', 'heads')
- up_w_grad: float32 [2048, 5632], P('dp', 'heads')
- down_w_grad: float32 [2048, 5632], P('dp', 'heads')
- gains_mom: float32 [5120], P(('dp', 'heads'))
- q_down_mom: float32 [2048, 1024], P(('dp', 'heads'))
- key_w_mom: float32 [2048, 256], P(('dp', 'heads'))
- value_w_mom: float32 [2048, 256], P(('dp', 'heads'))
- q_up_mom: float32 [1024, 4096], P('dp', 'heads')
- out_w_mom: float32 [2048, 4096], P('dp', 'heads')
- gate_w_mom: float32 [2048, 5632], P('dp', 'heads')
- up_w_mom: float32 [2048, 5632], P('dp', 'heads')
- down_w_mom: float32 [2048, 5632], P('dp', 'heads')
- gains_new: float32 [5120], P(('dp', 'heads'))
- q_down_new: float32 [2048, 1024], P(('dp', 'heads'))
- key_w_new: float32 [2048, 256], P(('dp', 'heads'))
- value_w_new: float32 [2048, 256], P(('dp', 'heads'))
- q_up_new: float32 [1024, 4096], P('dp', 'heads')
- out_w_new: float32 [2048, 4096], P('dp', 'heads')
- gate_w_new: float32 [2048, 5632], P('dp', 'heads')
- up_w_new: float32 [2048, 5632], P('dp', 'heads')
- down_w_new: float32 [2048, 5632], P('dp', 'heads')
Inputs may be any that keep to these rules, and one draw needn't show every extreme that they name: `seg_starts`: in each row the entries rise strictly and the first is 0.
All inputs are finite; a program needn't handle non-finite values.
Results may differ from a plain program's by a relative error of at most 0.029.
Values may be sent and summed in bfloat16 or wider, within the bound.
No kernel may reach another device: no remote copies, remote signals or barrier semaphores. Data moves between devices by JAX's collectives and lax.ppermute only.
A program may use at most 192 MiB of HBM per device.

v0:
```python
import math

import jax
import jax.numpy as jnp
from jax import lax
from jax.sharding import PartitionSpec as P

NS_STEPS = 3
FF_BLOCK = 352


highest = lax.Precision.HIGHEST
coef_first = 3.4445
coef_second = -4.775
coef_third = 2.0315
muon_rate = 0.5
gain_rate = 0.004
decay_rate = 0.5


def matmul(left, right):
    return jnp.dot(left, right, preferred_element_type=jnp.float32)


def matmul_nt(left, right):
    return lax.dot_general(
        left, right, (((1,), (1,)), ((), ())), preferred_element_type=jnp.float32
    )


def matmul_tn(left, right):
    return lax.dot_general(
        left, right, (((0,), (0,)), ((), ())), preferred_element_type=jnp.float32
    )


def rms_scale(values):
    return lax.rsqrt(jnp.mean(values * values, axis=-1, keepdims=True) + 1e-05)


def norm_back(values, scale, gain, grad_out):
    weighted = gain * grad_out
    inner = jnp.mean(values * weighted, axis=-1, keepdims=True)
    grad_in = scale * weighted - values * (scale * scale * scale) * inner
    gain_grad = jnp.sum(grad_out * values * scale, axis=0)
    return (grad_in, gain_grad)


def segment_info(starts, token_index):
    started = starts[None, :] <= token_index[:, None]
    seg_ids = jnp.sum(started.astype(jnp.int32), axis=1)
    seg_begin = jnp.max(jnp.where(started, starts[None, :], 0), axis=1)
    return (seg_ids, token_index - seg_begin)


def rotary_tables(positions, head_dim):
    half_dim = head_dim // 2
    frequency = jnp.exp(
        jnp.arange(half_dim, dtype=jnp.float32) * (-2.0 * math.log(10000.0) / head_dim)
    )
    angles = positions.astype(jnp.float32)[:, None] * frequency[None, :]
    return (jnp.cos(angles), jnp.sin(angles))


def rotate(values, cosine, sine_part):
    half_dim = values.shape[-1] // 2
    first_half = values[..., :half_dim]
    second_half = values[..., half_dim:]
    return jnp.concatenate(
        [
            first_half * cosine - second_half * sine_part,
            second_half * cosine + first_half * sine_part,
        ],
        axis=-1,
    )


def rotate_back(grads, cosine, sine_part):
    half_dim = grads.shape[-1] // 2
    first_half = grads[..., :half_dim]
    second_half = grads[..., half_dim:]
    return jnp.concatenate(
        [
            first_half * cosine + second_half * sine_part,
            second_half * cosine - first_half * sine_part,
        ],
        axis=-1,
    )


def block_mask(row_ids, first_row, end_row):
    query_ids = row_ids[first_row:end_row]
    key_ids = row_ids[:end_row]
    query_at = jnp.arange(first_row, end_row, dtype=jnp.int32)[:, None]
    key_at = jnp.arange(end_row, dtype=jnp.int32)[None, :]
    return (query_ids[:, None] == key_ids[None, :]) & (key_at <= query_at)


def gram_of(blocks):
    return jnp.einsum("brc,brd->bcd", blocks, blocks, precision=highest)


def newton_step(blocks, gram_sums):
    first_term = jnp.einsum("brc,bcd->brd", blocks, gram_sums, precision=highest)
    second_term = jnp.einsum("brc,bcd->brd", first_term, gram_sums, precision=highest)
    return coef_first * blocks + coef_second * first_term + coef_third * second_term


def trace_start(blocks, gram_sums):
    trace_sum = jnp.sum(jnp.diagonal(gram_sums, axis1=1, axis2=2), axis=1)
    factor = 1.0 / (jnp.sqrt(trace_sum) + 1e-07)
    return (blocks * factor[:, None, None], gram_sums * (factor * factor)[:, None, None])


def block_squares(blocks):
    return jnp.sum(blocks * blocks, axis=(1, 2))


def split_columns(matrix, block_cols):
    row_count = matrix.shape[0]
    return matrix.reshape(row_count, matrix.shape[1] // block_cols, block_cols).transpose(1, 0, 2)


def join_columns(blocks):
    return blocks.transpose(1, 0, 2).reshape(blocks.shape[1], blocks.shape[0] * blocks.shape[2])


def head_sums(query_blocks, output_blocks, ffn_blocks):
    return (
        lax.psum(gram_of(query_blocks).astype(jnp.bfloat16), "dp").astype(jnp.float32),
        lax.psum(gram_of(output_blocks).astype(jnp.bfloat16), "dp").astype(jnp.float32),
        lax.psum(gram_of(ffn_blocks).astype(jnp.bfloat16), "dp").astype(jnp.float32),
    )


def shared_sums(latent_blocks, pair_blocks):
    return lax.psum((gram_of(latent_blocks), gram_of(pair_blocks)), ("dp", "heads"))


def own_rows(weight, count, rank):
    share_rows = weight.shape[0] // count
    return lax.dynamic_slice_in_dim(weight, rank * share_rows, share_rows, 0).astype(jnp.float32)


def on_device(
    tokens_in,
    cotangent,
    seg_starts,
    gains,
    w_q_down,
    w_key,
    w_value,
    w_q_up,
    w_out,
    w_gate,
    w_up,
    w_down,
    mom_gains,
    mom_q_down,
    mom_key,
    mom_value,
    mom_q_up,
    mom_out,
    mom_gate,
    mom_up,
    mom_down,
):
    heads_count = lax.axis_size("heads")
    heads_rank = lax.axis_index("heads")
    dp_count = lax.axis_size("dp")
    dp_rank = lax.axis_index("dp")
    all_rank = lax.axis_index(("dp", "heads"))
    all_count = dp_count * heads_count
    local_rows = tokens_in.shape[0]
    row_len = local_rows * heads_count
    model_width = tokens_in.shape[1]
    latent_width = w_q_down.shape[1]
    head_dim = w_key.shape[1]
    local_heads = w_q_up.shape[1] // head_dim
    score_scale = head_dim ** (-0.5)
    block_len = min(512, row_len)
    block_count = row_len // block_len
    starts = seg_starts[0]
    whole_index = jnp.arange(row_len, dtype=jnp.int32)
    own_index = heads_rank * local_rows + jnp.arange(local_rows, dtype=jnp.int32)
    gain_one = gains[:model_width]
    gain_latent = gains[model_width : model_width + latent_width]
    gain_two = gains[model_width + latent_width :]
    inputs = tokens_in.astype(jnp.float32)
    scale_one = rms_scale(inputs)
    normed_one = (inputs * scale_one * gain_one).astype(jnp.bfloat16)
    latent_raw = matmul(normed_one, w_q_down)
    scale_latent = rms_scale(latent_raw)
    latent_normed = (latent_raw * scale_latent * gain_latent).astype(jnp.bfloat16)
    own_pos = segment_info(starts, own_index)[1]
    own_cos, own_sin = rotary_tables(own_pos, head_dim)
    key_local = rotate(matmul(normed_one, w_key), own_cos, own_sin).astype(jnp.bfloat16)
    value_local = matmul(normed_one, w_value).astype(jnp.bfloat16)
    latent_rows, key_rows, value_rows = (
        lax.all_gather(latent_normed, "heads", axis=0, tiled=True),
        lax.all_gather(key_local, "heads", axis=0, tiled=True),
        lax.all_gather(value_local, "heads", axis=0, tiled=True),
    )
    row_ids, row_pos = segment_info(starts, whole_index)
    row_cos, row_sin = rotary_tables(row_pos, head_dim)
    query_pre = matmul(latent_rows, w_q_up).reshape(row_len, local_heads, head_dim)
    query_rows = rotate(query_pre, row_cos[:, None, :], row_sin[:, None, :]).astype(jnp.bfloat16)
    attended_blocks = []
    lse_blocks = []
    for block_index in range(block_count):
        first_row = block_index * block_len
        end_row = first_row + block_len
        allowed = block_mask(row_ids, first_row, end_row)
        scores = (
            jnp.einsum(
                "qhd,kd->hqk",
                query_rows[first_row:end_row],
                key_rows[:end_row],
                preferred_element_type=jnp.float32,
            )
            * score_scale
        )
        scores = jnp.where(allowed[None], scores, -1e30)
        row_max = jnp.max(scores, axis=-1, keepdims=True)
        exponent = jnp.exp(scores - row_max)
        row_total = jnp.sum(exponent, axis=-1, keepdims=True)
        attn_probs = (exponent / row_total).astype(jnp.bfloat16)
        lse_blocks.append(row_max + jnp.log(row_total))
        attended_blocks.append(
            jnp.einsum(
                "hqk,kd->qhd", attn_probs, value_rows[:end_row], preferred_element_type=jnp.float32
            )
        )
    attended = (
        jnp.concatenate(attended_blocks, axis=0)
        .astype(jnp.bfloat16)
        .reshape(row_len, local_heads * head_dim)
    )
    attn_mixed = lax.psum_scatter(
        matmul_nt(attended, w_out).astype(jnp.bfloat16), "heads", scatter_dimension=0, tiled=True
    ).astype(jnp.float32)
    hidden_one = inputs + attn_mixed
    scale_two = rms_scale(hidden_one)
    normed_two = (hidden_one * scale_two * gain_two).astype(jnp.bfloat16)
    ffn_input = lax.all_gather(normed_two, "heads", axis=0, tiled=True)
    gate_raw = matmul(ffn_input, w_gate)
    up_raw = matmul(ffn_input, w_up)
    sigmoid_gate = jax.nn.sigmoid(gate_raw)
    activated = gate_raw * sigmoid_gate
    hidden_mid = (activated * up_raw).astype(jnp.bfloat16)
    ffn_mixed = lax.psum_scatter(
        matmul_nt(hidden_mid, w_down).astype(jnp.bfloat16), "heads", scatter_dimension=0, tiled=True
    ).astype(jnp.float32)
    layer_out = (hidden_one + ffn_mixed).astype(jnp.bfloat16)
    grad_rows = lax.all_gather(cotangent, "heads", axis=0, tiled=True)
    mid_back = matmul(grad_rows, w_down)
    down_w_part = matmul_tn(grad_rows, hidden_mid)
    gate_back = (mid_back * up_raw * sigmoid_gate * (1.0 + gate_raw * (1.0 - sigmoid_gate))).astype(
        jnp.bfloat16
    )
    up_back = (mid_back * activated).astype(jnp.bfloat16)
    gate_w_part = matmul_tn(ffn_input, gate_back)
    up_w_part = matmul_tn(ffn_input, up_back)
    normed_two_back = lax.psum_scatter(
        (matmul_nt(gate_back, w_gate) + matmul_nt(up_back, w_up)).astype(jnp.bfloat16),
        "heads",
        scatter_dimension=0,
        tiled=True,
    ).astype(jnp.float32)
    hidden_part, gain_two_grad = norm_back(hidden_one, scale_two, gain_two, normed_two_back)
    hidden_back = cotangent.astype(jnp.float32) + hidden_part
    hidden_rows = lax.all_gather(hidden_back.astype(jnp.bfloat16), "heads", axis=0, tiled=True)
    attended_back = matmul(hidden_rows, w_out).astype(jnp.bfloat16)
    out_w_part = matmul_tn(hidden_rows, attended)
    attended_back = attended_back.reshape(row_len, local_heads, head_dim)
    key_back = jnp.zeros((row_len, head_dim), jnp.float32)
    value_back = jnp.zeros((row_len, head_dim), jnp.float32)
    query_back_blocks = []
    for block_index in range(block_count):
        first_row = block_index * block_len
        end_row = first_row + block_len
        query_block = query_rows[first_row:end_row]
        keys_seen = key_rows[:end_row]
        values_seen = value_rows[:end_row]
        back_block = attended_back[first_row:end_row]
        allowed = block_mask(row_ids, first_row, end_row)
        scores = (
            jnp.einsum("qhd,kd->hqk", query_block, keys_seen, preferred_element_type=jnp.float32)
            * score_scale
        )
        scores = jnp.where(allowed[None], scores, -1e30)
        attn_probs = jnp.exp(scores - lse_blocks[block_index])
        probs_back = jnp.einsum(
            "qhd,kd->hqk", back_block, values_seen, preferred_element_type=jnp.float32
        )
        inner = jnp.sum(attn_probs * probs_back, axis=-1, keepdims=True)
        score_back = (attn_probs * (probs_back - inner)).astype(jnp.bfloat16)
        query_back_blocks.append(
            jnp.einsum("hqk,kd->qhd", score_back, keys_seen, preferred_element_type=jnp.float32)
            * score_scale
        )
        key_back = key_back.at[:end_row].add(
            jnp.einsum("hqk,qhd->kd", score_back, query_block, preferred_element_type=jnp.float32)
            * score_scale
        )
        value_back = value_back.at[:end_row].add(
            jnp.einsum(
                "hqk,qhd->kd",
                attn_probs.astype(jnp.bfloat16),
                back_block,
                preferred_element_type=jnp.float32,
            )
        )
    query_back = jnp.concatenate(query_back_blocks, axis=0)
    query_back = (
        rotate_back(query_back, row_cos[:, None, :], row_sin[:, None, :])
        .astype(jnp.bfloat16)
        .reshape(row_len, local_heads * head_dim)
    )
    q_up_part = matmul_tn(latent_rows, query_back)
    latent_part = matmul_nt(query_back, w_q_up)
    latent_back, key_sum, value_sum = (
        lax.psum_scatter(
            latent_part.astype(jnp.bfloat16), "heads", scatter_dimension=0, tiled=True
        ).astype(jnp.float32),
        lax.psum_scatter(
            key_back.astype(jnp.bfloat16), "heads", scatter_dimension=0, tiled=True
        ).astype(jnp.float32),
        lax.psum_scatter(
            value_back.astype(jnp.bfloat16), "heads", scatter_dimension=0, tiled=True
        ).astype(jnp.float32),
    )
    latent_raw_grad, gain_latent_grad = norm_back(
        latent_raw, scale_latent, gain_latent, latent_back
    )
    latent_raw_back = latent_raw_grad.astype(jnp.bfloat16)
    key_pre_back = rotate_back(key_sum, own_cos, own_sin).astype(jnp.bfloat16)
    values_low = value_sum.astype(jnp.bfloat16)
    normed_one_back = (
        matmul_nt(latent_raw_back, w_q_down)
        + matmul_nt(key_pre_back, w_key)
        + matmul_nt(values_low, w_value)
    )
    input_part, gain_one_grad = norm_back(inputs, scale_one, gain_one, normed_one_back)
    input_grad = hidden_back + input_part
    q_down_part = matmul_tn(normed_one, latent_raw_back)
    key_w_part = matmul_tn(normed_one, key_pre_back)
    value_w_part = matmul_tn(normed_one, values_low)
    gains_part = jnp.concatenate([gain_one_grad, gain_latent_grad, gain_two_grad])
    q_down_grad, key_w_grad, value_w_grad, gains_grad = (
        lax.psum_scatter(q_down_part, ("dp", "heads"), scatter_dimension=0, tiled=True),
        lax.psum_scatter(key_w_part, ("dp", "heads"), scatter_dimension=0, tiled=True),
        lax.psum_scatter(value_w_part, ("dp", "heads"), scatter_dimension=0, tiled=True),
        lax.psum_scatter(gains_part, ("dp", "heads"), scatter_dimension=0, tiled=True),
    )
    late_sums = (
        lax.psum_scatter(
            q_up_part.astype(jnp.bfloat16), "dp", scatter_dimension=0, tiled=True
        ).astype(jnp.float32),
        lax.psum_scatter(
            out_w_part.astype(jnp.bfloat16), "dp", scatter_dimension=0, tiled=True
        ).astype(jnp.float32),
        lax.psum_scatter(
            gate_w_part.astype(jnp.bfloat16), "dp", scatter_dimension=0, tiled=True
        ).astype(jnp.float32),
        lax.psum_scatter(
            up_w_part.astype(jnp.bfloat16), "dp", scatter_dimension=0, tiled=True
        ).astype(jnp.float32),
        lax.psum_scatter(
            down_w_part.astype(jnp.bfloat16), "dp", scatter_dimension=0, tiled=True
        ).astype(jnp.float32),
    )
    q_up_grad = late_sums[0]
    out_w_grad = late_sums[1]
    gate_w_grad, up_w_grad, down_w_grad = (late_sums[2], late_sums[3], late_sums[4])
    gains_mom = decay_rate * mom_gains + gains_grad
    q_down_mom = decay_rate * mom_q_down + q_down_grad
    key_w_mom = decay_rate * mom_key + key_w_grad
    value_w_mom = decay_rate * mom_value + value_w_grad
    q_up_mom = decay_rate * mom_q_up + q_up_grad
    out_w_mom = decay_rate * mom_out + out_w_grad
    gate_w_mom = decay_rate * mom_gate + gate_w_grad
    up_w_mom = decay_rate * mom_up + up_w_grad
    down_w_mom = decay_rate * mom_down + down_w_grad
    gains_new = own_rows(gains, all_count, all_rank) - gain_rate * gains_mom
    ffn_count = w_gate.shape[1] // FF_BLOCK
    head_blocks = (
        split_columns(q_up_mom, head_dim),
        split_columns(out_w_mom, head_dim),
        jnp.concatenate(
            [
                split_columns(gate_w_mom, FF_BLOCK),
                split_columns(up_w_mom, FF_BLOCK),
                split_columns(down_w_mom, FF_BLOCK),
            ],
            axis=0,
        ),
    )
    shared_blocks = (q_down_mom[None], jnp.stack([key_w_mom, value_w_mom]))
    first_shared = shared_sums(shared_blocks[0], shared_blocks[1])
    shared_pairs = [
        trace_start(blocks, gram_sums) for blocks, gram_sums in zip(shared_blocks, first_shared)
    ]
    shared_iter = tuple((pair_item[0] for pair_item in shared_pairs))
    shared_grams = tuple((pair_item[1] for pair_item in shared_pairs))
    for step_index in range(NS_STEPS):
        if step_index > 0:
            shared_grams = shared_sums(shared_iter[0], shared_iter[1])
        shared_iter = tuple(
            (newton_step(blocks, gram_sums) for blocks, gram_sums in zip(shared_iter, shared_grams))
        )
    square_sums = lax.psum(
        (
            block_squares(head_blocks[0]),
            block_squares(head_blocks[1]),
            block_squares(head_blocks[2]),
        ),
        "dp",
    )
    head_iter = tuple(
        (
            blocks / (jnp.sqrt(squares)[:, None, None] + 1e-07)
            for blocks, squares in zip(head_blocks, square_sums)
        )
    )
    head_grams = head_sums(head_iter[0], head_iter[1], head_iter[2])
    for step_index in range(NS_STEPS):
        if step_index > 0:
            head_grams = head_sums(head_iter[0], head_iter[1], head_iter[2])
        head_iter = tuple(
            (newton_step(blocks, gram_sums) for blocks, gram_sums in zip(head_iter, head_grams))
        )
    query_ortho, output_ortho, ffn_ortho = head_iter
    q_up_new = own_rows(w_q_up, dp_count, dp_rank) - muon_rate * math.sqrt(
        w_q_up.shape[0] / head_dim
    ) * join_columns(query_ortho)
    out_w_new = own_rows(w_out, dp_count, dp_rank) - muon_rate * math.sqrt(
        w_out.shape[0] / head_dim
    ) * join_columns(output_ortho)
    ffn_factor = muon_rate * math.sqrt(w_gate.shape[0] / FF_BLOCK)
    gate_w_new = own_rows(w_gate, dp_count, dp_rank) - ffn_factor * join_columns(
        ffn_ortho[:ffn_count]
    )
    up_w_new = own_rows(w_up, dp_count, dp_rank) - ffn_factor * join_columns(
        ffn_ortho[ffn_count : 2 * ffn_count]
    )
    down_w_new = own_rows(w_down, dp_count, dp_rank) - ffn_factor * join_columns(
        ffn_ortho[2 * ffn_count :]
    )
    q_down_new = (
        own_rows(w_q_down, all_count, all_rank)
        - muon_rate * math.sqrt(w_q_down.shape[0] / latent_width) * shared_iter[0][0]
    )
    pair_factor = muon_rate * math.sqrt(w_key.shape[0] / head_dim)
    key_w_new = own_rows(w_key, all_count, all_rank) - pair_factor * shared_iter[1][0]
    value_w_new = own_rows(w_value, all_count, all_rank) - pair_factor * shared_iter[1][1]
    return (
        layer_out,
        input_grad,
        gains_grad,
        q_down_grad,
        key_w_grad,
        value_w_grad,
        q_up_grad,
        out_w_grad,
        gate_w_grad,
        up_w_grad,
        down_w_grad,
        gains_mom,
        q_down_mom,
        key_w_mom,
        value_w_mom,
        q_up_mom,
        out_w_mom,
        gate_w_mom,
        up_w_mom,
        down_w_mom,
        gains_new,
        q_down_new,
        key_w_new,
        value_w_new,
        q_up_new,
        out_w_new,
        gate_w_new,
        up_w_new,
        down_w_new,
    )


def solution(mesh):
    placed = (
        P(("dp", "heads"), None),
        P(("dp", "heads"), None),
        P("dp", None),
        P(),
        P(),
        P(),
        P(),
        P(None, "heads"),
        P(None, "heads"),
        P(None, "heads"),
        P(None, "heads"),
        P(None, "heads"),
        P(("dp", "heads")),
        P(("dp", "heads"), None),
        P(("dp", "heads"), None),
        P(("dp", "heads"), None),
        P("dp", "heads"),
        P("dp", "heads"),
        P("dp", "heads"),
        P("dp", "heads"),
        P("dp", "heads"),
    )
    return jax.shard_map(
        on_device,
        mesh=mesh,
        in_specs=placed,
        out_specs=(
            P(("dp", "heads"), None),
            P(("dp", "heads"), None),
            P(("dp", "heads")),
            P(("dp", "heads"), None),
            P(("dp", "heads"), None),
            P(("dp", "heads"), None),
            P("dp", "heads"),
            P("dp", "heads"),
            P("dp", "heads"),
            P("dp", "heads"),
            P("dp", "heads"),
            P(("dp", "heads")),
            P(("dp", "heads"), None),
            P(("dp", "heads"), None),
            P(("dp", "heads"), None),
            P("dp", "heads"),
            P("dp", "heads"),
            P("dp", "heads"),
            P("dp", "heads"),
            P("dp", "heads"),
            P(("dp", "heads")),
            P(("dp", "heads"), None),
            P(("dp", "heads"), None),
            P(("dp", "heads"), None),
            P("dp", "heads"),
            P("dp", "heads"),
            P("dp", "heads"),
            P("dp", "heads"),
            P("dp", "heads"),
        ),
        check_vma=False,
    )
```

profile of v0, /device:TPU:1, one launch (start us, length us, event | category | flops | bytes accessed | tf_op | source)
XLA Modules:
  0.0 3515.6 jit_solution(6600696660348235303)
XLA Ops:
  17.6 16.1 all_gather.19
  34.0 14.9 all_gather.18
  75.5 36.6 %reduce-scatter.21.cloned.1.call-done = bf16[128,2048]{1,0:T(8,128)(2,1)} async-done(((bf16[1024,2048]{1,0:T(8,128)(2,1)}), bf16[128,2048]{1,0:T(8,128)(2,1)}) %reduce-scatter.21.cloned.1.call-update) | async-done | bytes 524304 | tf_op jit(solution)/shard_map/reduce_scatter | solution.py:239
  116.3 33.7 all-gather.7.cloned.1.call-done
  162.7 21.0 all-gather.9.cloned.1.call-done
  203.1 34.6 reduce-scatter.25.cloned.1.call-done
  323.4 30.7 reduce-scatter.43.cloned.1.call-done
  355.3 77.4 %reduce-scatter.45.cloned.1.call-done = bf16[128,704]{1,0:T(8,128)(2,1)} async-done(((bf16[2048,704]{1,0:T(8,128)(2,1)}), bf16[128,704]{1,0:T(8,128)(2,1)}) %reduce-scatter.45.cloned.1.call-update) | async-done | bytes 180240
  433.8 77.4 %reduce-scatter.47.cloned.1.call-done = bf16[128,704]{1,0:T(8,128)(2,1)} async-done(((bf16[2048,704]{1,0:T(8,128)(2,1)}), bf16[128,704]{1,0:T(8,128)(2,1)}) %reduce-scatter.47.cloned.1.call-update) | async-done | bytes 180240
  518.5 68.1 %reduce-scatter.39.cloned.1.call-done = bf16[64,512]{1,0:T(8,128)(2,1)} async-done(((bf16[1024,512]{1,0:T(8,128)(2,1)}), bf16[64,512]{1,0:T(8,128)(2,1)}) %reduce-scatter.39.cloned.1.call-update) | async-done | bytes 65552 | tf_op jit(solution)/shard_map/reduce_scatter | solution.py:357
  588.4 75.6 %reduce-scatter.41.cloned.1.call-done = bf16[128,512]{1,0:T(8,128)(2,1)} async-done(((bf16[2048,512]{1,0:T(8,128)(2,1)}), bf16[128,512]{1,0:T(8,128)(2,1)}) %reduce-scatter.41.cloned.1.call-update) | async-done | bytes 131088 | tf_op jit(solution)/shard_map/reduce_scatter | solution.py:360
  668.5 31.5 all-reduce.6
  731.8 31.5 reduce-scatter.27.cloned.1.call-done
  771.4 87.7 %all-reduce.27.cloned.1.call-done = (bf16[2,256,256]{2,1,0:T(8,128)(2,1)}, bf16[2,256,256]{2,1,0:T(8,128)(2,1)}, bf16[6,352,352]{2,1,0:T(8,128)(2,1)}) async-done(((bf16[2,256,256]{2,1,0:T(8,128)(2,1)}, bf16[2,256,256]{2,1,0:T(8,128)(2,1)}, bf16[6,352,352]{2,1,0:T(8,128)(2,1)}), (bf16[2,256,256]{2,1,0:T(8,128)(2,1)}, bf16[2,256,256]{2,1,0:T(8,128)(2,1)}, ...) | async-done | bytes 2011152 | tf_op jit(solution)/shard_map/psum | solution.py:130
  876.7 618.9 %reduce-scatter.35.cloned.1.call-done = f32[16,256]{1,0:T(8,128)} async-done(((f32[2048,256]{1,0:T(8,128)}), f32[16,256]{1,0:T(8,128)}) %reduce-scatter.35.cloned.1.call-update) | async-done | bytes 16400 | tf_op jit(solution)/shard_map/reduce_scatter | solution.py:352
  1496.4 635.7 %reduce-scatter.37.cloned.1.call-done = f32[16,256]{1,0:T(8,128)} async-done(((f32[2048,256]{1,0:T(8,128)}), f32[16,256]{1,0:T(8,128)}) %reduce-scatter.37.cloned.1.call-update) | async-done | bytes 16400 | tf_op jit(solution)/shard_map/reduce_scatter | solution.py:353
  2134.2 644.6 %reduce-scatter.33.cloned.1.call-done = f32[16,1024]{1,0:T(8,128)} async-done(((f32[2048,1024]{1,0:T(8,128)}), f32[16,1024]{1,0:T(8,128)}) %reduce-scatter.33.cloned.1.call-update) | async-done | bytes 65552 | tf_op jit(solution)/shard_map/reduce_scatter | solution.py:351
  2793.8 79.5 %all-reduce.25.cloned.1.call-done = (bf16[2,256,256]{2,1,0:T(8,128)(2,1)}, bf16[2,256,256]{2,1,0:T(8,128)(2,1)}, bf16[6,352,352]{2,1,0:T(8,128)(2,1)}) async-done(((bf16[2,256,256]{2,1,0:T(8,128)(2,1)}, bf16[2,256,256]{2,1,0:T(8,128)(2,1)}, bf16[6,352,352]{2,1,0:T(8,128)(2,1)}), (bf16[2,256,256]{2,1,0:T(8,128)(2,1)}, bf16[2,256,256]{2,1,0:T(8,128)(2,1)}, ...) | async-done | bytes 2011152 | tf_op jit(solution)/shard_map/psum | solution.py:130
  2892.9 142.7 %all-reduce.21.cloned.1.call-done = (f32[1,1024,1024]{2,1,0:T(8,128)}, f32[2,256,256]{2,1,0:T(8,128)}) async-done(((f32[1,1024,1024]{2,1,0:T(8,128)}, f32[2,256,256]{2,1,0:T(8,128)}), (f32[1,1024,1024]{2,1,0:T(8,128)}, f32[2,256,256]{2,1,0:T(8,128)})) %all-reduce.21.cloned.1.call-update) | async-done | bytes 4718608 | tf_op jit(solution)/shard_map/psum | solution.py:137
  3035.7 21.6 gather_fusion
  3059.3 17.4 copy.161
  3106.2 65.1 %all-reduce.2 = f32[5120]{0:T(1024)S(1)} all-reduce(f32[5120]{0:T(1024)S(1)} %pad_maximum_fusion.16), channel_id=8, replica_groups=mesh['dp'=16,'heads'=8] {'dp','heads'}, use_global_device_ids=true, to_apply=%region_24.25.clone | all-reduce | flops 5120 | bytes 40960
  3180.9 148.5 %all-reduce.19.cloned.1.call-done = (f32[1024,1024]{1,0:T(8,128)}, f32[2,256,256]{2,1,0:T(8,128)}) async-done(((f32[1024,1024]{1,0:T(8,128)}, f32[2,256,256]{2,1,0:T(8,128)}), (f32[1024,1024]{1,0:T(8,128)}, f32[2,256,256]{2,1,0:T(8,128)})) %all-reduce.19.cloned.1.call-update) | async-done | bytes 4718608 | tf_op jit(solution)/shard_map/psum | solution.py:137
  3361.0 136.4 %all-reduce.17.cloned.1.call-done = (f32[1024,1024]{1,0:T(8,128)}, f32[2,256,256]{2,1,0:T(8,128)}) async-done(((f32[1024,1024]{1,0:T(8,128)}, f32[2,256,256]{2,1,0:T(8,128)}), (f32[1024,1024]{1,0:T(8,128)}, f32[2,256,256]{2,1,0:T(8,128)})) %all-reduce.17.cloned.1.call-update) | async-done | bytes 4718608 | tf_op jit(solution)/shard_map/psum | solution.py:137
  (451 shorter events, 351.5 us)
Async XLA Ops:
  7.2 46.3 %all-gather.5.cloned.1.call-start = ((), (), s32[]{:S(2)}) async-start(), calls=%async_computation.14 | async-start | bytes 2359296 | tf_op jit(solution)/shard_map/all_gather | solution.py:200
  15.3 96.8 %reduce-scatter.21.cloned.1.call-start = ((), (), s32[]{:S(2)}) async-start(), calls=%async_computation.15 | async-start | bytes 4718592 | tf_op jit(solution)/shard_map/reduce_scatter | solution.py:239
  75.4 74.6 %all-gather.7.cloned.1.call-start = ((), (), s32[]{:S(2)}) async-start(), calls=%async_computation.16 | async-start | bytes 4718592 | tf_op jit(solution)/shard_map/all_gather | solution.py:245
  115.5 68.2 %all-gather.9.cloned.1.call-start = ((), (), s32[]{:S(2)}) async-start(), calls=%async_computation.18 | async-start | bytes 4718592 | tf_op jit(solution)/shard_map/all_gather | solution.py:255
  116.1 121.7 %reduce-scatter.25.cloned.1.call-start = ((), (), s32[]{:S(2)}) async-start(), calls=%async_computation.19 | async-start | bytes 4718592 | tf_op jit(solution)/shard_map/reduce_scatter | solution.py:264
  203.0 76.7 %all-gather.11.cloned.1.call-start = ((), (), s32[]{:S(2)}) async-start(), calls=%async_computation.20 | async-start | bytes 4718592 | tf_op jit(solution)/shard_map/all_gather | solution.py:272
  242.5 111.6 %reduce-scatter.43.cloned.1.call-start = ((), (), s32[]{:S(2)}) async-start(), calls=%async_computation.29 | async-start | bytes 3342336
  254.6 178.1 %reduce-scatter.45.cloned.1.call-start = ((), (), s32[]{:S(2)}) async-start(), calls=%async_computation.30 | async-start | bytes 3342336
  267.0 244.1 %reduce-scatter.47.cloned.1.call-start = ((), (), s32[]{:S(2)}) async-start(), calls=%async_computation.31 | async-start | bytes 3342336
  279.2 307.3 %reduce-scatter.39.cloned.1.call-start = ((), (), s32[]{:S(2)}) async-start(), calls=%async_computation.27 | async-start | bytes 1114112 | tf_op jit(solution)/shard_map/reduce_scatter | solution.py:357
  301.6 362.4 %reduce-scatter.41.cloned.1.call-start = ((), (), s32[]{:S(2)}) async-start(), calls=%async_computation.28 | async-start | bytes 2228224 | tf_op jit(solution)/shard_map/reduce_scatter | solution.py:360
  308.0 402.5 %reduce-scatter.29.cloned.1.call-start = ((), (), s32[]{:S(2)}) async-start(), calls=%async_computation.22 | async-start | bytes 589824 | tf_op jit(solution)/shard_map/reduce_scatter | solution.py:326
  313.0 415.7 %reduce-scatter.31.cloned.1.call-start = ((), (), s32[]{:S(2)}) async-start(), calls=%async_computation.23 | async-start | bytes 589824 | tf_op jit(solution)/shard_map/reduce_scatter | solution.py:329
  319.2 444.1 %reduce-scatter.27.cloned.1.call-start = ((), (), s32[]{:S(2)}) async-start(), calls=%async_computation.21 | async-start | bytes 2359296 | tf_op jit(solution)/shard_map/reduce_scatter | solution.py:323
  323.4 535.6 %all-reduce.27.cloned.1.call-start = ((), (), s32[]{:S(2)}) async-start(), calls=%async_computation.37 | async-start | bytes 4292608 | tf_op jit(solution)/shard_map/psum | solution.py:130
  710.5 785.2 %reduce-scatter.35.cloned.1.call-start = ((), (), s32[]{:S(2)}) async-start(), calls=%async_computation.25 | async-start | bytes 2113536 | tf_op jit(solution)/shard_map/reduce_scatter | solution.py:352
  714.9 1417.2 %reduce-scatter.37.cloned.1.call-start = ((), (), s32[]{:S(2)}) async-start(), calls=%async_computation.26 | async-start | bytes 2113536 | tf_op jit(solution)/shard_map/reduce_scatter | solution.py:353
  731.5 2047.3 %reduce-scatter.33.cloned.1.call-start = ((), (), s32[]{:S(2)}) async-start(), calls=%async_computation.24 | async-start | bytes 8454144 | tf_op jit(solution)/shard_map/reduce_scatter | solution.py:351
  771.3 2102.0 %all-reduce.25.cloned.1.call-start = ((), (), s32[]{:S(2)}) async-start(), calls=%async_computation.36 | async-start | bytes 4292608 | tf_op jit(solution)/shard_map/psum | solution.py:130
  876.7 2159.0 %all-reduce.21.cloned.1.call-start = ((), (), s32[]{:S(2)}) async-start(), calls=%async_computation.34 | async-start | bytes 9437184 | tf_op jit(solution)/shard_map/psum | solution.py:137
  2784.8 388.5 %reduce-scatter.23.cloned.1.call-start = ((), (), s32[]{:S(2)}) async-start(), calls=%async_computation.17 | async-start | bytes 4718592 | tf_op jit(solution)/shard_map/reduce_scatter | solution.py:251
  2793.0 384.2 %all-reduce.23.cloned.1.call-start = ((), (), s32[]{:S(2)}) async-start(), calls=%async_computation.35 | async-start | bytes 4292608 | tf_op jit(solution)/shard_map/psum | solution.py:130
  2890.0 439.4 %all-reduce.19.cloned.1.call-start = ((), (), s32[]{:S(2)}) async-start(), calls=%async_computation.33 | async-start | bytes 9437184 | tf_op jit(solution)/shard_map/psum | solution.py:137
  3098.6 398.8 %all-reduce.17.cloned.1.call-start = ((), (), s32[]{:S(2)}) async-start(), calls=%async_computation.32 | async-start | bytes 9437184 | tf_op jit(solution)/shard_map/psum | solution.py:137
  (115 other events, 6290.8 us)
Sparse Core Ops, SparseCore 0:
  15.4 28.7 all-gather.4
  75.6 36.5 reduce-scatter.20
  115.6 34.3 all-gather.6
  151.6 32.0 all-gather.8
  203.2 34.5 reduce-scatter.24
  242.7 34.2 all-gather.10
  280.3 73.8 reduce-scatter.42
  357.5 75.1 reduce-scatter.44
  436.0 75.0 reduce-scatter.46
  514.2 72.2 reduce-scatter.38
  590.2 73.8 reduce-scatter.40
  666.8 29.3 reduce-scatter.28
  699.3 29.4 reduce-scatter.30
  731.0 32.2 reduce-scatter.26
  767.5 91.4 all-reduce.26
  861.9 633.7 reduce-scatter.34
  1498.4 633.6 reduce-scatter.36
  2135.0 643.7 reduce-scatter.32
  2783.2 90.1 all-reduce.24
  2879.6 156.0 all-reduce.20
  3038.2 33.2 reduce-scatter.22
  3076.3 92.1 all-reduce.22
  3173.6 155.7 all-reduce.18
  3343.5 153.8 all-reduce.16
where the time goes:
time: 3520 us
  waiting for transfers between devices  3000 us (85%)
  matrix products  229 us (7%)
  blocking collectives  128 us (4%)
  local copies, waits for them, and re-layouts  88 us (2%)
  other arithmetic  56.3 us (2%)
    reduce_scatter x1, waiting for transfers between devices, on_device(): lax.psum_scatter(q_down_part, ('dp', 'heads'), scatter_dimension=0, tiled...  645 us
    reduce_scatter x1, waiting for transfers between devices, on_device(): lax.psum_scatter(value_w_part, ('dp', 'heads'), scatter_dimension=0, tile...  636 us
    reduce_scatter x1, waiting for transfers between devices, on_device(): lax.psum_scatter(key_w_part, ('dp', 'heads'), scatter_dimension=0, tiled=...  619 us
    psum x3, waiting for transfers between devices, shared_sums(): lax.psum((gram_of(latent_blocks), gram_of(pair_blocks)), ('dp', 'heads'))  428 us
    unnamed x27, waiting for transfers between devices  186 us
    psum x3, waiting for transfers between devices, head_sums(): lax.psum(gram_of(query_blocks).astype(jnp.bfloat16), 'dp')  167 us
    reduce_scatter x1, waiting for transfers between devices, on_device(): lax.psum_scatter(out_w_part.astype(jnp.bfloat16), 'dp', scatter_dimension...  75.6 us
  transfers between devices with their start and end apart: 24, of which 19 were waited for; matrix products, arithmetic and copies ran while one was open for 8% of the time, Pallas kernels for 0%

commit v1 on v0

--- a/solution.py
+++ b/solution.py
@@ -9,7 +9,6 @@
 FF_BLOCK = 352
 
 
-highest = lax.Precision.HIGHEST
 coef_first = 3.4445
 coef_second = -4.775
 coef_third = 2.0315
@@ -97,23 +96,35 @@
 
 
 def gram_of(blocks):
-    return jnp.einsum("brc,brd->bcd", blocks, blocks, precision=highest)
-
-
-def newton_step(blocks, gram_sums):
-    first_term = jnp.einsum("brc,bcd->brd", blocks, gram_sums, precision=highest)
-    second_term = jnp.einsum("brc,bcd->brd", first_term, gram_sums, precision=highest)
-    return coef_first * blocks + coef_second * first_term + coef_third * second_term
-
-
-def trace_start(blocks, gram_sums):
-    trace_sum = jnp.sum(jnp.diagonal(gram_sums, axis1=1, axis2=2), axis=1)
+    low = blocks.astype(jnp.bfloat16)
+    return jnp.einsum("brc,brd->bcd", low, low, preferred_element_type=jnp.float32)
+
+
+def times(left, right):
+    return jnp.einsum(
+        "brc,bcd->brd",
+        left.astype(jnp.bfloat16),
+        right.astype(jnp.bfloat16),
+        preferred_element_type=jnp.float32,
+    )
+
+
+def orthogonal(blocks, gram_sums):
+    diagonal = jnp.eye(gram_sums.shape[-1], dtype=jnp.bool_)
+    trace_sum = jnp.sum(jnp.where(diagonal, gram_sums, 0.0), axis=(1, 2))
     factor = 1.0 / (jnp.sqrt(trace_sum) + 1e-07)
-    return (blocks * factor[:, None, None], gram_sums * (factor * factor)[:, None, None])
-
-
-def block_squares(blocks):
-    return jnp.sum(blocks * blocks, axis=(1, 2))
+    iterate = blocks * factor[:, None, None]
+    gram = gram_sums * (factor * factor)[:, None, None]
+    for step_index in range(NS_STEPS):
+        first_term = times(iterate, gram)
+        second_term = times(first_term, gram)
+        iterate = coef_first * iterate + coef_second * first_term + coef_third * second_term
+        if step_index + 1 < NS_STEPS:
+            change = coef_second * gram + coef_third * times(gram, gram)
+            once = times(gram, change)
+            twice = times(once, change)
+            gram = (coef_first * coef_first) * gram + (2.0 * coef_first) * once + twice
+    return iterate
 
 
 def split_columns(matrix, block_cols):
@@ -123,18 +134,6 @@
 
 def join_columns(blocks):
     return blocks.transpose(1, 0, 2).reshape(blocks.shape[1], blocks.shape[0] * blocks.shape[2])
-
-
-def head_sums(query_blocks, output_blocks, ffn_blocks):
-    return (
-        lax.psum(gram_of(query_blocks).astype(jnp.bfloat16), "dp").astype(jnp.float32),
-        lax.psum(gram_of(output_blocks).astype(jnp.bfloat16), "dp").astype(jnp.float32),
-        lax.psum(gram_of(ffn_blocks).astype(jnp.bfloat16), "dp").astype(jnp.float32),
-    )
-
-
-def shared_sums(latent_blocks, pair_blocks):
-    return lax.psum((gram_of(latent_blocks), gram_of(pair_blocks)), ("dp", "heads"))
 
 
 def own_rows(weight, count, rank):
@@ -196,10 +195,21 @@
     own_cos, own_sin = rotary_tables(own_pos, head_dim)
     key_local = rotate(matmul(normed_one, w_key), own_cos, own_sin).astype(jnp.bfloat16)
     value_local = matmul(normed_one, w_value).astype(jnp.bfloat16)
-    latent_rows, key_rows, value_rows = (
-        lax.all_gather(latent_normed, "heads", axis=0, tiled=True),
-        lax.all_gather(key_local, "heads", axis=0, tiled=True),
-        lax.all_gather(value_local, "heads", axis=0, tiled=True),
+    packed_rows = lax.all_gather(
+        jnp.concatenate([latent_normed, key_local, value_local], axis=1), "heads", axis=0, tiled=True
+    )
+    latent_rows = packed_rows[:, :latent_width]
+    key_rows = packed_rows[:, latent_width : latent_width + head_dim]
+    value_rows = packed_rows[:, latent_width + head_dim :]
+    share_rows = model_width // all_count
+    normed_parts = lax.all_to_all(
+        normed_one.reshape(local_rows, dp_count, heads_count, share_rows)
+        .transpose(2, 0, 1, 3)
+        .reshape(heads_count * local_rows, dp_count * share_rows),
+        "heads",
+        split_axis=0,
+        concat_axis=0,
+        tiled=True,
     )
     row_ids, row_pos = segment_info(starts, whole_index)
     row_cos, row_sin = rotary_tables(row_pos, head_dim)
@@ -259,8 +269,7 @@
         jnp.bfloat16
     )
     up_back = (mid_back * activated).astype(jnp.bfloat16)
-    gate_w_part = matmul_tn(ffn_input, gate_back)
-    up_w_part = matmul_tn(ffn_input, up_back)
+    gate_up_part = matmul_tn(ffn_input, jnp.concatenate([gate_back, up_back], axis=1))
     normed_two_back = lax.psum_scatter(
         (matmul_nt(gate_back, w_gate) + matmul_nt(up_back, w_up)).astype(jnp.bfloat16),
         "heads",
@@ -319,17 +328,15 @@
     )
     q_up_part = matmul_tn(latent_rows, query_back)
     latent_part = matmul_nt(query_back, w_q_up)
-    latent_back, key_sum, value_sum = (
-        lax.psum_scatter(
-            latent_part.astype(jnp.bfloat16), "heads", scatter_dimension=0, tiled=True
-        ).astype(jnp.float32),
-        lax.psum_scatter(
-            key_back.astype(jnp.bfloat16), "heads", scatter_dimension=0, tiled=True
-        ).astype(jnp.float32),
-        lax.psum_scatter(
-            value_back.astype(jnp.bfloat16), "heads", scatter_dimension=0, tiled=True
-        ).astype(jnp.float32),
-    )
+    packed_sums = lax.psum_scatter(
+        jnp.concatenate([latent_part, key_back, value_back], axis=1).astype(jnp.bfloat16),
+        "heads",
+        scatter_dimension=0,
+        tiled=True,
+    ).astype(jnp.float32)
+    latent_back = packed_sums[:, :latent_width]
+    key_sum = packed_sums[:, latent_width : latent_width + head_dim]
+    value_sum = packed_sums[:, latent_width + head_dim :]
     latent_raw_grad, gain_latent_grad = norm_back(
         latent_raw, scale_latent, gain_latent, latent_back
     )
@@ -343,36 +350,47 @@
     )
     input_part, gain_one_grad = norm_back(inputs, scale_one, gain_one, normed_one_back)
     input_grad = hidden_back + input_part
-    q_down_part = matmul_tn(normed_one, latent_raw_back)
-    key_w_part = matmul_tn(normed_one, key_pre_back)
-    value_w_part = matmul_tn(normed_one, values_low)
+    packed_back = lax.all_gather(
+        jnp.concatenate([latent_raw_back, key_pre_back, values_low], axis=1),
+        "heads",
+        axis=0,
+        tiled=True,
+    )
+    shared_part = matmul_tn(normed_parts, packed_back).astype(jnp.bfloat16)
+    shared_grad = lax.psum_scatter(
+        shared_part, "dp", scatter_dimension=0, tiled=True
+    ).astype(jnp.float32)
+    q_down_grad = shared_grad[:, :latent_width]
+    key_w_grad = shared_grad[:, latent_width : latent_width + head_dim]
+    value_w_grad = shared_grad[:, latent_width + head_dim :]
     gains_part = jnp.concatenate([gain_one_grad, gain_latent_grad, gain_two_grad])
-    q_down_grad, key_w_grad, value_w_grad, gains_grad = (
-        lax.psum_scatter(q_down_part, ("dp", "heads"), scatter_dimension=0, tiled=True),
-        lax.psum_scatter(key_w_part, ("dp", "heads"), scatter_dimension=0, tiled=True),
-        lax.psum_scatter(value_w_part, ("dp", "heads"), scatter_dimension=0, tiled=True),
-        lax.psum_scatter(gains_part, ("dp", "heads"), scatter_dimension=0, tiled=True),
-    )
-    late_sums = (
-        lax.psum_scatter(
-            q_up_part.astype(jnp.bfloat16), "dp", scatter_dimension=0, tiled=True
-        ).astype(jnp.float32),
-        lax.psum_scatter(
-            out_w_part.astype(jnp.bfloat16), "dp", scatter_dimension=0, tiled=True
-        ).astype(jnp.float32),
-        lax.psum_scatter(
-            gate_w_part.astype(jnp.bfloat16), "dp", scatter_dimension=0, tiled=True
-        ).astype(jnp.float32),
-        lax.psum_scatter(
-            up_w_part.astype(jnp.bfloat16), "dp", scatter_dimension=0, tiled=True
-        ).astype(jnp.float32),
-        lax.psum_scatter(
-            down_w_part.astype(jnp.bfloat16), "dp", scatter_dimension=0, tiled=True
-        ).astype(jnp.float32),
-    )
-    q_up_grad = late_sums[0]
-    out_w_grad = late_sums[1]
-    gate_w_grad, up_w_grad, down_w_grad = (late_sums[2], late_sums[3], late_sums[4])
+    gains_grad = lax.psum_scatter(gains_part, ("dp", "heads"), scatter_dimension=0, tiled=True)
+    ffn_sums = lax.psum_scatter(
+        jnp.concatenate([gate_up_part, down_w_part], axis=1).astype(jnp.bfloat16),
+        "dp",
+        scatter_dimension=0,
+        tiled=True,
+    ).astype(jnp.float32)
+    local_ff = w_gate.shape[1]
+    gate_w_grad = ffn_sums[:, :local_ff]
+    up_w_grad = ffn_sums[:, local_ff : 2 * local_ff]
+    down_w_grad = ffn_sums[:, 2 * local_ff :]
+    local_q = w_q_up.shape[1]
+    head_sums = lax.psum_scatter(
+        jnp.concatenate(
+            [
+                q_up_part.reshape(dp_count, -1, local_q),
+                out_w_part.reshape(dp_count, -1, local_q),
+            ],
+            axis=1,
+        ).astype(jnp.bfloat16),
+        "dp",
+        scatter_dimension=0,
+        tiled=True,
+    ).astype(jnp.float32)[0]
+    q_up_rows = w_q_up.shape[0] // dp_count
+    q_up_grad = head_sums[:q_up_rows]
+    out_w_grad = head_sums[q_up_rows:]
     gains_mom = decay_rate * mom_gains + gains_grad
     q_down_mom = decay_rate * mom_q_down + q_down_grad
     key_w_mom = decay_rate * mom_key + key_w_grad
@@ -396,40 +414,26 @@
             axis=0,
         ),
     )
-    shared_blocks = (q_down_mom[None], jnp.stack([key_w_mom, value_w_mom]))
-    first_shared = shared_sums(shared_blocks[0], shared_blocks[1])
-    shared_pairs = [
-        trace_start(blocks, gram_sums) for blocks, gram_sums in zip(shared_blocks, first_shared)
-    ]
-    shared_iter = tuple((pair_item[0] for pair_item in shared_pairs))
-    shared_grams = tuple((pair_item[1] for pair_item in shared_pairs))
-    for step_index in range(NS_STEPS):
-        if step_index > 0:
-            shared_grams = shared_sums(shared_iter[0], shared_iter[1])
-        shared_iter = tuple(
-            (newton_step(blocks, gram_sums) for blocks, gram_sums in zip(shared_iter, shared_grams))
-        )
-    square_sums = lax.psum(
-        (
-            block_squares(head_blocks[0]),
-            block_squares(head_blocks[1]),
-            block_squares(head_blocks[2]),
-        ),
-        "dp",
+    mom_rows = jnp.concatenate([q_down_mom, key_w_mom, value_w_mom], axis=1).astype(jnp.bfloat16)
+    mom_rows = lax.all_gather(mom_rows, "dp", axis=0, tiled=True)
+    mom_rows = lax.all_gather(mom_rows, "heads", axis=0, tiled=True)
+    pair_rows = jnp.stack(
+        [
+            mom_rows[:, latent_width : latent_width + head_dim],
+            mom_rows[:, latent_width + head_dim :],
+        ]
+    )
+    shared_iter = (
+        orthogonal(q_down_mom[None], gram_of(mom_rows[None, :, :latent_width])),
+        orthogonal(jnp.stack([key_w_mom, value_w_mom]), gram_of(pair_rows)),
+    )
+    head_grams = lax.psum(
+        tuple(gram_of(blocks).astype(jnp.bfloat16) for blocks in head_blocks), "dp"
     )
     head_iter = tuple(
-        (
-            blocks / (jnp.sqrt(squares)[:, None, None] + 1e-07)
-            for blocks, squares in zip(head_blocks, square_sums)
-        )
-    )
-    head_grams = head_sums(head_iter[0], head_iter[1], head_iter[2])
-    for step_index in range(NS_STEPS):
-        if step_index > 0:
-            head_grams = head_sums(head_iter[0], head_iter[1], head_iter[2])
-        head_iter = tuple(
-            (newton_step(blocks, gram_sums) for blocks, gram_sums in zip(head_iter, head_grams))
-        )
+        orthogonal(blocks, grams.astype(jnp.float32))
+        for blocks, grams in zip(head_blocks, head_grams)
+    )
     query_ortho, output_ortho, ffn_ortho = head_iter
     q_up_new = own_rows(w_q_up, dp_count, dp_rank) - muon_rate * math.sqrt(
         w_q_up.shape[0] / head_dim

time: 3520 us -> 864 us (0.25)
  waiting for transfers between devices: 3000 us -> 433 us
  matrix products: 229 us -> 168 us
    reduce_scatter x8 -> x2, waiting for transfers between devices: 2090 us -> 103 us  [the longest x1 70.1 us: on_device(): lax.psum_scatter(shared_part, 'dp', scatter_dimension=0, tiled=True)]
    psum x6 -> x1, waiting for transfers between devices: 595 us -> 16.1 us  [on_device(): lax.psum(tuple((gram_of(blocks).astype(jnp.bfloat16) for blocks in head_b...]
    unnamed x27 -> x16, waiting for transfers between devices: 186 us -> 107 us
    all_gather x1 -> x3, waiting for transfers between devices: 0.01 us -> 49.7 us  [the longest x1 27 us: on_device(): lax.all_gather(jnp.concatenate([latent_normed, key_local, value_local], a...]
    dot_general x45 -> x65, matrix products: 98 us -> 59.6 us  [the longest x60 47 us: times(): jnp.einsum('brc,bcd->brd', left.astype(jnp.bfloat16), right.astype(jnp.bf...]
  transfers between devices with their start and end apart: 24 -> 14, of which waited for: 19 -> 12; matrix products, arithmetic and copies ran while one was open for 8% -> 17% of each run, Pallas kernels for 0% -> 0%
where the time goes in v1:
time: 864 us; the launch traced here: 853 us
  waiting for transfers between devices  433 us (50%)
  matrix products  168 us (19%)
  blocking collectives  107 us (12%)
  local copies, waits for them, and re-layouts  67.2 us (8%)
  other arithmetic  60.5 us (7%)
  between operations  16.6 us (2%)
    unnamed x16, waiting for transfers between devices  107 us
    unnamed x1, blocking collectives  70.9 us
    reduce_scatter x1, waiting for transfers between devices, on_device(): lax.psum_scatter(shared_part, 'dp', scatter_dimension=0, tiled=True)  70.1 us
    dot_general x60, matrix products, times(): jnp.einsum('brc,bcd->brd', left.astype(jnp.bfloat16), right.astype(jnp.bf...  47 us
    dot_general x8, matrix products, matmul(): return jnp.dot(left, right, preferred_element_type=jnp.float32)  35.7 us
    reduce_scatter x1, waiting for transfers between devices, on_device(): lax.psum_scatter(matmul_nt(attended, w_out).astype(jnp.bfloat16), 'heads'...  34.6 us
    reduce_scatter x1, waiting for transfers between devices, on_device(): lax.psum_scatter((matmul_nt(gate_back, w_gate) + matmul_nt(up_back, w_up)...  34.5 us
    all_gather x1, waiting for transfers between devices, on_device(): lax.all_gather(hidden_back.astype(jnp.bfloat16), 'heads', axis=0, tiled=T...  34.5 us
  transfers between devices with their start and end apart: 14, of which 12 were waited for; matrix products, arithmetic and copies ran while one was open for 17% of the time, Pallas kernels for 0%

profile of v1, /device:TPU:1, one launch (start us, length us, event | category | flops | bytes accessed | tf_op | source)
XLA Modules:
  0.0 853.4 jit_solution(10701716452057283913)
XLA Ops:
  22.8 27.0 %all-gather.7.cloned.1.call-done = bf16[1024,1536]{1,0:T(8,128)(2,1)} async-done(((bf16[128,1536]{1,0:T(8,128)(2,1)}), bf16[1024,1536]{1,0:T(8,128)(2,1)}) %all-gather.7.cloned.1.call-update) | async-done | bytes 3145744 | tf_op jit(solution)/shard_map/all_gather | solution.py:198
  81.1 34.6 %reduce-scatter.12.cloned.1.call-done = bf16[128,2048]{1,0:T(8,128)(2,1)} async-done(((bf16[1024,2048]{1,0:T(8,128)(2,1)}), bf16[128,2048]{1,0:T(8,128)(2,1)}) %reduce-scatter.12.cloned.1.call-update) | async-done | bytes 524304 | tf_op jit(solution)/shard_map/reduce_scatter | solution.py:249
  119.7 33.9 %all-gather.9.cloned.1.call-done = bf16[1024,2048]{1,0:T(8,128)(2,1)} async-done(((bf16[128,2048]{1,0:T(8,128)(2,1)}), bf16[1024,2048]{1,0:T(8,128)(2,1)}) %all-gather.9.cloned.1.call-update) | async-done | bytes 4194320 | tf_op jit(solution)/shard_map/all_gather | solution.py:255
  153.6 8.0 fusion.278
  166.4 20.9 %all-gather.11.cloned.1.call-done = bf16[1024,2048]{1,0:T(8,128)(2,1)} async-done(((bf16[128,2048]{1,0:T(8,128)(2,1)}), bf16[1024,2048]{1,0:T(8,128)(2,1)}) %all-gather.11.cloned.1.call-update) | async-done | bytes 4194320 | tf_op jit(solution)/shard_map/all_gather | solution.py:265
  187.3 10.2 %multiply_convert_fusion.1 = (bf16[1024,704]{0,1:T(8,128)(2,1)S(1)}, bf16[1024,704]{0,1:T(8,128)(2,1)S(1)}, bf16[1024,704]{0,1:T(8,128)(2,1)}) fusion(f32[1024,704]{0,1:T(8,128)} %fusion.278, f32[1024,704]{0,1:T(8,128)} %fusion.279, bf16[1024,2048]{1,0:T(8,128)(2,1)} %all-gather.11.cloned.1.call-done, bf16[2048,704]{0,1:T(8,128)(2,1)} %param.44), kind=kOutput, calls=%fused_computation.44 | convolution fusion | flops 2963603456 | bytes 17170432 | tf_op jit(solution)/shard_map/dot_general | solution.py:21
  206.9 34.5 %reduce-scatter.16.cloned.1.call-done = bf16[128,2048]{1,0:T(8,128)(2,1)} async-done(((bf16[1024,2048]{1,0:T(8,128)(2,1)}), bf16[128,2048]{1,0:T(8,128)(2,1)}) %reduce-scatter.16.cloned.1.call-update) | async-done | bytes 524304 | tf_op jit(solution)/shard_map/reduce_scatter | solution.py:273
  246.3 34.5 %all-gather.13.cloned.1.call-done = bf16[1024,2048]{1,0:T(8,128)(2,1)} async-done(((bf16[128,2048]{1,0:T(8,128)(2,1)}), bf16[1024,2048]{1,0:T(8,128)(2,1)}) %all-gather.13.cloned.1.call-update) | async-done | bytes 4194320 | tf_op jit(solution)/shard_map/all_gather | solution.py:281
  306.9 32.4 %reduce-scatter.18.cloned.1.call-done = bf16[128,1536]{1,0:T(8,128)(2,1)} async-done(((bf16[1024,1536]{1,0:T(8,128)(2,1)}), bf16[128,1536]{1,0:T(8,128)(2,1)}) %reduce-scatter.18.cloned.1.call-update) | async-done | bytes 393232 | tf_op jit(solution)/shard_map/reduce_scatter | solution.py:331
  345.4 5.9 fusion.15
  351.3 7.6 convolution_convert_fusion
  363.1 11.7 %copy.396 = bf16[2048,2112]{1,0:T(8,128)(2,1)} copy(bf16[2048,2112]{0,1:T(8,128)(2,1)} %pad_maximum_fusion) | data formatting | bytes 17301504
  382.3 6.4 copy.393
  398.5 15.6 %all_to_all.12 = bf16[8,128,256]{1,2,0:T(8,128)(2,1)S(1)} all-to-all(bf16[8,128,256]{1,2,0:T(8,128)(2,1)S(1)} %bitcast.345), channel_id=1, replica_groups=mesh['dp'=16,'heads'=8] {'heads'}, dimensions={0} | all-to-all | bytes 1048576 | tf_op jit(solution)/shard_map/all_to_all | solution.py:205
  419.2 7.9 convolution_convert_fusion.1
  429.6 34.0 %reduce-scatter.22.cloned.1.call-done = bf16[128,2112]{1,0:T(8,128)(2,1)} async-done(((bf16[2048,2112]{1,0:T(8,128)(2,1)}), bf16[128,2112]{1,0:T(8,128)(2,1)}) %reduce-scatter.22.cloned.1.call-update) | async-done | bytes 540688
  469.9 72.0 %reduce-scatter.24.cloned.1.call-done = bf16[1,192,512]{2,1,0:T(8,128)(2,1)} async-done(((bf16[16,192,512]{2,1,0:T(8,128)(2,1)}), bf16[1,192,512]{2,1,0:T(8,128)(2,1)}) %reduce-scatter.24.cloned.1.call-update) | async-done | bytes 196624
  547.9 70.1 %reduce-scatter.20.cloned.1.call-done = bf16[16,1536]{1,0:T(8,128)(2,1)} async-done(((bf16[256,1536]{1,0:T(8,128)(2,1)}), bf16[16,1536]{1,0:T(8,128)(2,1)}) %reduce-scatter.20.cloned.1.call-update) | async-done | bytes 49168 | tf_op jit(solution)/shard_map/reduce_scatter | solution.py:360
  620.9 20.7 %all_gather.26 = bf16[256,1536]{1,0:T(8,128)(2,1)} all-gather(bf16[16,1536]{1,0:T(8,128)(2,1)S(1)} %pad_maximum_fusion.15), channel_id=1, replica_groups=mesh['dp'=16,'heads'=8] {'dp'}, dimensions={0}, use_global_device_ids=true | all-gather | bytes 835584 | tf_op jit(solution)/shard_map/all_gather | solution.py:418
  660.3 70.9 %all-reduce.2 = f32[5120]{0:T(1024)S(1)} all-reduce(f32[5120]{0:T(1024)S(1)} %pad_maximum_fusion.16), channel_id=6, replica_groups=mesh['dp'=16,'heads'=8] {'dp','heads'}, use_global_device_ids=true, to_apply=%region_22.23.clone | all-reduce | flops 5120 | bytes 40960
  736.8 16.1 %all-reduce.7.cloned.1.call-done = (bf16[2,256,256]{2,1,0:T(8,128)(2,1)}, bf16[2,256,256]{2,1,0:T(8,128)(2,1)}, bf16[6,352,352]{2,1,0:T(8,128)(2,1)}) async-done(((bf16[2,256,256]{2,1,0:T(8,128)(2,1)}, bf16[2,256,256]{2,1,0:T(8,128)(2,1)}, bf16[6,352,352]{2,1,0:T(8,128)(2,1)}), (bf16[2,256,256]{2,1,0:T(8,128)(2,1)}, bf16[2,256,256]{2,1,0:T(8,128)(2,1)}, ...) | async-done | bytes 2011152 | tf_op jit(solution)/shard_map/psum | solution.py:430
  773.6 22.8 %all-gather.17.cloned.1.call-done = bf16[2048,1536]{1,0:T(8,128)(2,1)} async-done(((bf16[256,1536]{1,0:T(8,128)(2,1)}), bf16[2048,1536]{1,0:T(8,128)(2,1)}) %all-gather.17.cloned.1.call-update) | async-done | bytes 6291472 | tf_op jit(solution)/shard_map/all_gather | solution.py:419
  811.9 7.2 select_reduce_fusion
  819.9 7.4 add_convert_fusion.3
  (380 shorter events, 224.5 us)
Async XLA Ops:
  7.2 68.4 %copy-start = (bf16[2048,512]{1,0:T(8,128)(2,1)S(1)}, bf16[2048,512]{1,0:T(8,128)(2,1)}, u32[]{:S(2)}) copy-start(bf16[2048,512]{1,0:T(8,128)(2,1)} %param.41) | copy-start | bytes 6291460
  7.2 42.6 %all-gather.7.cloned.1.call-start = ((), (), s32[]{:S(2)}) async-start(), calls=%async_computation.8 | async-start | bytes 3538944 | tf_op jit(solution)/shard_map/all_gather | solution.py:198
  18.2 97.4 %reduce-scatter.12.cloned.1.call-start = ((), (), s32[]{:S(2)}) async-start(), calls=%async_computation.9 | async-start | bytes 4718592 | tf_op jit(solution)/shard_map/reduce_scatter | solution.py:249
  22.8 36.7 %copy-start.14 = (f32[1024,128]{1,0:T(8,128)}, f32[1024,128]{1,0:T(8,128)S(1)}, u32[]{:S(2)}) copy-start(f32[1024,128]{1,0:T(8,128)S(1)} %get-tuple-element.313) | copy-start | bytes 1572868
  81.0 34.7 %copy-start.6 = (bf16[128,2048]{1,0:T(8,128)(2,1)S(1)}, bf16[128,2048]{1,0:T(8,128)(2,1)}, u32[]{:S(2)}) copy-start(bf16[128,2048]{1,0:T(8,128)(2,1)} %param.33) | copy-start | bytes 1572868
  81.1 72.6 %all-gather.9.cloned.1.call-start = ((), (), s32[]{:S(2)}) async-start(), calls=%async_computation.10 | async-start | bytes 4718592 | tf_op jit(solution)/shard_map/all_gather | solution.py:255
  117.0 126.6 %copy-start.63 = (f32[128]{0:T(128)}, f32[128]{0:T(128)S(1)}, u32[]{:S(2)}) copy-start(f32[128]{0:T(128)S(1)} %get-tuple-element.322) | copy-start | bytes 1540
  117.0 126.6 %copy-start.66 = (f32[128]{0:T(128)}, f32[128]{0:T(128)S(1)}, u32[]{:S(2)}) copy-start(f32[128]{0:T(128)S(1)} %get-tuple-element.321) | copy-start | bytes 1540
  119.1 68.2 %all-gather.11.cloned.1.call-start = ((), (), s32[]{:S(2)}) async-start(), calls=%async_computation.12 | async-start | bytes 4718592 | tf_op jit(solution)/shard_map/all_gather | solution.py:265
  119.6 121.8 %reduce-scatter.16.cloned.1.call-start = ((), (), s32[]{:S(2)}) async-start(), calls=%async_computation.13 | async-start | bytes 4718592 | tf_op jit(solution)/shard_map/reduce_scatter | solution.py:273
  206.9 73.9 %all-gather.13.cloned.1.call-start = ((), (), s32[]{:S(2)}) async-start(), calls=%async_computation.14 | async-start | bytes 4718592 | tf_op jit(solution)/shard_map/all_gather | solution.py:281
  243.6 41.9 %copy-start.67 = (f32[128]{0:T(128)}, f32[128]{0:T(128)S(1)}, u32[]{:S(2)}) copy-start(f32[128]{0:T(128)S(1)} %broadcast_multiply_fusion.2) | copy-start | bytes 1540
  246.2 93.0 %reduce-scatter.18.cloned.1.call-start = ((), (), s32[]{:S(2)}) async-start(), calls=%async_computation.15 | async-start | bytes 3538944 | tf_op jit(solution)/shard_map/reduce_scatter | solution.py:331
  306.9 108.2 %all-gather.15.cloned.1.call-start = ((), (), s32[]{:S(2)}) async-start(), calls=%async_computation.16 | async-start | bytes 3538944 | tf_op jit(solution)/shard_map/all_gather | solution.py:353
  345.3 118.4 %reduce-scatter.22.cloned.1.call-start = ((), (), s32[]{:S(2)}) async-start(), calls=%async_computation.19 | async-start | bytes 9469952
  374.9 167.0 %reduce-scatter.24.cloned.1.call-start = ((), (), s32[]{:S(2)}) async-start(), calls=%async_computation.20 | async-start | bytes 3342336
  396.4 221.7 %reduce-scatter.20.cloned.1.call-start = ((), (), s32[]{:S(2)}) async-start(), calls=%async_computation.17 | async-start | bytes 835584 | tf_op jit(solution)/shard_map/reduce_scatter | solution.py:360
  419.1 314.0 %reduce-scatter.14.cloned.1.call-start = ((), (), s32[]{:S(2)}) async-start(), calls=%async_computation.11 | async-start | bytes 4718592 | tf_op jit(solution)/shard_map/reduce_scatter | solution.py:261
  427.0 38.0 %copy-start.44 = (f32[128,704]{0,1:T(8,128)S(1)}, f32[128,704]{0,1:T(8,128)}, u32[]{:S(2)}) copy-start(f32[128,704]{0,1:T(8,128)} %param.53) | copy-start | bytes 1081348
  427.1 325.9 %all-reduce.7.cloned.1.call-start = ((), (), s32[]{:S(2)}) async-start(), calls=%async_computation.21 | async-start | bytes 4292608 | tf_op jit(solution)/shard_map/psum | solution.py:430
  543.0 75.1 %copy-start.56 = (f32[16,256]{1,0:T(8,128)S(1)}, f32[16,256]{1,0:T(8,128)}, u32[]{:S(2)}) copy-start(f32[16,256]{1,0:T(8,128)} %param.48) | copy-start | bytes 49156
  543.0 75.1 %copy-start.57 = (f32[16,256]{1,0:T(8,128)S(1)}, f32[16,256]{1,0:T(8,128)}, u32[]{:S(2)}) copy-start(f32[16,256]{1,0:T(8,128)} %param.47) | copy-start | bytes 49156
  547.9 248.6 %all-gather.17.cloned.1.call-start = ((), (), s32[]{:S(2)}) async-start(), calls=%async_computation.18 | async-start | bytes 7077888 | tf_op jit(solution)/shard_map/all_gather | solution.py:419
  657.1 76.1 %copy-start.10 = (bf16[128,2048]{1,0:T(8,128)(2,1)S(1)}, bf16[128,2048]{1,0:T(8,128)(2,1)}, u32[]{:S(2)}) copy-start(bf16[128,2048]{1,0:T(8,128)(2,1)} %reduce-scatter.12.cloned.1.call-done) | copy-start | bytes 1572868
  (70 other events, 371.2 us)
Sparse Core Ops, SparseCore 0:
  18.4 31.3 all-gather.6
  81.2 34.4 reduce-scatter.11
  119.2 34.3 all-gather.8
  155.2 32.0 all-gather.10
  207.0 34.3 reduce-scatter.15
  246.4 34.3 all-gather.12
  307.0 32.2 reduce-scatter.17
  345.4 29.9 all-gather.14
  378.9 84.7 reduce-scatter.21
  467.2 74.6 reduce-scatter.23
  546.0 72.0 reduce-scatter.19
  620.4 36.1 reduce-scatter.13
  661.5 91.4 all-reduce.6
  754.5 41.8 all-gather.16

commit v2 on v1

v2 whole, which is shorter than its diff:
```python
import math

import jax
import jax.numpy as jnp
from jax import lax
from jax.experimental import pallas as pl
from jax.experimental.pallas import tpu as pltpu
from jax.sharding import PartitionSpec as P

NS_STEPS = 3
FF_BLOCK = 352
SIDE = 4
CORES = 2

coef_first = 3.4445
coef_second = -4.775
coef_third = 2.0315
muon_rate = 0.5
gain_rate = 0.004
decay_rate = 0.5
low_type = jnp.bfloat16
vmem_bytes = 28 * 1024 * 1024


def matmul(left, right):
    return jnp.dot(left, right, preferred_element_type=jnp.float32)


def matmul_nt(left, right):
    return lax.dot_general(
        left, right, (((1,), (1,)), ((), ())), preferred_element_type=jnp.float32
    )


def matmul_tn(left, right):
    return lax.dot_general(
        left, right, (((0,), (0,)), ((), ())), preferred_element_type=jnp.float32
    )


def rms_scale(values):
    return lax.rsqrt(jnp.mean(values * values, axis=-1, keepdims=True) + 1e-05)


def norm_back(values, scale, gain, grad_out):
    weighted = gain * grad_out
    inner = jnp.mean(values * weighted, axis=-1, keepdims=True)
    grad_in = scale * weighted - values * (scale * scale * scale) * inner
    gain_grad = jnp.sum(grad_out * values * scale, axis=0)
    return (grad_in, gain_grad)


def segment_info(starts, token_index):
    started = starts[None, :] <= token_index[:, None]
    seg_ids = jnp.sum(started.astype(jnp.int32), axis=1)
    seg_begin = jnp.max(jnp.where(started, starts[None, :], 0), axis=1)
    return (seg_ids, token_index - seg_begin)


def rotary_tables(positions, head_dim):
    half_dim = head_dim // 2
    frequency = jnp.exp(
        jnp.arange(half_dim, dtype=jnp.float32) * (-2.0 * math.log(10000.0) / head_dim)
    )
    angles = positions.astype(jnp.float32)[:, None] * frequency[None, :]
    return (jnp.cos(angles), jnp.sin(angles))


def rotate(values, cosine, sine_part):
    half_dim = values.shape[-1] // 2
    first_half = values[..., :half_dim]
    second_half = values[..., half_dim:]
    return jnp.concatenate(
        [
            first_half * cosine - second_half * sine_part,
            second_half * cosine + first_half * sine_part,
        ],
        axis=-1,
    )


def rotate_back(grads, cosine, sine_part):
    return rotate(grads, cosine, -sine_part)


def shift_heads(values, step, core):
    pairs = [
        (CORES * place + side, CORES * ((place + step) % SIDE) + (side ^ core))
        for place in range(SIDE)
        for side in range(CORES)
    ]
    return lax.ppermute(values, "heads", pairs)


def shift_dp(values, step_z, step_x):
    pairs = [
        (SIDE * z + x, SIDE * ((z + step_z) % SIDE) + (x + step_x) % SIDE)
        for z in range(SIDE)
        for x in range(SIDE)
    ]
    return lax.ppermute(values, "dp", pairs)


def gather_heads(own):
    ring = [own] + [shift_heads(own, -step, 0) for step in range(1, SIDE)]
    return ring + [shift_heads(piece, 0, 1) for piece in ring]


def scatter_heads(far_half, own_half):
    rows = own_half.shape[0] // SIDE
    chip_sum = own_half.astype(jnp.float32) + shift_heads(far_half, 0, 1).astype(jnp.float32)
    chip_sum = chip_sum.reshape(SIDE, rows, *own_half.shape[1:])
    total = chip_sum[0]
    for step in range(1, SIDE):
        total = total + shift_heads(chip_sum[step].astype(far_half.dtype), step, 0).astype(
            jnp.float32
        )
    return total


def scatter_dp(parts):
    place_z = lax.axis_index("dp") // SIDE
    place_x = lax.axis_index("dp") % SIDE
    kind = parts.dtype
    grid = parts.reshape(SIDE, SIDE, *parts.shape[1:])

    def pick(array, place, axis):
        return lax.dynamic_index_in_dim(array, place % SIDE, axis, keepdims=False)

    total = pick(grid, place_x, 1).astype(jnp.float32)
    for step in range(1, SIDE):
        total = total + shift_dp(pick(grid, place_x + step, 1), 0, step).astype(jnp.float32)
    column = total.astype(kind)
    total = pick(total, place_z, 0)
    for step in range(1, SIDE):
        total = total + shift_dp(pick(column, place_z + step, 0), step, 0).astype(jnp.float32)
    return total


def gather_dp(own):
    ring = jnp.concatenate([own] + [shift_dp(own, 0, step) for step in range(1, SIDE)], axis=0)
    return jnp.concatenate([ring] + [shift_dp(ring, step, 0) for step in range(1, SIDE)], axis=0)


def visible(ids_q, ids_k, first_row, rows, cols):
    query_at = first_row + lax.broadcasted_iota(jnp.int32, (rows, cols), 0)
    key_at = lax.broadcasted_iota(jnp.int32, (rows, cols), 1)
    return (ids_q == ids_k) & (key_at <= query_at)


def attend_kernel(
    slots, latent, weight, keys, values, cosine, sine, ids_q, ids_k, query_out, mixed_out, lse_out
):
    row_len, head_dim = keys.shape
    piece = row_len // (SIDE * CORES)
    block = CORES * piece
    scale = head_dim ** (-0.5)
    for index in range(SIDE):
        first = index * block
        end = first + block
        rows = slice(first, end)
        query = rotate(matmul(latent[rows, :], weight[...]), cosine[rows, :], sine[rows, :])
        query = query.astype(low_type)
        query_out[rows, :] = query
        scores = matmul_nt(query, keys[:end, :]) * scale
        allowed = visible(ids_q[rows, :], ids_k[:, :end], first, block, end)
        scores = jnp.where(allowed, scores, -1e30)
        row_max = jnp.max(scores, axis=-1, keepdims=True)
        exponent = jnp.exp(scores - row_max)
        row_total = jnp.sum(exponent, axis=-1, keepdims=True)
        probs = (exponent * (1.0 / row_total)).astype(low_type)
        lse_out[0, rows, :] = row_max + jnp.log(row_total)
        mixed = matmul(probs, values[:end, :]).astype(low_type)
        for side in range(CORES):
            place = pl.multiple_of(slots[CORES * index + side] * piece, piece)
            mixed_out[pl.ds(place, piece), :] = mixed[side * piece : (side + 1) * piece, :]


def attend(slots, latent_rows, w_q_up, key_rows, value_rows, cosine, sine, row_ids):
    row_len, head_dim = key_rows.shape
    latent_width, width = w_q_up.shape
    count = width // head_dim
    whole = lambda head, slots: (0, 0)
    column = lambda head, slots: (0, head)
    return pl.pallas_call(
        attend_kernel,
        grid_spec=pltpu.PrefetchScalarGridSpec(
            num_scalar_prefetch=1,
            grid=(count,),
            in_specs=[
                pl.BlockSpec((row_len, latent_width), whole),
                pl.BlockSpec((latent_width, head_dim), column),
                pl.BlockSpec((row_len, head_dim), whole),
                pl.BlockSpec((row_len, head_dim), whole),
                pl.BlockSpec((row_len, head_dim // 2), whole),
                pl.BlockSpec((row_len, head_dim // 2), whole),
                pl.BlockSpec((row_len, 1), whole),
                pl.BlockSpec((1, row_len), whole),
            ],
            out_specs=[
                pl.BlockSpec((row_len, head_dim), column),
                pl.BlockSpec((row_len, head_dim), column),
                pl.BlockSpec((1, row_len, 1), lambda head, slots: (head, 0, 0)),
            ],
        ),
        out_shape=[
            jax.ShapeDtypeStruct((row_len, width), low_type),
            jax.ShapeDtypeStruct((row_len, width), low_type),
            jax.ShapeDtypeStruct((count, row_len, 1), jnp.float32),
        ],
        compiler_params=pltpu.CompilerParams(vmem_limit_bytes=vmem_bytes),
        cost_estimate=pl.CostEstimate(
            flops=2 * width * row_len * (latent_width + 2 * row_len),
            bytes_accessed=8 * row_len * width,
            transcendentals=count * row_len * row_len,
        ),
        name="attend",
    )(
        slots,
        latent_rows,
        w_q_up,
        key_rows,
        value_rows,
        cosine,
        sine,
        row_ids[:, None],
        row_ids[None, :],
    )


def attend_back_kernel(
    slots,
    query_in,
    keys,
    values,
    mixed_back,
    lse,
    cosine,
    sine,
    ids_q,
    ids_k,
    query_back,
    pair_back,
    key_sum,
    value_sum,
):
    row_len, head_dim = keys.shape
    piece = row_len // (SIDE * CORES)
    block = CORES * piece
    scale = head_dim ** (-0.5)
    head = pl.program_id(0)

    @pl.when(head == 0)
    def _():
        key_sum[...] = jnp.zeros_like(key_sum)
        value_sum[...] = jnp.zeros_like(value_sum)

    for index in range(SIDE):
        first = index * block
        end = first + block
        rows = slice(first, end)
        places = [
            pl.multiple_of(slots[CORES * index + side] * piece, piece) for side in range(CORES)
        ]
        query = query_in[rows, :]
        back = jnp.concatenate([mixed_back[pl.ds(place, piece), :] for place in places], axis=0)
        scores = matmul_nt(query, keys[:end, :]) * scale
        allowed = visible(ids_q[rows, :], ids_k[:, :end], first, block, end)
        probs = jnp.where(allowed, jnp.exp(scores - lse[0, rows, :]), 0.0)
        probs_back = matmul_nt(back, values[:end, :])
        inner = jnp.sum(probs * probs_back, axis=-1, keepdims=True)
        score_back = (probs * (probs_back - inner)).astype(low_type)
        probs_low = probs.astype(low_type)
        value_sum[:end, :] += matmul_tn(probs_low, back)
        key_sum[:end, :] += matmul_tn(score_back, query) * scale
        query_grad = matmul(score_back, keys[:end, :]) * scale
        query_grad = rotate_back(query_grad, cosine[rows, :], sine[rows, :]).astype(low_type)
        for side, place in enumerate(places):
            query_back[pl.ds(place, piece), :] = query_grad[side * piece : (side + 1) * piece, :]

    @pl.when(head == pl.num_programs(0) - 1)
    def _():
        for index in range(SIDE * CORES):
            place = pl.multiple_of(slots[index] * piece, piece)
            rows = slice(index * piece, (index + 1) * piece)
            pair_back[pl.ds(place, piece), :head_dim] = key_sum[rows, :].astype(low_type)
            pair_back[pl.ds(place, piece), head_dim:] = value_sum[rows, :].astype(low_type)


def attend_back(slots, query_rows, key_rows, value_rows, mixed_back, lse, cosine, sine, row_ids):
    row_len, head_dim = key_rows.shape
    width = query_rows.shape[1]
    count = width // head_dim
    whole = lambda head, slots: (0, 0)
    column = lambda head, slots: (0, head)
    return pl.pallas_call(
        attend_back_kernel,
        grid_spec=pltpu.PrefetchScalarGridSpec(
            num_scalar_prefetch=1,
            grid=(count,),
            in_specs=[
                pl.BlockSpec((row_len, head_dim), column),
                pl.BlockSpec((row_len, head_dim), whole),
                pl.BlockSpec((row_len, head_dim), whole),
                pl.BlockSpec((row_len, head_dim), column),
                pl.BlockSpec((1, row_len, 1), lambda head, slots: (head, 0, 0)),
                pl.BlockSpec((row_len, head_dim // 2), whole),
                pl.BlockSpec((row_len, head_dim // 2), whole),
                pl.BlockSpec((row_len, 1), whole),
                pl.BlockSpec((1, row_len), whole),
            ],
            out_specs=[
                pl.BlockSpec((row_len, head_dim), column),
                pl.BlockSpec((row_len, 2 * head_dim), whole),
            ],
            scratch_shapes=[
                pltpu.VMEM((row_len, head_dim), jnp.float32),
                pltpu.VMEM((row_len, head_dim), jnp.float32),
            ],
        ),
        out_shape=[
            jax.ShapeDtypeStruct((row_len, width), low_type),
            jax.ShapeDtypeStruct((row_len, 2 * head_dim), low_type),
        ],
        compiler_params=pltpu.CompilerParams(vmem_limit_bytes=vmem_bytes),
        cost_estimate=pl.CostEstimate(
            flops=10 * width * row_len * row_len,
            bytes_accessed=8 * row_len * width,
            transcendentals=count * row_len * row_len,
        ),
        name="attend_back",
    )(
        slots,
        query_rows,
        key_rows,
        value_rows,
        mixed_back,
        lse,
        cosine,
        sine,
        row_ids[:, None],
        row_ids[None, :],
    )


def place_kernel(slots, source, target):
    target[...] = source[...]


def place_blocks(slots, rows, count):
    piece = rows.shape[0] // count
    width = rows.shape[1]
    return pl.pallas_call(
        place_kernel,
        grid_spec=pltpu.PrefetchScalarGridSpec(
            num_scalar_prefetch=1,
            grid=(count,),
            in_specs=[pl.BlockSpec((piece, width), lambda index, slots: (index, 0))],
            out_specs=pl.BlockSpec((piece, width), lambda index, slots: (slots[index], 0)),
        ),
        out_shape=jax.ShapeDtypeStruct(rows.shape, rows.dtype),
        cost_estimate=pl.CostEstimate(
            flops=0, bytes_accessed=4 * rows.shape[0] * width, transcendentals=0
        ),
        name="place_blocks",
    )(slots, rows)


def gram_of(blocks):
    low = blocks.astype(low_type)
    return jnp.einsum("brc,brd->bcd", low, low, preferred_element_type=jnp.float32)


def times(left, right):
    return jnp.einsum(
        "brc,bcd->brd",
        left.astype(low_type),
        right.astype(low_type),
        preferred_element_type=jnp.float32,
    )


def orthogonal(blocks, gram_sums):
    diagonal = jnp.eye(gram_sums.shape[-1], dtype=jnp.bool_)
    trace_sum = jnp.sum(jnp.where(diagonal, gram_sums, 0.0), axis=(1, 2))
    factor = 1.0 / (jnp.sqrt(trace_sum) + 1e-07)
    iterate = blocks * factor[:, None, None]
    gram = gram_sums * (factor * factor)[:, None, None]
    for step_index in range(NS_STEPS):
        first_term = times(iterate, gram)
        second_term = times(first_term, gram)
        iterate = coef_first * iterate + coef_second * first_term + coef_third * second_term
        if step_index + 1 < NS_STEPS:
            change = coef_second * gram + coef_third * times(gram, gram)
            once = times(gram, change)
            twice = times(once, change)
            gram = (coef_first * coef_first) * gram + (2.0 * coef_first) * once + twice
    return iterate


def split_columns(matrix, block_cols):
    row_count = matrix.shape[0]
    return matrix.reshape(row_count, matrix.shape[1] // block_cols, block_cols).transpose(1, 0, 2)


def join_columns(blocks):
    return blocks.transpose(1, 0, 2).reshape(blocks.shape[1], blocks.shape[0] * blocks.shape[2])


def own_rows(weight, count, rank):
    share_rows = weight.shape[0] // count
    return lax.dynamic_slice_in_dim(weight, rank * share_rows, share_rows, 0).astype(jnp.float32)


def on_device(
    tokens_in,
    cotangent,
    seg_starts,
    gains,
    w_q_down,
    w_key,
    w_value,
    w_q_up,
    w_out,
    w_gate,
    w_up,
    w_down,
    mom_gains,
    mom_q_down,
    mom_key,
    mom_value,
    mom_q_up,
    mom_out,
    mom_gate,
    mom_up,
    mom_down,
):
    heads_count = lax.axis_size("heads")
    heads_rank = lax.axis_index("heads")
    dp_count = lax.axis_size("dp")
    dp_rank = lax.axis_index("dp")
    all_rank = lax.axis_index(("dp", "heads"))
    all_count = dp_count * heads_count
    local_rows = tokens_in.shape[0]
    row_len = local_rows * heads_count
    half_len = row_len // 2
    model_width = tokens_in.shape[1]
    latent_width = w_q_down.shape[1]
    head_dim = w_key.shape[1]
    local_q = w_q_up.shape[1]
    local_ff = w_gate.shape[1]
    starts = seg_starts[0]
    whole_index = jnp.arange(row_len, dtype=jnp.int32)
    own_index = heads_rank * local_rows + jnp.arange(local_rows, dtype=jnp.int32)
    ranks = jnp.arange(heads_count, dtype=jnp.int32)
    far_core = (ranks % CORES) ^ (heads_rank % CORES)
    slots = SIDE * far_core + (ranks // CORES - heads_rank // CORES) % SIDE
    gain_one = gains[:model_width]
    gain_latent = gains[model_width : model_width + latent_width]
    gain_two = gains[model_width + latent_width :]
    inputs = tokens_in.astype(jnp.float32)
    scale_one = rms_scale(inputs)
    normed_one = (inputs * scale_one * gain_one).astype(low_type)
    latent_raw = matmul(normed_one, w_q_down)
    scale_latent = rms_scale(latent_raw)
    latent_normed = (latent_raw * scale_latent * gain_latent).astype(low_type)
    own_pos = segment_info(starts, own_index)[1]
    own_cos, own_sin = rotary_tables(own_pos, head_dim)
    key_local = rotate(matmul(normed_one, w_key), own_cos, own_sin).astype(low_type)
    value_local = matmul(normed_one, w_value).astype(low_type)
    packed_rows = lax.all_gather(
        jnp.concatenate([latent_normed, key_local, value_local], axis=1), "heads", axis=0, tiled=True
    )
    latent_rows = packed_rows[:, :latent_width]
    key_rows = packed_rows[:, latent_width : latent_width + head_dim]
    value_rows = packed_rows[:, latent_width + head_dim :]
    share_rows = model_width // all_count
    normed_parts = lax.all_to_all(
        normed_one.reshape(local_rows, dp_count, heads_count, share_rows)
        .transpose(2, 0, 1, 3)
        .reshape(heads_count * local_rows, dp_count * share_rows),
        "heads",
        split_axis=0,
        concat_axis=0,
        tiled=True,
    )
    normed_parts = place_blocks(slots, normed_parts, heads_count)
    grad_rows = place_blocks(
        slots, lax.all_gather(cotangent, "heads", axis=0, tiled=True), heads_count
    )
    row_ids, row_pos = segment_info(starts, whole_index)
    row_cos, row_sin = rotary_tables(row_pos, head_dim)
    query_rows, attended, lse = attend(
        slots, latent_rows, w_q_up, key_rows, value_rows, row_cos, row_sin, row_ids
    )
    attn_mixed = scatter_heads(
        matmul_nt(attended[half_len:], w_out).astype(low_type),
        matmul_nt(attended[:half_len], w_out),
    )
    hidden_one = inputs + attn_mixed
    scale_two = rms_scale(hidden_one)
    normed_two = (hidden_one * scale_two * gain_two).astype(low_type)
    ffn_input = jnp.concatenate(gather_heads(normed_two), axis=0)
    gate_raw = matmul(ffn_input, w_gate)
    up_raw = matmul(ffn_input, w_up)
    sigmoid_gate = jax.nn.sigmoid(gate_raw)
    activated = gate_raw * sigmoid_gate
    hidden_mid = (activated * up_raw).astype(low_type)
    mid_back = matmul(grad_rows, w_down)
    gate_back = (mid_back * up_raw * sigmoid_gate * (1.0 + gate_raw * (1.0 - sigmoid_gate))).astype(
        low_type
    )
    up_back = (mid_back * activated).astype(low_type)
    normed_two_back = scatter_heads(
        (matmul_nt(gate_back[half_len:], w_gate) + matmul_nt(up_back[half_len:], w_up)).astype(
            low_type
        ),
        matmul_nt(gate_back[:half_len], w_gate) + matmul_nt(up_back[:half_len], w_up),
    )
    gate_up_part = matmul_tn(ffn_input, jnp.concatenate([gate_back, up_back], axis=1))
    down_w_part = matmul_tn(grad_rows, hidden_mid)
    ffn_sums = lax.psum_scatter(
        jnp.concatenate([gate_up_part, down_w_part], axis=1).astype(low_type),
        "dp",
        scatter_dimension=0,
        tiled=True,
    ).astype(jnp.float32)
    hidden_part, gain_two_grad = norm_back(hidden_one, scale_two, gain_two, normed_two_back)
    hidden_back = cotangent.astype(jnp.float32) + hidden_part
    hidden_rows = jnp.concatenate(gather_heads(hidden_back.astype(low_type)), axis=0)
    attended_back = matmul(hidden_rows, w_out).astype(low_type)
    late_mid, _ = lax.optimization_barrier((hidden_mid, attended_back))
    ffn_mixed = scatter_heads(
        matmul_nt(late_mid[half_len:], w_down).astype(low_type),
        matmul_nt(late_mid[:half_len], w_down),
    )
    layer_out = (hidden_one + ffn_mixed).astype(low_type)
    out_w_part = matmul_tn(hidden_rows, attended)
    query_back, pair_back = attend_back(
        slots, query_rows, key_rows, value_rows, attended_back, lse, row_cos, row_sin, row_ids
    )
    packed_sums = scatter_heads(
        jnp.concatenate(
            [matmul_nt(query_back[half_len:], w_q_up).astype(low_type), pair_back[half_len:]],
            axis=1,
        ),
        jnp.concatenate(
            [matmul_nt(query_back[:half_len], w_q_up).astype(low_type), pair_back[:half_len]],
            axis=1,
        ),
    )
    latent_back = packed_sums[:, :latent_width]
    key_sum = packed_sums[:, latent_width : latent_width + head_dim]
    value_sum = packed_sums[:, latent_width + head_dim :]
    latent_raw_grad, gain_latent_grad = norm_back(
        latent_raw, scale_latent, gain_latent, latent_back
    )
    latent_raw_back = latent_raw_grad.astype(low_type)
    key_pre_back = rotate_back(key_sum, own_cos, own_sin).astype(low_type)
    values_low = value_sum.astype(low_type)
    packed_back = jnp.concatenate(
        gather_heads(jnp.concatenate([latent_raw_back, key_pre_back, values_low], axis=1)), axis=0
    )
    shared_part = matmul_tn(normed_parts, packed_back).astype(low_type)
    shared_grad = scatter_dp(shared_part.reshape(dp_count, share_rows, shared_part.shape[1]))
    q_down_grad = shared_grad[:, :latent_width]
    key_w_grad = shared_grad[:, latent_width : latent_width + head_dim]
    value_w_grad = shared_grad[:, latent_width + head_dim :]
    latent_ordered = place_blocks(slots, latent_rows, heads_count)
    q_up_part = matmul_tn(latent_ordered, query_back)
    head_sums = scatter_dp(
        jnp.concatenate(
            [
                q_up_part.astype(low_type).reshape(dp_count, -1, local_q),
                out_w_part.astype(low_type).reshape(dp_count, -1, local_q),
            ],
            axis=1,
        )
    )
    q_up_rows = w_q_up.shape[0] // dp_count
    q_up_grad = head_sums[:q_up_rows]
    out_w_grad = head_sums[q_up_rows:]
    gate_w_grad = ffn_sums[:, :local_ff]
    up_w_grad = ffn_sums[:, local_ff : 2 * local_ff]
    down_w_grad = ffn_sums[:, 2 * local_ff :]
    normed_one_back = (
        matmul_nt(latent_raw_back, w_q_down)
        + matmul_nt(key_pre_back, w_key)
        + matmul_nt(values_low, w_value)
    )
    input_part, gain_one_grad = norm_back(inputs, scale_one, gain_one, normed_one_back)
    input_grad = hidden_back + input_part
    share_gains = gains.shape[0] // all_count
    gains_part = jnp.concatenate([gain_one_grad, gain_latent_grad, gain_two_grad])
    gains_part = gains_part.reshape(dp_count, heads_count, share_gains).transpose(1, 0, 2)
    gains_part = gains_part.reshape(SIDE, CORES, dp_count * share_gains)
    own_core = heads_rank % CORES
    own_step = heads_rank // CORES

    def by_step(array, core):
        side = lax.dynamic_index_in_dim(array, core, 1, keepdims=False)
        return lax.dynamic_slice_in_dim(jnp.concatenate([side, side], axis=0), own_step, SIDE, 0)

    gains_sum = scatter_heads(by_step(gains_part, 1 - own_core), by_step(gains_part, own_core))
    gains_grad = scatter_dp(gains_sum.reshape(dp_count, 1, share_gains))[0]
    gains_mom = decay_rate * mom_gains + gains_grad
    q_down_mom = decay_rate * mom_q_down + q_down_grad
    key_w_mom = decay_rate * mom_key + key_w_grad
    value_w_mom = decay_rate * mom_value + value_w_grad
    q_up_mom = decay_rate * mom_q_up + q_up_grad
    out_w_mom = decay_rate * mom_out + out_w_grad
    gate_w_mom = decay_rate * mom_gate + gate_w_grad
    up_w_mom = decay_rate * mom_up + up_w_grad
    down_w_mom = decay_rate * mom_down + down_w_grad
    gains_new = own_rows(gains, all_count, all_rank) - gain_rate * gains_mom
    ffn_count = w_gate.shape[1] // FF_BLOCK
    ffn_blocks = jnp.concatenate(
        [
            split_columns(gate_w_mom, FF_BLOCK),
            split_columns(up_w_mom, FF_BLOCK),
            split_columns(down_w_mom, FF_BLOCK),
        ],
        axis=0,
    )
    ffn_gram = lax.psum(gram_of(ffn_blocks).astype(low_type), "dp").astype(jnp.float32)
    ffn_ortho = orthogonal(ffn_blocks, ffn_gram)
    query_blocks = split_columns(q_up_mom, head_dim)
    output_blocks = split_columns(out_w_mom, head_dim)
    head_grams = jnp.concatenate([gram_of(query_blocks), gram_of(output_blocks)], axis=0)
    gram_rows = head_dim // dp_count
    head_count = query_blocks.shape[0]
    head_grams = (
        head_grams.astype(low_type)
        .reshape(2 * head_count, dp_count, gram_rows, head_dim)
        .transpose(1, 0, 2, 3)
        .reshape(dp_count, 2 * head_count * gram_rows, head_dim)
    )
    head_grams = scatter_dp(head_grams).astype(low_type)
    place_z = dp_rank // SIDE
    place_x = dp_rank % SIDE
    head_grams = gather_dp(head_grams[None])
    head_grams = head_grams.reshape(SIDE, SIDE, 2 * head_count, gram_rows, head_dim)
    order_z = (place_z - jnp.arange(SIDE)) % SIDE
    order_x = (place_x - jnp.arange(SIDE)) % SIDE
    head_grams = jnp.concatenate(
        [lax.dynamic_index_in_dim(head_grams, order_z[z], 0) for z in range(SIDE)], axis=0
    )
    head_grams = jnp.concatenate(
        [lax.dynamic_index_in_dim(head_grams, order_x[x], 1) for x in range(SIDE)], axis=1
    )
    head_grams = head_grams.transpose(2, 0, 1, 3, 4).reshape(2 * head_count, head_dim, head_dim)
    head_grams = head_grams.astype(jnp.float32)
    query_ortho = orthogonal(query_blocks, head_grams[:head_count])
    output_ortho = orthogonal(output_blocks, head_grams[head_count:])
    mom_rows = jnp.concatenate([q_down_mom, key_w_mom, value_w_mom], axis=1).astype(low_type)
    mom_rows = gather_dp(mom_rows)
    mom_rows = jnp.concatenate(gather_heads(mom_rows), axis=0)
    pair_rows = jnp.stack(
        [
            mom_rows[:, latent_width : latent_width + head_dim],
            mom_rows[:, latent_width + head_dim :],
        ]
    )
    shared_iter = (
        orthogonal(q_down_mom[None], gram_of(mom_rows[None, :, :latent_width])),
        orthogonal(jnp.stack([key_w_mom, value_w_mom]), gram_of(pair_rows)),
    )
    q_up_new = own_rows(w_q_up, dp_count, dp_rank) - muon_rate * math.sqrt(
        w_q_up.shape[0] / head_dim
    ) * join_columns(query_ortho)
    out_w_new = own_rows(w_out, dp_count, dp_rank) - muon_rate * math.sqrt(
        w_out.shape[0] / head_dim
    ) * join_columns(output_ortho)
    ffn_factor = muon_rate * math.sqrt(w_gate.shape[0] / FF_BLOCK)
    gate_w_new = own_rows(w_gate, dp_count, dp_rank) - ffn_factor * join_columns(
        ffn_ortho[:ffn_count]
    )
    up_w_new = own_rows(w_up, dp_count, dp_rank) - ffn_factor * join_columns(
        ffn_ortho[ffn_count : 2 * ffn_count]
    )
    down_w_new = own_rows(w_down, dp_count, dp_rank) - ffn_factor * join_columns(
        ffn_ortho[2 * ffn_count :]
    )
    q_down_new = (
        own_rows(w_q_down, all_count, all_rank)
        - muon_rate * math.sqrt(w_q_down.shape[0] / latent_width) * shared_iter[0][0]
    )
    pair_factor = muon_rate * math.sqrt(w_key.shape[0] / head_dim)
    key_w_new = own_rows(w_key, all_count, all_rank) - pair_factor * shared_iter[1][0]
    value_w_new = own_rows(w_value, all_count, all_rank) - pair_factor * shared_iter[1][1]
    return (
        layer_out,
        input_grad,
        gains_grad,
        q_down_grad,
        key_w_grad,
        value_w_grad,
        q_up_grad,
        out_w_grad,
        gate_w_grad,
        up_w_grad,
        down_w_grad,
        gains_mom,
        q_down_mom,
        key_w_mom,
        value_w_mom,
        q_up_mom,
        out_w_mom,
        gate_w_mom,
        up_w_mom,
        down_w_mom,
        gains_new,
        q_down_new,
        key_w_new,
        value_w_new,
        q_up_new,
        out_w_new,
        gate_w_new,
        up_w_new,
        down_w_new,
    )


def solution(mesh):
    placed = (
        P(("dp", "heads"), None),
        P(("dp", "heads"), None),
        P("dp", None),
        P(),
        P(),
        P(),
        P(),
        P(None, "heads"),
        P(None, "heads"),
        P(None, "heads"),
        P(None, "heads"),
        P(None, "heads"),
        P(("dp", "heads")),
        P(("dp", "heads"), None),
        P(("dp", "heads"), None),
        P(("dp", "heads"), None),
        P("dp", "heads"),
        P("dp", "heads"),
        P("dp", "heads"),
        P("dp", "heads"),
        P("dp", "heads"),
    )
    return jax.shard_map(
        on_device,
        mesh=mesh,
        in_specs=placed,
        out_specs=(
            P(("dp", "heads"), None),
            P(("dp", "heads"), None),
            P(("dp", "heads")),
            P(("dp", "heads"), None),
            P(("dp", "heads"), None),
            P(("dp", "heads"), None),
            P("dp", "heads"),
            P("dp", "heads"),
            P("dp", "heads"),
            P("dp", "heads"),
            P("dp", "heads"),
            P(("dp", "heads")),
            P(("dp", "heads"), None),
            P(("dp", "heads"), None),
            P(("dp", "heads"), None),
            P("dp", "heads"),
            P("dp", "heads"),
            P("dp", "heads"),
            P("dp", "heads"),
            P("dp", "heads"),
            P(("dp", "heads")),
            P(("dp", "heads"), None),
            P(("dp", "heads"), None),
            P(("dp", "heads"), None),
            P("dp", "heads"),
            P("dp", "heads"),
            P("dp", "heads"),
            P("dp", "heads"),
            P("dp", "heads"),
        ),
        check_vma=False,
    )
```

time: 864 us -> 768 us (0.89)
  waiting for transfers between devices: 433 us -> 288 us
  starting transfers between devices: 0.79 us -> 139 us
  blocking collectives: 107 us -> 0 us
  Pallas kernels: 0 us -> 33.3 us
  matrix products: 168 us -> 135 us
  between operations: 16.6 us -> 32.9 us
    reduce_scatter x5 -> x0, waiting for transfers between devices: 172 us -> none  [the longest x1 70.1 us: on_device(): lax.psum_scatter(shared_part, 'dp', scatter_dimension=0, tiled=True)]
    ppermute x0 -> x84, waiting for transfers between devices: none -> 164 us  [the longest x48 102 us: shift_heads(): return lax.ppermute(values, 'heads', pairs)]
    ppermute x0 -> x84, starting transfers between devices: none -> 134 us  [the longest x48 87.8 us: shift_heads(): return lax.ppermute(values, 'heads', pairs)]
    unnamed x16 -> x5, waiting for transfers between devices: 107 us -> 0.75 us
    all_gather x5 -> x1, waiting for transfers between devices: 112 us -> 14.7 us  [on_device(): lax.all_gather(cotangent, 'heads', axis=0, tiled=True)]
    unnamed x1 -> x0, blocking collectives: 70.9 us -> none
    psum x1, waiting for transfers between devices: 16.1 us -> 81.8 us  [on_device(): lax.psum(gram_of(ffn_blocks).astype(low_type), 'dp').astype(jnp.float32)]
    pallas_call x0 -> x5, Pallas kernels: none -> 33.3 us  [the longest x3 19 us: place_blocks(): pl.pallas_call(place_kernel, grid_spec=pltpu.PrefetchScalarGridSpec(num_s...]
  transfers between devices with their start and end apart: 14 -> 89, of which waited for: 12 -> 39; matrix products, arithmetic and copies ran while one was open for 17% -> 25% of each run, Pallas kernels for 0% -> 3%
where the time goes in v2:
time: 768 us; the launch traced here: 756 us
  waiting for transfers between devices  288 us (38%)
  starting transfers between devices  139 us (18%)
  matrix products  135 us (18%)
  local copies, waits for them, and re-layouts  73.1 us (10%)
  other arithmetic  54.9 us (7%)
  Pallas kernels  33.3 us (4%)
  between operations  32.9 us (4%)
    ppermute x48, waiting for transfers between devices, shift_heads(): return lax.ppermute(values, 'heads', pairs)  102 us
    ppermute x48, starting transfers between devices, shift_heads(): return lax.ppermute(values, 'heads', pairs)  87.8 us
    psum x1, waiting for transfers between devices, on_device(): lax.psum(gram_of(ffn_blocks).astype(low_type), 'dp').astype(jnp.float32)  81.8 us
    ppermute x36, waiting for transfers between devices, shift_dp(): return lax.ppermute(values, 'dp', pairs)  61.5 us
    dot_general x60, matrix products, times(): jnp.einsum('brc,bcd->brd', left.astype(low_type), right.astype(low_type),...  49.9 us
    ppermute x36, starting transfers between devices, shift_dp(): return lax.ppermute(values, 'dp', pairs)  46.5 us
    unnamed x253, local copies, waits for them, and re-layouts  42.9 us
    dot_general x13, matrix products, matmul_nt(): lax.dot_general(left, right, (((1,), (1,)), ((), ())), preferred_element_...  31.4 us
  transfers between devices with their start and end apart: 89, of which 39 were waited for; matrix products, arithmetic and copies ran while one was open for 25% of the time, Pallas kernels for 3%

profile of v2, /device:TPU:1, one launch (start us, length us, event | category | flops | bytes accessed | tf_op | source)
XLA Modules:
  0.0 756.4 jit_solution(11941844966168389789)
XLA Ops:
  23.8 27.4 %all-gather.3.cloned.1.call-done = bf16[1024,1536]{1,0:T(8,128)(2,1)} async-done(((bf16[128,1536]{1,0:T(8,128)(2,1)}), bf16[1024,1536]{1,0:T(8,128)(2,1)}) %all-gather.3.cloned.1.call-update) | async-done | bytes 3145744 | tf_op jit(solution)/shard_map/all_gather | solution.py:471
  55.2 7.2 attend.1
  76.9 14.7 %all-gather.5.cloned.1.call-done.source = bf16[1024,2048]{1,0:T(8,128)(2,1)} async-done(((bf16[128,2048]{1,0:T(8,128)(2,1)}), bf16[1024,2048]{1,0:T(8,128)(2,1)}) %all-gather.5.cloned.1.call-update) | async-done | bytes 4194320 | tf_op jit(solution)/shard_map/all_gather | solution.py:489
  91.6 7.3 place_blocks.3
  98.9 7.0 collective-permute-done.2
  128.0 9.7 %collective-permute-done.6 = bf16[128,2048]{1,0:T(8,128)(2,1)S(1)} collective-permute-done((bf16[128,2048]{1,0:T(8,128)(2,1)S(1)}, bf16[128,2048]{1,0:T(8,128)(2,1)S(1)}, u32[]{:S(2)}, u32[]{:S(2)}) %collective-permute-start.6) | collective-permute-done | bytes 524320 | tf_op jit(solution)/shard_map/ppermute | solution.py:92
  143.2 5.5 multiply_convert_fusion.1
  191.0 6.3 place_blocks.5
  210.4 7.6 %convolution_convert_fusion = bf16[2048,1408]{0,1:T(8,128)(2,1)S(1)} fusion(bf16[1024,2048]{1,0:T(8,128)(2,1)S(1)} %copy-done.77, bf16[1024,704]{0,1:T(8,128)(2,1)S(1)} %copy-done.59, bf16[1024,704]{0,1:T(8,128)(2,1)S(1)} %copy-done.55), kind=kOutput, calls=%fused_computation.1 | convolution fusion | flops 5914230784 | bytes 12845056 | tf_op jit(solution)/shard_map/dot_general | solution.py:36
  220.1 11.9 %collective-permute-done.13 = bf16[128,2048]{1,0:T(8,128)(2,1)S(1)} collective-permute-done((bf16[128,2048]{1,0:T(8,128)(2,1)S(1)}, bf16[128,2048]{1,0:T(8,128)(2,1)S(1)}, u32[]{:S(2)}, u32[]{:S(2)}) %collective-permute-start.13) | collective-permute-done | bytes 524320 | tf_op jit(solution)/shard_map/ppermute | solution.py:92
  243.8 15.5 %collective-permute-done.15 = bf16[128,2048]{1,0:T(8,128)(2,1)S(1)} collective-permute-done((bf16[128,2048]{1,0:T(8,128)(2,1)S(1)}, bf16[128,2048]{1,0:T(8,128)(2,1)S(1)}, u32[]{:S(2)}, u32[]{:S(2)}) %collective-permute-start.15) | collective-permute-done | bytes 524320 | tf_op jit(solution)/shard_map/ppermute | solution.py:92
  270.9 7.1 attend_back.1
  290.1 11.6 %copy.217 = bf16[2048,2112]{1,0:T(8,128)(2,1)} copy(bf16[2048,2112]{0,1:T(8,128)(2,1)} %pad_maximum_fusion) | data formatting | bytes 17301504
  305.0 20.4 %collective-permute-done.54 = bf16[4,192,512]{2,1,0:T(8,128)(2,1)} collective-permute-done((bf16[4,192,512]{2,1,0:T(8,128)(2,1)}, bf16[4,192,512]{2,1,0:T(8,128)(2,1)}, u32[]{:S(2)}, u32[]{:S(2)}) %collective-permute-start.54) | collective-permute-done | bytes 786464 | tf_op jit(solution)/shard_map/ppermute | solution.py:101
  347.4 12.3 %collective-permute-done.57 = bf16[192,512]{0,1:T(8,128)(2,1)} collective-permute-done((bf16[192,512]{0,1:T(8,128)(2,1)}, bf16[192,512]{0,1:T(8,128)(2,1)}, u32[]{:S(2)}, u32[]{:S(2)}) %collective-permute-start.57) | collective-permute-done | bytes 196640 | tf_op jit(solution)/shard_map/ppermute | solution.py:101
  418.7 6.6 collective-permute-done.27
  425.3 8.1 %collective-permute-done.28 = bf16[128,1536]{1,0:T(8,128)(2,1)S(1)} collective-permute-done((bf16[128,1536]{1,0:T(8,128)(2,1)S(1)}, bf16[128,1536]{1,0:T(8,128)(2,1)S(1)}, u32[]{:S(2)}, u32[]{:S(2)}) %collective-permute-start.28) | collective-permute-done | bytes 393248 | tf_op jit(solution)/shard_map/ppermute | solution.py:92
  454.8 7.1 collective-permute-done.33
  537.0 15.7 %collective-permute-start.68 = (bf16[256,1536]{1,0:T(8,128)(2,1)S(1)}, bf16[256,1536]{1,0:T(8,128)(2,1)S(1)}, u32[]{:S(2)}, u32[]{:S(2)}) collective-permute-start(bf16[256,1536]{1,0:T(8,128)(2,1)S(1)} %get-tuple-element.275), channel_id=1, source_target_pairs={{0,1},{1,0},{2,3},{3,2},{4,5},{5,4},{6,7},{7,6},{8,9},{9,8},{10,11... | collective-permute-start | bytes 2359304 | tf_op jit(solution)/shard_map/ppermute | solution.py:92
  553.8 14.8 %collective-permute-done.65 = bf16[256,1536]{1,0:T(8,128)(2,1)S(1)} collective-permute-done((bf16[256,1536]{1,0:T(8,128)(2,1)S(1)}, bf16[256,1536]{1,0:T(8,128)(2,1)S(1)}, u32[]{:S(2)}, u32[]{:S(2)}) %collective-permute-start.65) | collective-permute-done | bytes 786464 | tf_op jit(solution)/shard_map/ppermute | solution.py:92
  568.6 10.2 %collective-permute-start.69 = (bf16[256,1536]{1,0:T(8,128)(2,1)S(1)}, bf16[256,1536]{1,0:T(8,128)(2,1)S(1)}, u32[]{:S(2)}, u32[]{:S(2)}) collective-permute-start(bf16[256,1536]{1,0:T(8,128)(2,1)S(1)} %collective-permute-done.65), channel_id=1, source_target_pairs={{0,1},{1,0},{2,3},{3,2},{4,5},{5,4},{6,7},{7,6},{8,9},{9,8},{10,11... | collective-permute-start | bytes 2359304 | tf_op jit(solution)/shard_map/ppermute | solution.py:92
  595.5 10.7 %select_reduce_fusion = (f32[]{:T(128)}, f32[1024,1024]{1,0:T(8,128)}) fusion(bf16[2048,1536]{1,0:T(8,128)(2,1)} %copy-done.60), kind=kOutput, calls=%fused_computation.12 | convolution fusion | flops 4298113024 | bytes 8388612 | tf_op jit(solution)/shard_map/brc,brd->bcd/dot_general | solution.py:371
  636.4 7.8 %add_convert_fusion = bf16[1024,1024]{1,0:T(8,128)(2,1)S(1)} fusion(f32[1024,1024]{1,0:T(8,128)} %fusion.303, f32[1024,1024]{1,0:T(8,128)} %copy-done.101, bf16[1024,1024]{1,0:T(8,128)(2,1)} %copy-done.102), kind=kOutput, calls=%fused_computation.8 | convolution fusion | flops 2153775104 | bytes 12582912 | tf_op jit(solution)/shard_map/brc,bcd->brd/dot_general | solution.py:375
  646.4 81.8 %all-reduce.2.cloned.1.call-done = bf16[6,352,352]{2,1,0:T(8,128)(2,1)} async-done(((bf16[6,352,352]{2,1,0:T(8,128)(2,1)}), bf16[6,352,352]{2,1,0:T(8,128)(2,1)}) %all-reduce.2.cloned.1.call-update) | async-done | bytes 1486864 | tf_op jit(solution)/shard_map/psum | solution.py:625
  (631 shorter events, 389.0 us)
Async XLA Ops:
  7.2 44.0 %all-gather.3.cloned.1.call-start = ((), (), s32[]{:S(2)}) async-start(), calls=%async_computation.2 | async-start | bytes 3538944 | tf_op jit(solution)/shard_map/all_gather | solution.py:471
  19.6 72.0 %all-gather.5.cloned.1.call-start = ((), (), s32[]{:S(2)}) async-start(), calls=%async_computation.3 | async-start | bytes 4718592 | tf_op jit(solution)/shard_map/all_gather | solution.py:489
  72.6 26.3 %collective-permute-start.1 = (bf16[128,2048]{1,0:T(8,128)(2,1)}, bf16[128,2048]{1,0:T(8,128)(2,1)}, u32[]{:S(2)}, u32[]{:S(2)}) collective-permute-start(bf16[128,2048]{1,0:T(8,128)(2,1)} %get-tuple-element.230), channel_id=1, source_target_pairs={{0,2},{1,3},{2,4},{3,5},{4,6},{5,7},{6,0},{7,1},{8,10},{9,11},{10,... | collective-permute-start | bytes 1572872 | tf_op jit(solution)/shard_map/ppermute | solution.py:92
  73.4 32.5 %collective-permute-start.2 = (bf16[128,2048]{1,0:T(8,128)(2,1)}, bf16[128,2048]{1,0:T(8,128)(2,1)}, u32[]{:S(2)}, u32[]{:S(2)}) collective-permute-start(bf16[128,2048]{1,0:T(8,128)(2,1)} %get-tuple-element.232), channel_id=1, source_target_pairs={{0,4},{1,5},{2,6},{3,7},{4,0},{5,1},{6,2},{7,3},{8,12},{9,13},{10,... | collective-permute-start | bytes 1572872 | tf_op jit(solution)/shard_map/ppermute | solution.py:92
  75.8 30.1 %collective-permute-start.3 = (bf16[128,2048]{1,0:T(8,128)(2,1)}, bf16[128,2048]{1,0:T(8,128)(2,1)}, u32[]{:S(2)}, u32[]{:S(2)}) collective-permute-start(bf16[128,2048]{1,0:T(8,128)(2,1)} %get-tuple-element.231), channel_id=1, source_target_pairs={{0,6},{1,7},{2,0},{3,1},{4,2},{5,3},{6,4},{7,5},{8,14},{9,15},{10,... | collective-permute-start | bytes 1572872 | tf_op jit(solution)/shard_map/ppermute | solution.py:92
  153.9 47.4 %collective-permute-start.11 = (bf16[512,2048]{1,0:T(8,128)(2,1)}, bf16[512,2048]{1,0:T(8,128)(2,1)}, u32[]{:S(2)}, u32[]{:S(2)}) collective-permute-start(bf16[512,2048]{1,0:T(8,128)(2,1)} %add_convert_fusion.3), channel_id=1, source_target_pairs={{0,1},{1,0},{2,3},{3,2},{4,5},{5,4},{6,7},{7,6},{8,9},{9,8},{10,11... | collective-permute-start | bytes 6291464 | tf_op jit(solution)/shard_map/ppermute | solution.py:92
  158.4 25.2 %all-to-all-start = ((bf16[8,128,256]{1,2,0:T(8,128)(2,1)}), bf16[8,128,256]{1,2,0:T(8,128)(2,1)}, u32[]{:S(2)}, u32[]{:S(2)}) async-start(bf16[8,128,256]{1,2,0:T(8,128)(2,1)} %bitcast.389), calls=%async_computation | async-start | bytes 1048576 | tf_op jit(solution)/shard_map/all_to_all | solution.py:478
  162.6 466.4 %reduce-scatter.4.cloned.1.call-start = ((), (), s32[]{:S(2)}) async-start(), calls=%async_computation.5 | async-start | bytes 9469952
  207.0 25.0 %collective-permute-start.13 = (bf16[128,2048]{1,0:T(8,128)(2,1)S(1)}, bf16[128,2048]{1,0:T(8,128)(2,1)S(1)}, u32[]{:S(2)}, u32[]{:S(2)}) collective-permute-start(bf16[128,2048]{1,0:T(8,128)(2,1)S(1)} %get-tuple-element.229), channel_id=1, source_target_pairs={{0,4},{1,5},{2,6},{3,7},{4,0},{5,1},{6,2},{7,3},{8,12},{9,13},{10,... | collective-permute-start | bytes 1572872 | tf_op jit(solution)/shard_map/ppermute | solution.py:92
  234.7 24.6 %collective-permute-start.15 = (bf16[128,2048]{1,0:T(8,128)(2,1)S(1)}, bf16[128,2048]{1,0:T(8,128)(2,1)S(1)}, u32[]{:S(2)}, u32[]{:S(2)}) collective-permute-start(bf16[128,2048]{1,0:T(8,128)(2,1)S(1)} %get-tuple-element.205), channel_id=1, source_target_pairs={{0,6},{1,7},{2,0},{3,1},{4,2},{5,3},{6,4},{7,5},{8,14},{9,15},{10,... | collective-permute-start | bytes 1572872 | tf_op jit(solution)/shard_map/ppermute | solution.py:92
  237.6 26.2 %collective-permute-start.17 = (bf16[128,2048]{1,0:T(8,128)(2,1)S(1)}, bf16[128,2048]{1,0:T(8,128)(2,1)S(1)}, u32[]{:S(2)}, u32[]{:S(2)}) collective-permute-start(bf16[128,2048]{1,0:T(8,128)(2,1)S(1)} %get-tuple-element.205), channel_id=1, source_target_pairs={{0,2},{1,3},{2,4},{3,5},{4,6},{5,7},{6,0},{7,1},{8,10},{9,11},{10,... | collective-permute-start | bytes 1572872 | tf_op jit(solution)/shard_map/ppermute | solution.py:92
  282.4 43.1 %collective-permute-start.54 = (bf16[4,192,512]{2,1,0:T(8,128)(2,1)}, bf16[4,192,512]{2,1,0:T(8,128)(2,1)}, u32[]{:S(2)}, u32[]{:S(2)}) collective-permute-start(bf16[4,192,512]{2,1,0:T(8,128)(2,1)} %get-tuple-element.218), channel_id=1, source_target_pairs={{0,16},{8,24},{16,0},{24,8},{32,48},{40,56},{48,32},{56,40},{64,80... | collective-permute-start | bytes 2359304 | tf_op jit(solution)/shard_map/ppermute | solution.py:101
  284.8 42.3 %collective-permute-start.55 = (bf16[4,192,512]{2,1,0:T(8,128)(2,1)}, bf16[4,192,512]{2,1,0:T(8,128)(2,1)}, u32[]{:S(2)}, u32[]{:S(2)}) collective-permute-start(bf16[4,192,512]{2,1,0:T(8,128)(2,1)} %get-tuple-element.219), channel_id=1, source_target_pairs={{0,24},{8,0},{16,8},{24,16},{32,56},{40,32},{48,40},{56,48},{64,88... | collective-permute-start | bytes 2359304 | tf_op jit(solution)/shard_map/ppermute | solution.py:101
  301.8 426.4 %all-reduce.2.cloned.1.call-start = ((), (), s32[]{:S(2)}) async-start(), calls=%async_computation.4 | async-start | bytes 3244032 | tf_op jit(solution)/shard_map/psum | solution.py:625
  371.1 40.5 %collective-permute-start.26 = (bf16[512,1536]{1,0:T(8,128)(2,1)}, bf16[512,1536]{1,0:T(8,128)(2,1)}, u32[]{:S(2)}, u32[]{:S(2)}) collective-permute-start(bf16[512,1536]{1,0:T(8,128)(2,1)} %pad_maximum_fusion.1), channel_id=1, source_target_pairs={{0,1},{1,0},{2,3},{3,2},{4,5},{5,4},{6,7},{7,6},{8,9},{9,8},{10,11... | collective-permute-start | bytes 4718600 | tf_op jit(solution)/shard_map/ppermute | solution.py:92
  390.3 106.3 %collective-permute-start.22 = (bf16[512,2048]{1,0:T(8,128)(2,1)}, bf16[512,2048]{1,0:T(8,128)(2,1)}, u32[]{:S(2)}, u32[]{:S(2)}) collective-permute-start(bf16[512,2048]{1,0:T(8,128)(2,1)} %convolution_convert_fusion.3), channel_id=1, source_target_pairs={{0,1},{1,0},{2,3},{3,2},{4,5},{5,4},{6,7},{7,6},{8,9},{9,8},{10,11... | collective-permute-start | bytes 6291464 | tf_op jit(solution)/shard_map/ppermute | solution.py:92
  484.8 45.6 %collective-permute-start.37 = (f32[1,40]{1,0:T(1,128)S(1)}, f32[1,40]{1,0:T(1,128)S(1)}, u32[]{:S(2)}, u32[]{:S(2)}) collective-permute-start(f32[1,40]{1,0:T(1,128)S(1)} %get-tuple-element.315), channel_id=1, source_target_pairs={{0,32},{8,40},{16,48},{24,56},{32,64},{40,72},{48,80},{56,88},{64,... | collective-permute-start | bytes 488 | tf_op jit(solution)/shard_map/ppermute | solution.py:101
  488.5 42.1 %collective-permute-start.38 = (f32[1,40]{1,0:T(1,128)S(1)}, f32[1,40]{1,0:T(1,128)S(1)}, u32[]{:S(2)}, u32[]{:S(2)}) collective-permute-start(f32[1,40]{1,0:T(1,128)S(1)} %get-tuple-element.317), channel_id=1, source_target_pairs={{0,64},{8,72},{16,80},{24,88},{32,96},{40,104},{48,112},{56,120},{... | collective-permute-start | bytes 488 | tf_op jit(solution)/shard_map/ppermute | solution.py:101
  506.5 25.8 %collective-permute-start.39 = (f32[1,40]{1,0:T(1,128)S(1)}, f32[1,40]{1,0:T(1,128)S(1)}, u32[]{:S(2)}, u32[]{:S(2)}) collective-permute-start(f32[1,40]{1,0:T(1,128)S(1)} %get-tuple-element.316), channel_id=1, source_target_pairs={{0,96},{8,104},{16,112},{24,120},{32,0},{40,8},{48,16},{56,24},{64... | collective-permute-start | bytes 488 | tf_op jit(solution)/shard_map/ppermute | solution.py:101
  508.3 28.3 %collective-permute-start.23 = (bf16[128,2048]{1,0:T(8,128)(2,1)S(1)}, bf16[128,2048]{1,0:T(8,128)(2,1)S(1)}, u32[]{:S(2)}, u32[]{:S(2)}) collective-permute-start(bf16[128,2048]{1,0:T(8,128)(2,1)S(1)} %get-tuple-element.224), channel_id=1, source_target_pairs={{0,2},{1,3},{2,4},{3,5},{4,6},{5,7},{6,0},{7,1},{8,10},{9,11},{10,... | collective-permute-start | bytes 1572872 | tf_op jit(solution)/shard_map/ppermute | solution.py:92
  530.6 38.1 %collective-permute-start.65 = (bf16[256,1536]{1,0:T(8,128)(2,1)S(1)}, bf16[256,1536]{1,0:T(8,128)(2,1)S(1)}, u32[]{:S(2)}, u32[]{:S(2)}) collective-permute-start(bf16[256,1536]{1,0:T(8,128)(2,1)S(1)} %get-tuple-element.275), channel_id=1, source_target_pairs={{0,6},{1,7},{2,0},{3,1},{4,2},{5,3},{6,4},{7,5},{8,14},{9,15},{10,... | collective-permute-start | bytes 2359304 | tf_op jit(solution)/shard_map/ppermute | solution.py:92
  533.6 45.4 %collective-permute-start.66 = (bf16[256,1536]{1,0:T(8,128)(2,1)S(1)}, bf16[256,1536]{1,0:T(8,128)(2,1)S(1)}, u32[]{:S(2)}, u32[]{:S(2)}) collective-permute-start(bf16[256,1536]{1,0:T(8,128)(2,1)S(1)} %get-tuple-element.275), channel_id=1, source_target_pairs={{0,4},{1,5},{2,6},{3,7},{4,0},{5,1},{6,2},{7,3},{8,12},{9,13},{10,... | collective-permute-start | bytes 2359304 | tf_op jit(solution)/shard_map/ppermute | solution.py:92
  536.6 42.6 %collective-permute-start.67 = (bf16[256,1536]{1,0:T(8,128)(2,1)S(1)}, bf16[256,1536]{1,0:T(8,128)(2,1)S(1)}, u32[]{:S(2)}, u32[]{:S(2)}) collective-permute-start(bf16[256,1536]{1,0:T(8,128)(2,1)S(1)} %get-tuple-element.275), channel_id=1, source_target_pairs={{0,2},{1,3},{2,4},{3,5},{4,6},{5,7},{6,0},{7,1},{8,10},{9,11},{10,... | collective-permute-start | bytes 2359304 | tf_op jit(solution)/shard_map/ppermute | solution.py:92
  537.0 42.9 %collective-permute-start.68 = (bf16[256,1536]{1,0:T(8,128)(2,1)S(1)}, bf16[256,1536]{1,0:T(8,128)(2,1)S(1)}, u32[]{:S(2)}, u32[]{:S(2)}) collective-permute-start(bf16[256,1536]{1,0:T(8,128)(2,1)S(1)} %get-tuple-element.275), channel_id=1, source_target_pairs={{0,1},{1,0},{2,3},{3,2},{4,5},{5,4},{6,7},{7,6},{8,9},{9,8},{10,11... | collective-permute-start | bytes 2359304 | tf_op jit(solution)/shard_map/ppermute | solution.py:92
  (168 other events, 2704.6 us)
Sparse Core Ops, SparseCore 0:
  19.7 31.4 all-gather.2
  52.9 38.6 all-gather.4
  301.9 99.7 reduce-scatter.3
  634.4 93.7 all-reduce.1

commit v3 on v2

--- a/solution.py
+++ b/solution.py
@@ -148,21 +148,43 @@
     return (ids_q == ids_k) & (key_at <= query_at)
 
 
-def attend_kernel(
-    slots, latent, weight, keys, values, cosine, sine, ids_q, ids_k, query_out, mixed_out, lse_out
-):
-    row_len, head_dim = keys.shape
-    piece = row_len // (SIDE * CORES)
+def block_at(index, piece):
+    return pl.ds(pl.multiple_of(index * piece, piece), piece)
+
+
+def store_by_distance(where, rows_ref, near_ref, far_ref, piece):
+    core = where[SIDE * CORES]
+    for step in range(SIDE):
+        near = CORES * step + core
+        far = CORES * step + 1 - core
+        near_ref[block_at(where[near], piece), :] = rows_ref[block_at(near, piece), :]
+        far_ref[block_at(where[far] - SIDE, piece), :] = rows_ref[block_at(far, piece), :]
+
+
+def attend_kernel(where, owner, *refs):
+    pieces = refs[: SIDE * CORES]
+    weight, cosine, sine, ids_q, ids_k = refs[SIDE * CORES : SIDE * CORES + 5]
+    packed, query_out, near_out, far_out, lse_out, mixed_rows = refs[SIDE * CORES + 5 :]
+    latent_width, head_dim = weight.shape
+    piece = pieces[0].shape[0]
     block = CORES * piece
     scale = head_dim ** (-0.5)
+
+    @pl.when(pl.program_id(0) == 0)
+    def _():
+        for index, source in enumerate(pieces):
+            packed[block_at(owner[index], piece), :] = source[...]
+
+    key_cols = slice(latent_width, latent_width + head_dim)
+    value_cols = slice(latent_width + head_dim, latent_width + 2 * head_dim)
     for index in range(SIDE):
         first = index * block
         end = first + block
         rows = slice(first, end)
-        query = rotate(matmul(latent[rows, :], weight[...]), cosine[rows, :], sine[rows, :])
-        query = query.astype(low_type)
+        query = matmul(packed[rows, :latent_width], weight[...])
+        query = rotate(query, cosine[rows, :], sine[rows, :]).astype(low_type)
         query_out[rows, :] = query
-        scores = matmul_nt(query, keys[:end, :]) * scale
+        scores = matmul_nt(query, packed[:end, key_cols]) * scale
         allowed = visible(ids_q[rows, :], ids_k[:, :end], first, block, end)
         scores = jnp.where(allowed, scores, -1e30)
         row_max = jnp.max(scores, axis=-1, keepdims=True)
@@ -170,42 +192,44 @@
         row_total = jnp.sum(exponent, axis=-1, keepdims=True)
         probs = (exponent * (1.0 / row_total)).astype(low_type)
         lse_out[0, rows, :] = row_max + jnp.log(row_total)
-        mixed = matmul(probs, values[:end, :]).astype(low_type)
-        for side in range(CORES):
-            place = pl.multiple_of(slots[CORES * index + side] * piece, piece)
-            mixed_out[pl.ds(place, piece), :] = mixed[side * piece : (side + 1) * piece, :]
-
-
-def attend(slots, latent_rows, w_q_up, key_rows, value_rows, cosine, sine, row_ids):
-    row_len, head_dim = key_rows.shape
+        mixed_rows[rows, :] = matmul(probs, packed[:end, value_cols]).astype(low_type)
+    store_by_distance(where, mixed_rows, near_out, far_out, piece)
+
+
+def attend(where, owner, pieces, w_q_up, head_dim, cosine, sine, row_ids):
+    piece, packed_width = pieces[0].shape
+    row_len = piece * SIDE * CORES
     latent_width, width = w_q_up.shape
     count = width // head_dim
-    whole = lambda head, slots: (0, 0)
-    column = lambda head, slots: (0, head)
+    whole = lambda head, where, owner: (0, 0)
+    column = lambda head, where, owner: (0, head)
     return pl.pallas_call(
         attend_kernel,
         grid_spec=pltpu.PrefetchScalarGridSpec(
-            num_scalar_prefetch=1,
+            num_scalar_prefetch=2,
             grid=(count,),
-            in_specs=[
-                pl.BlockSpec((row_len, latent_width), whole),
+            in_specs=[pl.BlockSpec((piece, packed_width), whole)] * (SIDE * CORES)
+            + [
                 pl.BlockSpec((latent_width, head_dim), column),
-                pl.BlockSpec((row_len, head_dim), whole),
-                pl.BlockSpec((row_len, head_dim), whole),
                 pl.BlockSpec((row_len, head_dim // 2), whole),
                 pl.BlockSpec((row_len, head_dim // 2), whole),
                 pl.BlockSpec((row_len, 1), whole),
                 pl.BlockSpec((1, row_len), whole),
             ],
             out_specs=[
+                pl.BlockSpec((row_len, packed_width), whole),
                 pl.BlockSpec((row_len, head_dim), column),
-                pl.BlockSpec((row_len, head_dim), column),
-                pl.BlockSpec((1, row_len, 1), lambda head, slots: (head, 0, 0)),
+                pl.BlockSpec((row_len // 2, head_dim), column),
+                pl.BlockSpec((row_len // 2, head_dim), column),
+                pl.BlockSpec((1, row_len, 1), lambda head, where, owner: (head, 0, 0)),
             ],
+            scratch_shapes=[pltpu.VMEM((row_len, head_dim), low_type)],
         ),
         out_shape=[
+            jax.ShapeDtypeStruct((row_len, packed_width), low_type),
             jax.ShapeDtypeStruct((row_len, width), low_type),
-            jax.ShapeDtypeStruct((row_len, width), low_type),
+            jax.ShapeDtypeStruct((row_len // 2, width), low_type),
+            jax.ShapeDtypeStruct((row_len // 2, width), low_type),
             jax.ShapeDtypeStruct((count, row_len, 1), jnp.float32),
         ],
         compiler_params=pltpu.CompilerParams(vmem_limit_bytes=vmem_bytes),
@@ -215,84 +239,90 @@
             transcendentals=count * row_len * row_len,
         ),
         name="attend",
-    )(
-        slots,
-        latent_rows,
-        w_q_up,
-        key_rows,
-        value_rows,
-        cosine,
-        sine,
-        row_ids[:, None],
-        row_ids[None, :],
-    )
+    )(where, owner, *pieces, w_q_up, cosine, sine, row_ids[:, None], row_ids[None, :])
 
 
 def attend_back_kernel(
-    slots,
+    where,
     query_in,
-    keys,
-    values,
+    packed,
     mixed_back,
     lse,
     cosine,
     sine,
     ids_q,
     ids_k,
+    weight,
+    weight_back,
+    near_out,
+    far_out,
     query_back,
-    pair_back,
-    key_sum,
-    value_sum,
+    totals,
 ):
-    row_len, head_dim = keys.shape
+    row_len, packed_width = packed.shape
+    latent_width, head_dim = weight.shape
     piece = row_len // (SIDE * CORES)
     block = CORES * piece
     scale = head_dim ** (-0.5)
     head = pl.program_id(0)
+    key_cols = slice(latent_width, latent_width + head_dim)
+    value_cols = slice(latent_width + head_dim, latent_width + 2 * head_dim)
 
     @pl.when(head == 0)
     def _():
-        key_sum[...] = jnp.zeros_like(key_sum)
-        value_sum[...] = jnp.zeros_like(value_sum)
+        totals[...] = jnp.zeros_like(totals)
 
     for index in range(SIDE):
         first = index * block
         end = first + block
         rows = slice(first, end)
-        places = [
-            pl.multiple_of(slots[CORES * index + side] * piece, piece) for side in range(CORES)
-        ]
         query = query_in[rows, :]
-        back = jnp.concatenate([mixed_back[pl.ds(place, piece), :] for place in places], axis=0)
-        scores = matmul_nt(query, keys[:end, :]) * scale
+        back = jnp.concatenate(
+            [
+                mixed_back[block_at(where[CORES * index + side], piece), :]
+                for side in range(CORES)
+            ],
+            axis=0,
+        )
+        keys = packed[:end, key_cols]
+        scores = matmul_nt(query, keys) * scale
         allowed = visible(ids_q[rows, :], ids_k[:, :end], first, block, end)
         probs = jnp.where(allowed, jnp.exp(scores - lse[0, rows, :]), 0.0)
-        probs_back = matmul_nt(back, values[:end, :])
+        probs_back = matmul_nt(back, packed[:end, value_cols])
         inner = jnp.sum(probs * probs_back, axis=-1, keepdims=True)
         score_back = (probs * (probs_back - inner)).astype(low_type)
-        probs_low = probs.astype(low_type)
-        value_sum[:end, :] += matmul_tn(probs_low, back)
-        key_sum[:end, :] += matmul_tn(score_back, query) * scale
-        query_grad = matmul(score_back, keys[:end, :]) * scale
-        query_grad = rotate_back(query_grad, cosine[rows, :], sine[rows, :]).astype(low_type)
-        for side, place in enumerate(places):
-            query_back[pl.ds(place, piece), :] = query_grad[side * piece : (side + 1) * piece, :]
+        totals[:end, value_cols] += matmul_tn(probs.astype(low_type), back)
+        totals[:end, key_cols] += matmul_tn(score_back, query) * scale
+        query_grad = matmul(score_back, keys) * scale
+        query_back[rows, :] = rotate_back(query_grad, cosine[rows, :], sine[rows, :]).astype(
+            low_type
+        )
+    weight_back[...] = matmul_tn(packed[:, :latent_width], query_back[...]).astype(low_type)
+    for index in range(SIDE):
+        rows = slice(index * block, (index + 1) * block)
+        totals[rows, :latent_width] += matmul_nt(query_back[rows, :], weight[...])
 
     @pl.when(head == pl.num_programs(0) - 1)
     def _():
-        for index in range(SIDE * CORES):
-            place = pl.multiple_of(slots[index] * piece, piece)
-            rows = slice(index * piece, (index + 1) * piece)
-            pair_back[pl.ds(place, piece), :head_dim] = key_sum[rows, :].astype(low_type)
-            pair_back[pl.ds(place, piece), head_dim:] = value_sum[rows, :].astype(low_type)
-
-
-def attend_back(slots, query_rows, key_rows, value_rows, mixed_back, lse, cosine, sine, row_ids):
-    row_len, head_dim = key_rows.shape
-    width = query_rows.shape[1]
+        core = where[SIDE * CORES]
+        for step in range(SIDE):
+            near = CORES * step + core
+            far = CORES * step + 1 - core
+            near_out[block_at(where[near], piece), :] = totals[block_at(near, piece), :].astype(
+                low_type
+            )
+            far_out[block_at(where[far] - SIDE, piece), :] = totals[
+                block_at(far, piece), :
+            ].astype(low_type)
+
+
+def attend_back(where, query_rows, packed, mixed_back, lse, cosine, sine, row_ids, w_q_up):
+    row_len, packed_width = packed.shape
+    latent_width, width = w_q_up.shape
+    head_dim = (packed_width - latent_width) // 2
     count = width // head_dim
-    whole = lambda head, slots: (0, 0)
-    column = lambda head, slots: (0, head)
+    whole = lambda head, where: (0, 0)
+    column = lambda head, where: (0, head)
     return pl.pallas_call(
         attend_back_kernel,
         grid_spec=pltpu.PrefetchScalarGridSpec(
@@ -300,27 +330,29 @@
             grid=(count,),
             in_specs=[
                 pl.BlockSpec((row_len, head_dim), column),
-                pl.BlockSpec((row_len, head_dim), whole),
-                pl.BlockSpec((row_len, head_dim), whole),
+                pl.BlockSpec((row_len, packed_width), whole),
                 pl.BlockSpec((row_len, head_dim), column),
-                pl.BlockSpec((1, row_len, 1), lambda head, slots: (head, 0, 0)),
+                pl.BlockSpec((1, row_len, 1), lambda head, where: (head, 0, 0)),
                 pl.BlockSpec((row_len, head_dim // 2), whole),
                 pl.BlockSpec((row_len, head_dim // 2), whole),
                 pl.BlockSpec((row_len, 1), whole),
                 pl.BlockSpec((1, row_len), whole),
+                pl.BlockSpec((latent_width, head_dim), column),
             ],
             out_specs=[
-                pl.BlockSpec((row_len, head_dim), column),
-                pl.BlockSpec((row_len, 2 * head_dim), whole),
+                pl.BlockSpec((latent_width, head_dim), column),
+                pl.BlockSpec((row_len // 2, packed_width), whole),
+                pl.BlockSpec((row_len // 2, packed_width), whole),
             ],
             scratch_shapes=[
-                pltpu.VMEM((row_len, head_dim), jnp.float32),
-                pltpu.VMEM((row_len, head_dim), jnp.float32),
+                pltpu.VMEM((row_len, head_dim), low_type),
+                pltpu.VMEM((row_len, packed_width), jnp.float32),
             ],
         ),
         out_shape=[
-            jax.ShapeDtypeStruct((row_len, width), low_type),
-            jax.ShapeDtypeStruct((row_len, 2 * head_dim), low_type),
+            jax.ShapeDtypeStruct((latent_width, width), low_type),
+            jax.ShapeDtypeStruct((row_len // 2, packed_width), low_type),
+            jax.ShapeDtypeStruct((row_len // 2, packed_width), low_type),
         ],
         compiler_params=pltpu.CompilerParams(vmem_limit_bytes=vmem_bytes),
         cost_estimate=pl.CostEstimate(
@@ -330,24 +362,24 @@
         ),
         name="attend_back",
     )(
-        slots,
+        where,
         query_rows,
-        key_rows,
-        value_rows,
+        packed,
         mixed_back,
         lse,
         cosine,
         sine,
         row_ids[:, None],
         row_ids[None, :],
-    )
-
-
-def place_kernel(slots, source, target):
+        w_q_up,
+    )
+
+
+def place_kernel(where, source, target):
     target[...] = source[...]
 
 
-def place_blocks(slots, rows, count):
+def place_blocks(where, rows, count):
     piece = rows.shape[0] // count
     width = rows.shape[1]
     return pl.pallas_call(
@@ -355,15 +387,147 @@
         grid_spec=pltpu.PrefetchScalarGridSpec(
             num_scalar_prefetch=1,
             grid=(count,),
-            in_specs=[pl.BlockSpec((piece, width), lambda index, slots: (index, 0))],
-            out_specs=pl.BlockSpec((piece, width), lambda index, slots: (slots[index], 0)),
+            in_specs=[pl.BlockSpec((piece, width), lambda index, where: (index, 0))],
+            out_specs=pl.BlockSpec((piece, width), lambda index, where: (where[index], 0)),
         ),
         out_shape=jax.ShapeDtypeStruct(rows.shape, rows.dtype),
         cost_estimate=pl.CostEstimate(
             flops=0, bytes_accessed=4 * rows.shape[0] * width, transcendentals=0
         ),
         name="place_blocks",
-    )(slots, rows)
+    )(where, rows)
+
+
+def ffn_grads_kernel(features, grads, gate_back, up_back, middle, target):
+    width = gate_back.shape[1]
+    stride = target.shape[1] // 3
+    pairs = ((features, gate_back), (features, up_back), (grads, middle))
+    for index, (left, right) in enumerate(pairs):
+        first = index * stride
+        target[:, first : first + width] = matmul_tn(left[...], right[...]).astype(low_type)
+        if stride > width:
+            target[:, first + width : first + stride] = jnp.zeros(
+                (target.shape[0], stride - width), low_type
+            )
+
+
+def ffn_grads(features, grads, gate_back, up_back, middle):
+    row_len, model_width = features.shape
+    width = gate_back.shape[1]
+    stride = -(-width // 128) * 128
+    block = model_width // 8
+    whole = lambda index: (0, 0)
+    column = lambda index: (0, index)
+    return pl.pallas_call(
+        ffn_grads_kernel,
+        grid=(8,),
+        in_specs=[
+            pl.BlockSpec((row_len, block), column),
+            pl.BlockSpec((row_len, block), column),
+            pl.BlockSpec((row_len, width), whole),
+            pl.BlockSpec((row_len, width), whole),
+            pl.BlockSpec((row_len, width), whole),
+        ],
+        out_specs=pl.BlockSpec((block, 3 * stride), lambda index: (index, 0)),
+        out_shape=jax.ShapeDtypeStruct((model_width, 3 * stride), low_type),
+        compiler_params=pltpu.CompilerParams(vmem_limit_bytes=vmem_bytes),
+        cost_estimate=pl.CostEstimate(
+            flops=6 * row_len * model_width * width,
+            bytes_accessed=4 * row_len * model_width + 6 * model_width * width,
+            transcendentals=0,
+        ),
+        name="ffn_grads",
+    )(features, grads, gate_back, up_back, middle)
+
+
+def polish(gram, gram_low, change_low, once_low, iterate, size):
+    block = min(size, 256)
+    count = size // block
+    for step_index in range(NS_STEPS):
+        last = step_index + 1 == NS_STEPS
+        if last:
+            first_term = matmul(iterate.astype(low_type), gram_low[...])
+            second_term = matmul(first_term.astype(low_type), gram_low[...])
+            return coef_first * iterate + coef_second * first_term + coef_third * second_term
+
+        def make_change(index, carry):
+            rows = block_at(index, block)
+            square = matmul(gram_low[rows, :], gram_low[...])
+            change_low[rows, :] = (coef_second * gram[rows, :] + coef_third * square).astype(
+                low_type
+            )
+            return carry
+
+        def make_once(index, carry):
+            rows = block_at(index, block)
+            once = matmul(gram_low[rows, :], change_low[...])
+            once_low[rows, :] = once.astype(low_type)
+            gram[rows, :] = (coef_first * coef_first) * gram[rows, :] + (2.0 * coef_first) * once
+            return carry
+
+        def make_gram(index, carry):
+            rows = block_at(index, block)
+            total = gram[rows, :] + matmul(once_low[rows, :], change_low[...])
+            gram[rows, :] = total
+            gram_low[rows, :] = total.astype(low_type)
+            return carry
+
+        lax.fori_loop(0, count, make_change, 0)
+        iterate = coef_first * iterate + matmul(iterate.astype(low_type), change_low[...])
+        lax.fori_loop(0, count, make_once, 0)
+        lax.fori_loop(0, count, make_gram, 0)
+
+
+def shared_kernel(*refs):
+    pieces = refs[: SIDE * CORES]
+    own, target, gram, gram_low, change_low, once_low = refs[SIDE * CORES :]
+    rows_each = pieces[0].shape[0] - own.shape[0]
+    wide = gram.shape[0]
+    narrow = (own.shape[1] - wide) // 2
+    for first, size in ((0, wide), (wide, narrow), (wide + narrow, narrow)):
+        cols = slice(first, first + size)
+        area = (slice(0, size), slice(0, size))
+        block = min(size, 256)
+        trace = jnp.zeros((1, 1), jnp.float32)
+        for index in range(size // block):
+            rows = slice(index * block, (index + 1) * block)
+            part = slice(first + index * block, first + (index + 1) * block)
+            total = jnp.zeros((block, size), jnp.float32)
+            for source in pieces:
+                total += matmul_tn(source[:rows_each, part], source[:rows_each, cols])
+            gram[rows, area[1]] = total
+            row_at = index * block + lax.broadcasted_iota(jnp.int32, (block, size), 0)
+            col_at = lax.broadcasted_iota(jnp.int32, (block, size), 1)
+            diagonal = jnp.where(row_at == col_at, total, 0.0)
+            trace += jnp.sum(jnp.sum(diagonal, axis=0, keepdims=True), axis=1, keepdims=True)
+        factor = 1.0 / (jnp.sqrt(trace) + 1e-07)
+        for index in range(size // block):
+            rows = slice(index * block, (index + 1) * block)
+            scaled = gram[rows, area[1]] * (factor * factor)
+            gram[rows, area[1]] = scaled
+            gram_low[rows, area[1]] = scaled.astype(low_type)
+        target[:, cols] = polish(
+            gram.at[area],
+            gram_low.at[area],
+            change_low.at[area],
+            once_low.at[area],
+            own[:, cols] * factor,
+            size,
+        )
+
+
+def shared_ortho(pieces, own, wide):
+    return pl.pallas_call(
+        shared_kernel,
+        out_shape=jax.ShapeDtypeStruct(own.shape, jnp.float32),
+        scratch_shapes=[pltpu.VMEM((wide, wide), jnp.float32)]
+        + [pltpu.VMEM((wide, wide), low_type)] * 3,
+        compiler_params=pltpu.CompilerParams(vmem_limit_bytes=vmem_bytes),
+        cost_estimate=pl.CostEstimate(
+            flops=20 * wide * wide * wide, bytes_accessed=8 * wide * wide, transcendentals=0
+        ),
+        name="shared_ortho",
+    )(*pieces, own)
 
 
 def gram_of(blocks):
@@ -452,9 +616,12 @@
     starts = seg_starts[0]
     whole_index = jnp.arange(row_len, dtype=jnp.int32)
     own_index = heads_rank * local_rows + jnp.arange(local_rows, dtype=jnp.int32)
+    own_core = heads_rank % CORES
+    own_step = heads_rank // CORES
     ranks = jnp.arange(heads_count, dtype=jnp.int32)
-    far_core = (ranks % CORES) ^ (heads_rank % CORES)
-    slots = SIDE * far_core + (ranks // CORES - heads_rank // CORES) % SIDE
+    where = SIDE * ((ranks % CORES) ^ own_core) + (ranks // CORES - own_step) % SIDE
+    owner = CORES * ((ranks % SIDE + own_step) % SIDE) + ((ranks // SIDE) ^ own_core)
+    where_core = jnp.concatenate([where, own_core[None].astype(jnp.int32)])
     gain_one = gains[:model_width]
     gain_latent = gains[model_width : model_width + latent_width]
     gain_two = gains[model_width + latent_width :]
@@ -468,34 +635,33 @@
     own_cos, own_sin = rotary_tables(own_pos, head_dim)
     key_local = rotate(matmul(normed_one, w_key), own_cos, own_sin).astype(low_type)
     value_local = matmul(normed_one, w_value).astype(low_type)
-    packed_rows = lax.all_gather(
-        jnp.concatenate([latent_normed, key_local, value_local], axis=1), "heads", axis=0, tiled=True
-    )
-    latent_rows = packed_rows[:, :latent_width]
-    key_rows = packed_rows[:, latent_width : latent_width + head_dim]
-    value_rows = packed_rows[:, latent_width + head_dim :]
+    row_ids, row_pos = segment_info(starts, whole_index)
+    row_cos, row_sin = rotary_tables(row_pos, head_dim)
+    grad_gathered = lax.all_gather(cotangent, "heads", axis=0, tiled=True)
+    pieces = gather_heads(jnp.concatenate([latent_normed, key_local, value_local], axis=1))
     share_rows = model_width // all_count
-    normed_parts = lax.all_to_all(
+    normed_columns = (
         normed_one.reshape(local_rows, dp_count, heads_count, share_rows)
         .transpose(2, 0, 1, 3)
-        .reshape(heads_count * local_rows, dp_count * share_rows),
-        "heads",
-        split_axis=0,
-        concat_axis=0,
-        tiled=True,
-    )
-    normed_parts = place_blocks(slots, normed_parts, heads_count)
-    grad_rows = place_blocks(
-        slots, lax.all_gather(cotangent, "heads", axis=0, tiled=True), heads_count
-    )
-    row_ids, row_pos = segment_info(starts, whole_index)
-    row_cos, row_sin = rotary_tables(row_pos, head_dim)
-    query_rows, attended, lse = attend(
-        slots, latent_rows, w_q_up, key_rows, value_rows, row_cos, row_sin, row_ids
-    )
+        .reshape(heads_count, local_rows, dp_count * share_rows)
+    )
+    normed_parts = [None] * heads_count
+    for core in range(CORES):
+        for step in range(SIDE):
+            part = lax.dynamic_index_in_dim(
+                normed_columns, owner[SIDE * core + step], 0, keepdims=False
+            )
+            if core or step:
+                part = shift_heads(part, step, core)
+            normed_parts[SIDE * core + (-step) % SIDE] = part
+    normed_parts = jnp.concatenate(normed_parts, axis=0)
+    pieces, normed_parts = lax.optimization_barrier((pieces, normed_parts))
+    packed, query_rows, attended_near, attended_far, lse = attend(
+        where_core, owner, pieces, w_q_up, head_dim, row_cos, row_sin, row_ids
+    )
+    grad_rows = place_blocks(where, grad_gathered, heads_count)
     attn_mixed = scatter_heads(
-        matmul_nt(attended[half_len:], w_out).astype(low_type),
-        matmul_nt(attended[:half_len], w_out),
+        matmul_nt(attended_far, w_out).astype(low_type), matmul_nt(attended_near, w_out)
     )
     hidden_one = inputs + attn_mixed
     scale_two = rms_scale(hidden_one)
@@ -517,10 +683,8 @@
         ),
         matmul_nt(gate_back[:half_len], w_gate) + matmul_nt(up_back[:half_len], w_up),
     )
-    gate_up_part = matmul_tn(ffn_input, jnp.concatenate([gate_back, up_back], axis=1))
-    down_w_part = matmul_tn(grad_rows, hidden_mid)
     ffn_sums = lax.psum_scatter(
-        jnp.concatenate([gate_up_part, down_w_part], axis=1).astype(low_type),
+        ffn_grads(ffn_input, grad_rows, gate_back, up_back, hidden_mid),
         "dp",
         scatter_dimension=0,
         tiled=True,
@@ -529,26 +693,25 @@
     hidden_back = cotangent.astype(jnp.float32) + hidden_part
     hidden_rows = jnp.concatenate(gather_heads(hidden_back.astype(low_type)), axis=0)
     attended_back = matmul(hidden_rows, w_out).astype(low_type)
-    late_mid, _ = lax.optimization_barrier((hidden_mid, attended_back))
-    ffn_mixed = scatter_heads(
-        matmul_nt(late_mid[half_len:], w_down).astype(low_type),
-        matmul_nt(late_mid[:half_len], w_down),
-    )
-    layer_out = (hidden_one + ffn_mixed).astype(low_type)
-    out_w_part = matmul_tn(hidden_rows, attended)
-    query_back, pair_back = attend_back(
-        slots, query_rows, key_rows, value_rows, attended_back, lse, row_cos, row_sin, row_ids
-    )
-    packed_sums = scatter_heads(
+    out_w_part = matmul_tn(
+        hidden_rows, jnp.concatenate([attended_near, attended_far], axis=0)
+    ).astype(low_type)
+    q_up_part, sums_near, sums_far = attend_back(
+        where_core, query_rows, packed, attended_back, lse, row_cos, row_sin, row_ids, w_q_up
+    )
+    packed_sums = scatter_heads(sums_far, sums_near)
+    head_sums = scatter_dp(
         jnp.concatenate(
-            [matmul_nt(query_back[half_len:], w_q_up).astype(low_type), pair_back[half_len:]],
+            [
+                q_up_part.reshape(dp_count, -1, local_q),
+                out_w_part.reshape(dp_count, -1, local_q),
+            ],
             axis=1,
-        ),
-        jnp.concatenate(
-            [matmul_nt(query_back[:half_len], w_q_up).astype(low_type), pair_back[:half_len]],
-            axis=1,
-        ),
-    )
+        )
+    )
+    q_up_rows = w_q_up.shape[0] // dp_count
+    q_up_grad = head_sums[:q_up_rows]
+    out_w_grad = head_sums[q_up_rows:]
     latent_back = packed_sums[:, :latent_width]
     key_sum = packed_sums[:, latent_width : latent_width + head_dim]
     value_sum = packed_sums[:, latent_width + head_dim :]
@@ -562,57 +725,13 @@
         gather_heads(jnp.concatenate([latent_raw_back, key_pre_back, values_low], axis=1)), axis=0
     )
     shared_part = matmul_tn(normed_parts, packed_back).astype(low_type)
-    shared_grad = scatter_dp(shared_part.reshape(dp_count, share_rows, shared_part.shape[1]))
-    q_down_grad = shared_grad[:, :latent_width]
-    key_w_grad = shared_grad[:, latent_width : latent_width + head_dim]
-    value_w_grad = shared_grad[:, latent_width + head_dim :]
-    latent_ordered = place_blocks(slots, latent_rows, heads_count)
-    q_up_part = matmul_tn(latent_ordered, query_back)
-    head_sums = scatter_dp(
-        jnp.concatenate(
-            [
-                q_up_part.astype(low_type).reshape(dp_count, -1, local_q),
-                out_w_part.astype(low_type).reshape(dp_count, -1, local_q),
-            ],
-            axis=1,
-        )
-    )
-    q_up_rows = w_q_up.shape[0] // dp_count
-    q_up_grad = head_sums[:q_up_rows]
-    out_w_grad = head_sums[q_up_rows:]
+    ffn_stride = ffn_sums.shape[1] // 3
     gate_w_grad = ffn_sums[:, :local_ff]
-    up_w_grad = ffn_sums[:, local_ff : 2 * local_ff]
-    down_w_grad = ffn_sums[:, 2 * local_ff :]
-    normed_one_back = (
-        matmul_nt(latent_raw_back, w_q_down)
-        + matmul_nt(key_pre_back, w_key)
-        + matmul_nt(values_low, w_value)
-    )
-    input_part, gain_one_grad = norm_back(inputs, scale_one, gain_one, normed_one_back)
-    input_grad = hidden_back + input_part
-    share_gains = gains.shape[0] // all_count
-    gains_part = jnp.concatenate([gain_one_grad, gain_latent_grad, gain_two_grad])
-    gains_part = gains_part.reshape(dp_count, heads_count, share_gains).transpose(1, 0, 2)
-    gains_part = gains_part.reshape(SIDE, CORES, dp_count * share_gains)
-    own_core = heads_rank % CORES
-    own_step = heads_rank // CORES
-
-    def by_step(array, core):
-        side = lax.dynamic_index_in_dim(array, core, 1, keepdims=False)
-        return lax.dynamic_slice_in_dim(jnp.concatenate([side, side], axis=0), own_step, SIDE, 0)
-
-    gains_sum = scatter_heads(by_step(gains_part, 1 - own_core), by_step(gains_part, own_core))
-    gains_grad = scatter_dp(gains_sum.reshape(dp_count, 1, share_gains))[0]
-    gains_mom = decay_rate * mom_gains + gains_grad
-    q_down_mom = decay_rate * mom_q_down + q_down_grad
-    key_w_mom = decay_rate * mom_key + key_w_grad
-    value_w_mom = decay_rate * mom_value + value_w_grad
-    q_up_mom = decay_rate * mom_q_up + q_up_grad
-    out_w_mom = decay_rate * mom_out + out_w_grad
+    up_w_grad = ffn_sums[:, ffn_stride : ffn_stride + local_ff]
+    down_w_grad = ffn_sums[:, 2 * ffn_stride : 2 * ffn_stride + local_ff]
     gate_w_mom = decay_rate * mom_gate + gate_w_grad
     up_w_mom = decay_rate * mom_up + up_w_grad
     down_w_mom = decay_rate * mom_down + down_w_grad
-    gains_new = own_rows(gains, all_count, all_rank) - gain_rate * gains_mom
     ffn_count = w_gate.shape[1] // FF_BLOCK
     ffn_blocks = jnp.concatenate(
         [
@@ -622,7 +741,60 @@
         ],
         axis=0,
     )
-    ffn_gram = lax.psum(gram_of(ffn_blocks).astype(low_type), "dp").astype(jnp.float32)
+    ffn_gram = gram_of(ffn_blocks).astype(low_type)
+    normed_one_back = (
+        matmul_nt(latent_raw_back, w_q_down)
+        + matmul_nt(key_pre_back, w_key)
+        + matmul_nt(values_low, w_value)
+    )
+    input_part, gain_one_grad = norm_back(inputs, scale_one, gain_one, normed_one_back)
+    input_grad = hidden_back + input_part
+    share_gains = gains.shape[0] // all_count
+    gains_part = jnp.concatenate([gain_one_grad, gain_latent_grad, gain_two_grad])
+    gains_part = gains_part.reshape(dp_count, heads_count, share_gains).astype(low_type)
+    gains_part = jnp.pad(
+        gains_part, ((0, 0), (0, share_rows - heads_count), (0, 128 - share_gains))
+    )
+    mixed_far = matmul_nt(hidden_mid[half_len:], w_down).astype(low_type)
+    mixed_near = matmul_nt(hidden_mid[:half_len], w_down).astype(low_type)
+    shared_part, ffn_gram, mixed_far, mixed_near = lax.optimization_barrier(
+        (shared_part, ffn_gram, mixed_far, mixed_near)
+    )
+    ffn_gram = lax.psum(ffn_gram, "dp").astype(jnp.float32)
+    packed_width = shared_part.shape[1]
+    shared_grad = scatter_dp(
+        jnp.concatenate(
+            [shared_part.reshape(dp_count, share_rows, packed_width), gains_part], axis=2
+        )
+    )
+    layer_out = (hidden_one + scatter_heads(mixed_far, mixed_near)).astype(low_type)
+    q_down_grad = shared_grad[:, :latent_width]
+    key_w_grad = shared_grad[:, latent_width : latent_width + head_dim]
+    value_w_grad = shared_grad[:, latent_width + head_dim : packed_width]
+    q_down_mom = decay_rate * mom_q_down + q_down_grad
+    key_w_mom = decay_rate * mom_key + key_w_grad
+    value_w_mom = decay_rate * mom_value + value_w_grad
+    shared_mom = jnp.concatenate([q_down_mom, key_w_mom, value_w_mom], axis=1)
+    gains_rows = jnp.pad(
+        shared_grad[:, packed_width : packed_width + share_gains],
+        ((0, 0), (0, packed_width - share_gains)),
+    )
+    mom_pieces = gather_heads(
+        jnp.concatenate(
+            [gather_dp(shared_mom.astype(low_type)), gains_rows.astype(low_type)], axis=0
+        )
+    )
+    gains_grad = sum(
+        lax.dynamic_index_in_dim(
+            piece[dp_count * share_rows :, :share_gains], heads_rank, 0, keepdims=False
+        ).astype(jnp.float32)
+        for piece in mom_pieces
+    )
+    shared_done = shared_ortho(mom_pieces, shared_mom, latent_width)
+    gains_mom = decay_rate * mom_gains + gains_grad
+    q_up_mom = decay_rate * mom_q_up + q_up_grad
+    out_w_mom = decay_rate * mom_out + out_w_grad
+    gains_new = own_rows(gains, all_count, all_rank) - gain_rate * gains_mom
     ffn_ortho = orthogonal(ffn_blocks, ffn_gram)
     query_blocks = split_columns(q_up_mom, head_dim)
     output_blocks = split_columns(out_w_mom, head_dim)
@@ -652,19 +824,6 @@
     head_grams = head_grams.astype(jnp.float32)
     query_ortho = orthogonal(query_blocks, head_grams[:head_count])
     output_ortho = orthogonal(output_blocks, head_grams[head_count:])
-    mom_rows = jnp.concatenate([q_down_mom, key_w_mom, value_w_mom], axis=1).astype(low_type)
-    mom_rows = gather_dp(mom_rows)
-    mom_rows = jnp.concatenate(gather_heads(mom_rows), axis=0)
-    pair_rows = jnp.stack(
-        [
-            mom_rows[:, latent_width : latent_width + head_dim],
-            mom_rows[:, latent_width + head_dim :],
-        ]
-    )
-    shared_iter = (
-        orthogonal(q_down_mom[None], gram_of(mom_rows[None, :, :latent_width])),
-        orthogonal(jnp.stack([key_w_mom, value_w_mom]), gram_of(pair_rows)),
-    )
     q_up_new = own_rows(w_q_up, dp_count, dp_rank) - muon_rate * math.sqrt(
         w_q_up.shape[0] / head_dim
     ) * join_columns(query_ortho)
@@ -683,11 +842,11 @@
     )
     q_down_new = (
         own_rows(w_q_down, all_count, all_rank)
-        - muon_rate * math.sqrt(w_q_down.shape[0] / latent_width) * shared_iter[0][0]
+        - muon_rate * math.sqrt(w_q_down.shape[0] / latent_width) * shared_done[:, :latent_width]
     )
     pair_factor = muon_rate * math.sqrt(w_key.shape[0] / head_dim)
-    key_w_new = own_rows(w_key, all_count, all_rank) - pair_factor * shared_iter[1][0]
-    value_w_new = own_rows(w_value, all_count, all_rank) - pair_factor * shared_iter[1][1]
+    key_w_new = own_rows(w_key, all_count, all_rank) - pair_factor * shared_done[:, latent_width : latent_width + head_dim]
+    value_w_new = own_rows(w_value, all_count, all_rank) - pair_factor * shared_done[:, latent_width + head_dim :]
     return (
         layer_out,
         input_grad,

time: 768 us -> 731 us (0.952)
  matrix products: 135 us -> 87.1 us
  Pallas kernels: 33.3 us -> 69.7 us
  waiting for transfers between devices: 288 us -> 262 us
  starting transfers between devices: 139 us -> 120 us
  between operations: 32.9 us -> 47.4 us
    ppermute x48 -> x58, waiting for transfers between devices: 102 us -> 159 us  [shift_heads(): return lax.ppermute(values, 'heads', pairs)]
    psum x1, waiting for transfers between devices: 81.8 us -> 30.2 us  [on_device(): ffn_gram = lax.psum(ffn_gram, 'dp').astype(jnp.float32)]
    pallas_call x0 -> x2, Pallas kernels: none -> 42.4 us  [the longest x1 29.6 us: shared_ortho(): pl.pallas_call(shared_kernel, out_shape=jax.ShapeDtypeStruct(own.shape, j...]
    all_gather x2 -> x1, waiting for transfers between devices: 42.2 us -> 0.01 us  [on_device(): grad_gathered = lax.all_gather(cotangent, 'heads', axis=0, tiled=True)]
    dot_general x60 -> x36, matrix products: 49.9 us -> 20.8 us  [times(): jnp.einsum('brc,bcd->brd', left.astype(low_type), right.astype(low_type),...]
    dot_general x5 -> x3, matrix products: 15.1 us -> 2.31 us  [gram_of(): jnp.einsum('brc,brd->bcd', low, low, preferred_element_type=jnp.float32)]
    dot_general x5 -> x2, matrix products: 17.8 us -> 5.48 us  [matmul_tn(): lax.dot_general(left, right, (((0,), (0,)), ((), ())), preferred_element_...]
    pallas_call x3 -> x1, Pallas kernels: 19 us -> 7.31 us  [place_blocks(): pl.pallas_call(place_kernel, grid_spec=pltpu.PrefetchScalarGridSpec(num_s...]
  transfers between devices with their start and end apart: 89 -> 91, of which waited for: 39 -> 42; matrix products, arithmetic and copies ran while one was open for 25% -> 20% of each run, Pallas kernels for 3% -> 6%
where the time goes in v3:
time: 731 us; the launch traced here: 721 us
  waiting for transfers between devices  262 us (36%)
  starting transfers between devices  120 us (16%)
  matrix products  87.1 us (12%)
  local copies, waits for them, and re-layouts  77.2 us (11%)
  Pallas kernels  69.7 us (10%)
  other arithmetic  57.9 us (8%)
  between operations  47.4 us (6%)
    ppermute x58, waiting for transfers between devices, shift_heads(): return lax.ppermute(values, 'heads', pairs)  159 us
    ppermute x58, starting transfers between devices, shift_heads(): return lax.ppermute(values, 'heads', pairs)  83.3 us
    ppermute x30, waiting for transfers between devices, shift_dp(): return lax.ppermute(values, 'dp', pairs)  71.8 us
    unnamed x239, local copies, waits for them, and re-layouts  43.8 us
    ppermute x30, starting transfers between devices, shift_dp(): return lax.ppermute(values, 'dp', pairs)  36.4 us
    dot_general x7, matrix products, matmul(): return jnp.dot(left, right, preferred_element_type=jnp.float32)  32.3 us
    psum x1, waiting for transfers between devices, on_device(): ffn_gram = lax.psum(ffn_gram, 'dp').astype(jnp.float32)  30.2 us
    pallas_call x1, Pallas kernels, shared_ortho(): pl.pallas_call(shared_kernel, out_shape=jax.ShapeDtypeStruct(own.shape, j...  29.6 us
  transfers between devices with their start and end apart: 91, of which 42 were waited for; matrix products, arithmetic and copies ran while one was open for 20% of the time, Pallas kernels for 6%

profile of v3, /device:TPU:1, one launch (start us, length us, event | category | flops | bytes accessed | tf_op | source)
XLA Modules:
  0.0 721.0 jit_solution(3840434626621813137)
XLA Ops:
  81.3 8.9 %attend.1 = (bf16[1024,1536]{1,0:T(8,128)(2,1)S(1)}, bf16[1024,512]{1,0:T(8,128)(2,1)S(1)}, bf16[512,512]{1,0:T(8,128)(2,1)S(1)}, bf16[512,512]{1,0:T(8,128)(2,1)S(1)}, f32[2,1024,1]{2,1,0:T(8,128)S(1)}) custom-call(s32[9]{0:T(128)S(1)} %pad_add_fusion.where, s32[8]{0:T(128)S(1)} %fusion.171.owner, bf16[128,1536]{1,0:T(8,128)(2,1)S(1)} %pad_maximum_fusion.5.refs_0_, ...), custom_call_target="tpu_custom_call" | custom-call | flops 3221225472 | bytes 4194304 | tf_op jit(solution)/shard_map/attend/pallas_call | solution.py:206
  102.7 19.8 %collective-permute-done.17 = bf16[128,2048]{1,0:T(8,128)(2,1)S(1)} collective-permute-done((bf16[128,2048]{1,0:T(8,128)(2,1)S(1)}, bf16[128,2048]{1,0:T(8,128)(2,1)S(1)}, u32[]{:S(2)}, u32[]{:S(2)}) %collective-permute-start.17) | collective-permute-done | bytes 524320 | tf_op jit(solution)/shard_map/ppermute | solution.py:92
  124.5 14.7 %collective-permute-done.15 = bf16[128,2048]{1,0:T(8,128)(2,1)S(1)} collective-permute-done((bf16[128,2048]{1,0:T(8,128)(2,1)S(1)}, bf16[128,2048]{1,0:T(8,128)(2,1)S(1)}, u32[]{:S(2)}, u32[]{:S(2)}) %collective-permute-start.15) | collective-permute-done | bytes 524320 | tf_op jit(solution)/shard_map/ppermute | solution.py:92
  148.2 18.7 %collective-permute-done.18 = bf16[128,2048]{1,0:T(8,128)(2,1)S(1)} collective-permute-done((bf16[128,2048]{1,0:T(8,128)(2,1)S(1)}, bf16[128,2048]{1,0:T(8,128)(2,1)S(1)}, u32[]{:S(2)}, u32[]{:S(2)}) %collective-permute-start.18) | collective-permute-done | bytes 524320 | tf_op jit(solution)/shard_map/ppermute | solution.py:92
  184.7 8.2 %fusion.241 = f32[1024,704]{1,0:T(8,128)} fusion(bf16[1024,2048]{1,0:T(8,128)(2,1)} %copy-done.20, bf16[2048,704]{0,1:T(8,128)(2,1)} %param.30), kind=kOutput, calls=%fused_computation.498 | convolution fusion | flops 2952790016 | bytes 9961472 | tf_op jit(solution)/shard_map/dot_general | solution.py:26
  192.9 7.3 %place_blocks.1.grads = bf16[1024,2048]{1,0:T(8,128)(2,1)} custom-call(s32[8]{0:T(128)} %copy-done.91, bf16[1024,2048]{1,0:T(8,128)(2,1)} %all-gather.2.cloned.1.call-done.source), custom_call_target="tpu_custom_call" | custom-call | bytes 8388608 | tf_op jit(solution)/shard_map/place_blocks/pallas_call | solution.py:385
  200.2 9.7 %fusion.233 = (f32[1024,704]{0,1:T(8,128)}, f32[1024,704]{0,1:T(8,128)}) fusion(f32[1024,704]{0,1:T(8,128)} %fusion.240, bf16[1024,2048]{1,0:T(8,128)(2,1)} %place_blocks.1.grads, bf16[2048,704]{0,1:T(8,128)(2,1)} %param.32), kind=kOutput, calls=%fused_computation.490 | convolution fusion | flops 2953510912 | bytes 15728640 | tf_op jit(solution)/shard_map/dot_general | solution.py:26
  217.0 6.6 multiply_convert_fusion
  237.3 11.0 %collective-permute-done.28 = bf16[128,2048]{1,0:T(8,128)(2,1)S(1)} collective-permute-done((bf16[128,2048]{1,0:T(8,128)(2,1)S(1)}, bf16[128,2048]{1,0:T(8,128)(2,1)S(1)}, u32[]{:S(2)}, u32[]{:S(2)}) %collective-permute-start.28) | collective-permute-done | bytes 524320 | tf_op jit(solution)/shard_map/ppermute | solution.py:92
  251.1 11.6 %collective-permute-done.26 = bf16[128,2048]{1,0:T(8,128)(2,1)S(1)} collective-permute-done((bf16[128,2048]{1,0:T(8,128)(2,1)S(1)}, bf16[128,2048]{1,0:T(8,128)(2,1)S(1)}, u32[]{:S(2)}, u32[]{:S(2)}) %collective-permute-start.26) | collective-permute-done | bytes 524320 | tf_op jit(solution)/shard_map/ppermute | solution.py:92
  267.8 10.1 %collective-permute-done.29 = bf16[128,2048]{1,0:T(8,128)(2,1)} collective-permute-done((bf16[128,2048]{1,0:T(8,128)(2,1)}, bf16[128,2048]{1,0:T(8,128)(2,1)}, u32[]{:S(2)}, u32[]{:S(2)}) %collective-permute-start.29) | collective-permute-done | bytes 524320 | tf_op jit(solution)/shard_map/ppermute | solution.py:92
  284.2 7.6 %collective-permute-done.31 = bf16[128,2048]{1,0:T(8,128)(2,1)S(1)} collective-permute-done((bf16[128,2048]{1,0:T(8,128)(2,1)}, bf16[128,2048]{1,0:T(8,128)(2,1)S(1)}, u32[]{:S(2)}, u32[]{:S(2)}) %collective-permute-start.31) | collective-permute-done | bytes 524320 | tf_op jit(solution)/shard_map/ppermute | solution.py:92
  304.6 11.1 %attend_back.1 = (bf16[1024,512]{1,0:T(8,128)(2,1)S(1)}, bf16[512,1536]{1,0:T(8,128)(2,1)S(1)}, bf16[512,1536]{1,0:T(8,128)(2,1)}) custom-call(s32[9]{0:T(128)S(1)} %pad_add_fusion.where, bf16[1024,512]{1,0:T(8,128)(2,1)S(1)} %copy-done.33, bf16[1024,1536]{1,0:T(8,128)(2,1)S(1)} %copy-done.29, bf16[1024,512]{1,0:T(8,128)(2,1)S(1)} %convolution_convert_fusion.6.mixed_back, ...), custom_call_target="tpu_custom_call" | custom-call | flops 5368709120 | bytes 4194304 | tf_op jit(solution)/shard_map/attend_back/pallas_call | solution.py:326
  320.9 12.8 %ffn_grads.1 = bf16[2048,2304]{1,0:T(8,128)(2,1)S(1)} custom-call(bf16[1024,2048]{1,0:T(8,128)(2,1)S(1)} %copy-done.21, bf16[1024,2048]{1,0:T(8,128)(2,1)S(1)} %copy-done.5, bf16[1024,704]{1,0:T(8,128)(2,1)S(1)} %copy-done.9, bf16[1024,704]{1,0:T(8,128)(2,1)S(1)} %copy-done.4, bf16[1024,704]{1,0:T(8,128)(2,1)S(1)} %copy-done.6), custom_call_target="tpu_custom_call" | custom-call | flops 8858370048 | bytes 17039360 | tf_op jit(solution)/shard_map/ffn_grads/pallas_call | solution.py:421
  340.8 10.3 %collective-permute-done.72 = bf16[4,192,512]{2,1,0:T(8,128)(2,1)} collective-permute-done((bf16[4,192,512]{2,1,0:T(8,128)(2,1)}, bf16[4,192,512]{2,1,0:T(8,128)(2,1)}, u32[]{:S(2)}, u32[]{:S(2)}) %collective-permute-start.72) | collective-permute-done | bytes 786464 | tf_op jit(solution)/shard_map/ppermute | solution.py:101
  351.1 12.4 %collective-permute-done.70 = bf16[4,192,512]{2,1,0:T(8,128)(2,1)} collective-permute-done((bf16[4,192,512]{2,1,0:T(8,128)(2,1)}, bf16[4,192,512]{2,1,0:T(8,128)(2,1)}, u32[]{:S(2)}, u32[]{:S(2)}) %collective-permute-start.70) | collective-permute-done | bytes 786464 | tf_op jit(solution)/shard_map/ppermute | solution.py:101
  374.7 8.0 %collective-permute-done.75 = bf16[192,512]{0,1:T(8,128)(2,1)S(1)} collective-permute-done((bf16[192,512]{0,1:T(8,128)(2,1)}, bf16[192,512]{0,1:T(8,128)(2,1)S(1)}, u32[]{:S(2)}, u32[]{:S(2)}) %collective-permute-start.75) | collective-permute-done | bytes 196640 | tf_op jit(solution)/shard_map/ppermute | solution.py:101
  386.1 7.4 %collective-permute-done.73 = bf16[192,512]{0,1:T(8,128)(2,1)S(1)} collective-permute-done((bf16[192,512]{0,1:T(8,128)(2,1)}, bf16[192,512]{0,1:T(8,128)(2,1)S(1)}, u32[]{:S(2)}, u32[]{:S(2)}) %collective-permute-start.73) | collective-permute-done | bytes 196640 | tf_op jit(solution)/shard_map/ppermute | solution.py:101
  480.6 9.2 %collective-permute-done.37 = bf16[128,1536]{1,0:T(8,128)(2,1)} collective-permute-done((bf16[128,1536]{1,0:T(8,128)(2,1)S(1)}, bf16[128,1536]{1,0:T(8,128)(2,1)}, u32[]{:S(2)}, u32[]{:S(2)}) %collective-permute-start.37) | collective-permute-done | bytes 393248 | tf_op jit(solution)/shard_map/ppermute | solution.py:92
  579.0 6.6 collective-permute-start.66
  593.2 6.9 collective-permute-done.65.refs_3_
  600.1 16.3 %collective-permute-start.69 = (bf16[272,1536]{1,0:T(8,128)(2,1)S(1)}, bf16[272,1536]{1,0:T(8,128)(2,1)}, u32[]{:S(2)}, u32[]{:S(2)}) collective-permute-start(bf16[272,1536]{1,0:T(8,128)(2,1)S(1)} %collective-permute-done.65.refs_3_), channel_id=1, source_target_pairs={{0,1},{1,0},{2,3},{3,2},{4,5},{5,4},{6,7},{7,6},{8,9},{9,8},{10,11... | collective-permute-start | bytes 2506760 | tf_op jit(solution)/shard_map/ppermute | solution.py:92
  618.7 30.2 %all-reduce.4.cloned.1.call-done = bf16[6,352,352]{2,1,0:T(8,128)(2,1)} async-done(((bf16[6,352,352]{2,1,0:T(8,128)(2,1)}), bf16[6,352,352]{2,1,0:T(8,128)(2,1)}) %all-reduce.4.cloned.1.call-update) | async-done | bytes 1486864 | tf_op jit(solution)/shard_map/psum | solution.py:763
  679.3 29.6 %shared_ortho.1 = f32[16,1536]{1,0:T(8,128)S(1)} custom-call(bf16[272,1536]{1,0:T(8,128)(2,1)S(1)} %constant_dynamic-update-slice_fusion.32.refs_0_, bf16[272,1536]{1,0:T(8,128)(2,1)} %collective-permute-done.63.refs_1_, bf16[272,1536]{1,0:T(8,128)(2,1)S(1)} %copy-done.27, bf16[272,1536]{1,0:T(8,128)(2,1)S(1)} %copy-done.25, ...), custom_call_target="tpu_custom_call" | custom-call | flops 21474836480 | bytes 8388608 | tf_op jit(solution)/shard_map/shared_ortho/pallas_call | solution.py:520
  (596 shorter events, 378.4 us)
Async XLA Ops:
  7.2 185.6 %all-gather.2.cloned.1.call-start = ((), (), s32[]{:S(2)}) async-start(), calls=%async_computation.1 | async-start | bytes 4718592 | tf_op jit(solution)/shard_map/all_gather | solution.py:640
  18.7 44.0 %collective-permute-start = (bf16[128,1536]{1,0:T(8,128)(2,1)S(1)}, bf16[128,1536]{1,0:T(8,128)(2,1)}, u32[]{:S(2)}, u32[]{:S(2)}) collective-permute-start(bf16[128,1536]{1,0:T(8,128)(2,1)S(1)} %pad_maximum_fusion.5.refs_0_), channel_id=1, source_target_pairs={{0,6},{1,7},{2,0},{3,1},{4,2},{5,3},{6,4},{7,5},{8,14},{9,15},{10,... | collective-permute-start | bytes 1179656 | tf_op jit(solution)/shard_map/ppermute | solution.py:92
  22.3 40.7 %collective-permute-start.1 = (bf16[128,1536]{1,0:T(8,128)(2,1)S(1)}, bf16[128,1536]{1,0:T(8,128)(2,1)}, u32[]{:S(2)}, u32[]{:S(2)}) collective-permute-start(bf16[128,1536]{1,0:T(8,128)(2,1)S(1)} %pad_maximum_fusion.5.refs_0_), channel_id=1, source_target_pairs={{0,4},{1,5},{2,6},{3,7},{4,0},{5,1},{6,2},{7,3},{8,12},{9,13},{10,... | collective-permute-start | bytes 1179656 | tf_op jit(solution)/shard_map/ppermute | solution.py:92
  22.7 40.5 %collective-permute-start.2 = (bf16[128,1536]{1,0:T(8,128)(2,1)S(1)}, bf16[128,1536]{1,0:T(8,128)(2,1)}, u32[]{:S(2)}, u32[]{:S(2)}) collective-permute-start(bf16[128,1536]{1,0:T(8,128)(2,1)S(1)} %pad_maximum_fusion.5.refs_0_), channel_id=1, source_target_pairs={{0,2},{1,3},{2,4},{3,5},{4,6},{5,7},{6,0},{7,1},{8,10},{9,11},{10,... | collective-permute-start | bytes 1179656 | tf_op jit(solution)/shard_map/ppermute | solution.py:92
  23.4 55.6 %collective-permute-start.3 = (bf16[128,1536]{1,0:T(8,128)(2,1)S(1)}, bf16[128,1536]{1,0:T(8,128)(2,1)}, u32[]{:S(2)}, u32[]{:S(2)}) collective-permute-start(bf16[128,1536]{1,0:T(8,128)(2,1)S(1)} %pad_maximum_fusion.5.refs_0_), channel_id=1, source_target_pairs={{0,1},{1,0},{2,3},{3,2},{4,5},{5,4},{6,7},{7,6},{8,9},{9,8},{10,11... | collective-permute-start | bytes 1179656 | tf_op jit(solution)/shard_map/ppermute | solution.py:92
  93.9 429.7 %reduce-scatter.2.cloned.1.call-start = ((), (), s32[]{:S(2)}) async-start(), calls=%async_computation.2 | async-start | bytes 10027008 | tf_op jit(solution)/shard_map/reduce_scatter | solution.py:686
  101.9 37.3 %collective-permute-start.15 = (bf16[128,2048]{1,0:T(8,128)(2,1)S(1)}, bf16[128,2048]{1,0:T(8,128)(2,1)S(1)}, u32[]{:S(2)}, u32[]{:S(2)}) collective-permute-start(bf16[128,2048]{1,0:T(8,128)(2,1)S(1)} %get-tuple-element.250), channel_id=1, source_target_pairs={{0,2},{1,3},{2,4},{3,5},{4,6},{5,7},{6,0},{7,1},{8,10},{9,11},{10,... | collective-permute-start | bytes 1572872 | tf_op jit(solution)/shard_map/ppermute | solution.py:92
  139.9 27.1 %collective-permute-start.18 = (bf16[128,2048]{1,0:T(8,128)(2,1)S(1)}, bf16[128,2048]{1,0:T(8,128)(2,1)S(1)}, u32[]{:S(2)}, u32[]{:S(2)}) collective-permute-start(bf16[128,2048]{1,0:T(8,128)(2,1)S(1)} %get-tuple-element.229), channel_id=1, source_target_pairs={{0,6},{1,7},{2,0},{3,1},{4,2},{5,3},{6,4},{7,5},{8,14},{9,15},{10,... | collective-permute-start | bytes 1572872 | tf_op jit(solution)/shard_map/ppermute | solution.py:92
  266.5 26.8 %collective-permute-start.32 = (bf16[128,2048]{1,0:T(8,128)(2,1)}, bf16[128,2048]{1,0:T(8,128)(2,1)S(1)}, u32[]{:S(2)}, u32[]{:S(2)}) collective-permute-start(bf16[128,2048]{1,0:T(8,128)(2,1)} %get-tuple-element.225), channel_id=1, source_target_pairs={{0,1},{1,0},{2,3},{3,2},{4,5},{5,4},{6,7},{7,6},{8,9},{9,8},{10,11... | collective-permute-start | bytes 1572872 | tf_op jit(solution)/shard_map/ppermute | solution.py:92
  317.3 33.8 %collective-permute-start.72 = (bf16[4,192,512]{2,1,0:T(8,128)(2,1)}, bf16[4,192,512]{2,1,0:T(8,128)(2,1)}, u32[]{:S(2)}, u32[]{:S(2)}) collective-permute-start(bf16[4,192,512]{2,1,0:T(8,128)(2,1)} %get-tuple-element.238), channel_id=1, source_target_pairs={{0,24},{8,0},{16,8},{24,16},{32,56},{40,32},{48,40},{56,48},{64,88... | collective-permute-start | bytes 2359304 | tf_op jit(solution)/shard_map/ppermute | solution.py:101
  319.7 31.4 %collective-permute-start.71 = (bf16[4,192,512]{2,1,0:T(8,128)(2,1)}, bf16[4,192,512]{2,1,0:T(8,128)(2,1)}, u32[]{:S(2)}, u32[]{:S(2)}) collective-permute-start(bf16[4,192,512]{2,1,0:T(8,128)(2,1)} %get-tuple-element.237), channel_id=1, source_target_pairs={{0,16},{8,24},{16,0},{24,8},{32,48},{40,56},{48,32},{56,40},{64,80... | collective-permute-start | bytes 2359304 | tf_op jit(solution)/shard_map/ppermute | solution.py:101
  320.3 43.2 %collective-permute-start.70 = (bf16[4,192,512]{2,1,0:T(8,128)(2,1)}, bf16[4,192,512]{2,1,0:T(8,128)(2,1)}, u32[]{:S(2)}, u32[]{:S(2)}) collective-permute-start(bf16[4,192,512]{2,1,0:T(8,128)(2,1)} %get-tuple-element.236), channel_id=1, source_target_pairs={{0,8},{8,16},{16,24},{24,0},{32,40},{40,48},{48,56},{56,32},{64,72... | collective-permute-start | bytes 2359304 | tf_op jit(solution)/shard_map/ppermute | solution.py:101
  337.3 311.7 %all-reduce.4.cloned.1.call-start = ((), (), s32[]{:S(2)}) async-start(), calls=%async_computation.3 | async-start | bytes 3244032 | tf_op jit(solution)/shard_map/psum | solution.py:763
  395.4 26.2 %collective-permute-start.78 = (bf16[4,64,256]{2,1,0:T(8,128)(2,1)}, bf16[4,64,256]{2,1,0:T(8,128)(2,1)S(1)}, u32[]{:S(2)}, u32[]{:S(2)}) collective-permute-start(bf16[4,64,256]{2,1,0:T(8,128)(2,1)} %get-tuple-element.288), channel_id=1, source_target_pairs={{0,24},{8,0},{16,8},{24,16},{32,56},{40,32},{48,40},{56,48},{64,88... | collective-permute-start | bytes 393224 | tf_op jit(solution)/shard_map/ppermute | solution.py:101
  576.3 40.1 %collective-permute-start.64 = (bf16[272,1536]{1,0:T(8,128)(2,1)S(1)}, bf16[272,1536]{1,0:T(8,128)(2,1)S(1)}, u32[]{:S(2)}, u32[]{:S(2)}) collective-permute-start(bf16[272,1536]{1,0:T(8,128)(2,1)S(1)} %constant_dynamic-update-slice_fusion.32.refs_0_), channel_id=1, source_target_pairs={{0,4},{1,5},{2,6},{3,7},{4,0},{5,1},{6,2},{7,3},{8,12},{9,13},{10,... | collective-permute-start | bytes 2506760 | tf_op jit(solution)/shard_map/ppermute | solution.py:92
  576.4 40.1 %collective-permute-start.63 = (bf16[272,1536]{1,0:T(8,128)(2,1)S(1)}, bf16[272,1536]{1,0:T(8,128)(2,1)}, u32[]{:S(2)}, u32[]{:S(2)}) collective-permute-start(bf16[272,1536]{1,0:T(8,128)(2,1)S(1)} %constant_dynamic-update-slice_fusion.32.refs_0_), channel_id=1, source_target_pairs={{0,6},{1,7},{2,0},{3,1},{4,2},{5,3},{6,4},{7,5},{8,14},{9,15},{10,... | collective-permute-start | bytes 2506760 | tf_op jit(solution)/shard_map/ppermute | solution.py:92
  579.0 39.0 %collective-permute-start.66 = (bf16[272,1536]{1,0:T(8,128)(2,1)S(1)}, bf16[272,1536]{1,0:T(8,128)(2,1)}, u32[]{:S(2)}, u32[]{:S(2)}) collective-permute-start(bf16[272,1536]{1,0:T(8,128)(2,1)S(1)} %constant_dynamic-update-slice_fusion.32.refs_0_), channel_id=1, source_target_pairs={{0,1},{1,0},{2,3},{3,2},{4,5},{5,4},{6,7},{7,6},{8,9},{9,8},{10,11... | collective-permute-start | bytes 2506760 | tf_op jit(solution)/shard_map/ppermute | solution.py:92
  588.6 82.3 %collective-permute-start.47 = (bf16[512,2048]{1,0:T(8,128)(2,1)}, bf16[512,2048]{1,0:T(8,128)(2,1)}, u32[]{:S(2)}, u32[]{:S(2)}) collective-permute-start(bf16[512,2048]{1,0:T(8,128)(2,1)} %convolution_convert_fusion.2), channel_id=1, source_target_pairs={{0,1},{1,0},{2,3},{3,2},{4,5},{5,4},{6,7},{7,6},{8,9},{9,8},{10,11... | collective-permute-start | bytes 6291464 | tf_op jit(solution)/shard_map/ppermute | solution.py:92
  600.1 76.5 %collective-permute-start.69 = (bf16[272,1536]{1,0:T(8,128)(2,1)S(1)}, bf16[272,1536]{1,0:T(8,128)(2,1)}, u32[]{:S(2)}, u32[]{:S(2)}) collective-permute-start(bf16[272,1536]{1,0:T(8,128)(2,1)S(1)} %collective-permute-done.65.refs_3_), channel_id=1, source_target_pairs={{0,1},{1,0},{2,3},{3,2},{4,5},{5,4},{6,7},{7,6},{8,9},{9,8},{10,11... | collective-permute-start | bytes 2506760 | tf_op jit(solution)/shard_map/ppermute | solution.py:92
  616.5 61.4 %collective-permute-start.68 = (bf16[272,1536]{1,0:T(8,128)(2,1)S(1)}, bf16[272,1536]{1,0:T(8,128)(2,1)}, u32[]{:S(2)}, u32[]{:S(2)}) collective-permute-start(bf16[272,1536]{1,0:T(8,128)(2,1)S(1)} %collective-permute-done.64.refs_2_), channel_id=1, source_target_pairs={{0,1},{1,0},{2,3},{3,2},{4,5},{5,4},{6,7},{7,6},{8,9},{9,8},{10,11... | collective-permute-start | bytes 2506760 | tf_op jit(solution)/shard_map/ppermute | solution.py:92
  616.6 62.0 %collective-permute-start.67 = (bf16[272,1536]{1,0:T(8,128)(2,1)}, bf16[272,1536]{1,0:T(8,128)(2,1)}, u32[]{:S(2)}, u32[]{:S(2)}) collective-permute-start(bf16[272,1536]{1,0:T(8,128)(2,1)} %collective-permute-done.63.refs_1_), channel_id=1, source_target_pairs={{0,1},{1,0},{2,3},{3,2},{4,5},{5,4},{6,7},{7,6},{8,9},{9,8},{10,11... | collective-permute-start | bytes 2506760 | tf_op jit(solution)/shard_map/ppermute | solution.py:92
  673.5 39.4 %collective-permute-start.50 = (bf16[128,2048]{1,0:T(8,128)(2,1)S(1)}, bf16[128,2048]{1,0:T(8,128)(2,1)S(1)}, u32[]{:S(2)}, u32[]{:S(2)}) collective-permute-start(bf16[128,2048]{1,0:T(8,128)(2,1)S(1)} %get-tuple-element.245), channel_id=1, source_target_pairs={{0,6},{1,7},{2,0},{3,1},{4,2},{5,3},{6,4},{7,5},{8,14},{9,15},{10,... | collective-permute-start | bytes 1572872 | tf_op jit(solution)/shard_map/ppermute | solution.py:92
  676.1 36.9 %collective-permute-start.49 = (bf16[128,2048]{1,0:T(8,128)(2,1)S(1)}, bf16[128,2048]{1,0:T(8,128)(2,1)S(1)}, u32[]{:S(2)}, u32[]{:S(2)}) collective-permute-start(bf16[128,2048]{1,0:T(8,128)(2,1)S(1)} %get-tuple-element.246), channel_id=1, source_target_pairs={{0,4},{1,5},{2,6},{3,7},{4,0},{5,1},{6,2},{7,3},{8,12},{9,13},{10,... | collective-permute-start | bytes 1572872 | tf_op jit(solution)/shard_map/ppermute | solution.py:92
  676.6 36.3 %collective-permute-start.48 = (bf16[128,2048]{1,0:T(8,128)(2,1)S(1)}, bf16[128,2048]{1,0:T(8,128)(2,1)S(1)}, u32[]{:S(2)}, u32[]{:S(2)}) collective-permute-start(bf16[128,2048]{1,0:T(8,128)(2,1)S(1)} %get-tuple-element.244), channel_id=1, source_target_pairs={{0,2},{1,3},{2,4},{3,5},{4,6},{5,7},{6,0},{7,1},{8,10},{9,11},{10,... | collective-permute-start | bytes 1572872 | tf_op jit(solution)/shard_map/ppermute | solution.py:92
  (161 other events, 2227.4 us)
Sparse Core Ops, SparseCore 0:
  94.0 52.6 all-gather.1
  337.4 106.3 reduce-scatter.1
  562.1 86.7 all-reduce.3

commit v4 on v3

v4 whole, which is shorter than its diff:
```python
import math

import jax
import jax.numpy as jnp
from jax import lax
from jax.experimental import pallas as pl
from jax.experimental.pallas import tpu as pltpu
from jax.sharding import PartitionSpec as P

NS_STEPS = 3
FF_BLOCK = 352
SIDE = 4
CORES = 2
LANES = 128

coef_first = 3.4445
coef_second = -4.775
coef_third = 2.0315
muon_rate = 0.5
gain_rate = 0.004
decay_rate = 0.5
low_type = jnp.bfloat16


def matmul(left, right):
    return jnp.dot(left, right, preferred_element_type=jnp.float32)


def matmul_nt(left, right):
    return lax.dot_general(
        left, right, (((1,), (1,)), ((), ())), preferred_element_type=jnp.float32
    )


def matmul_tn(left, right):
    return lax.dot_general(
        left, right, (((0,), (0,)), ((), ())), preferred_element_type=jnp.float32
    )


def rms_scale(values):
    return lax.rsqrt(jnp.mean(values * values, axis=-1, keepdims=True) + 1e-05)


def norm_back(values, scale, gain, grad_out):
    weighted = gain * grad_out
    inner = jnp.mean(values * weighted, axis=-1, keepdims=True)
    grad_in = scale * weighted - values * (scale * scale * scale) * inner
    gain_grad = jnp.sum(grad_out * values * scale, axis=0)
    return (grad_in, gain_grad)


def segment_info(starts, token_index):
    started = starts[None, :] <= token_index[:, None]
    seg_ids = jnp.sum(started.astype(jnp.int32), axis=1)
    seg_begin = jnp.max(jnp.where(started, starts[None, :], 0), axis=1)
    return (seg_ids, token_index - seg_begin)


def rotary_tables(positions, head_dim):
    half_dim = head_dim // 2
    frequency = jnp.exp(
        jnp.arange(half_dim, dtype=jnp.float32) * (-2.0 * math.log(10000.0) / head_dim)
    )
    angles = positions.astype(jnp.float32)[:, None] * frequency[None, :]
    return (jnp.cos(angles), jnp.sin(angles))


def rotate(values, cosine, sine_part):
    half_dim = values.shape[-1] // 2
    first_half = values[..., :half_dim]
    second_half = values[..., half_dim:]
    return jnp.concatenate(
        [
            first_half * cosine - second_half * sine_part,
            second_half * cosine + first_half * sine_part,
        ],
        axis=-1,
    )


def rotate_back(grads, cosine, sine_part):
    return rotate(grads, cosine, -sine_part)


def shift_heads(values, step, core):
    pairs = [
        (CORES * place + side, CORES * ((place + step) % SIDE) + (side ^ core))
        for place in range(SIDE)
        for side in range(CORES)
    ]
    return lax.ppermute(values, "heads", pairs)


def shift_dp(values, step_z, step_x):
    pairs = [
        (SIDE * z + x, SIDE * ((z + step_z) % SIDE) + (x + step_x) % SIDE)
        for z in range(SIDE)
        for x in range(SIDE)
    ]
    return lax.ppermute(values, "dp", pairs)


def gather_heads(own):
    ring = [own] + [shift_heads(own, -step, 0) for step in range(1, SIDE)]
    return ring + [shift_heads(piece, 0, 1) for piece in ring]


def chip_sums(far_half, near_half):
    rows = near_half.shape[0] // SIDE
    total = near_half.astype(jnp.float32) + shift_heads(far_half, 0, 1).astype(jnp.float32)
    return total.astype(far_half.dtype).reshape(SIDE, rows, *near_half.shape[1:])


def ring_sums(chip):
    total = chip[0].astype(jnp.float32)
    for step in range(1, SIDE):
        total = total + shift_heads(chip[step], step, 0).astype(jnp.float32)
    return total


def pick(array, place, axis):
    return lax.dynamic_index_in_dim(array, place % SIDE, axis, keepdims=False)


def scatter_x(parts):
    place_x = lax.axis_index("dp") % SIDE
    grid = parts.reshape(SIDE, SIDE, *parts.shape[1:])
    total = pick(grid, place_x, 1).astype(jnp.float32)
    for step in range(1, SIDE):
        total = total + shift_dp(pick(grid, place_x + step, 1), 0, step).astype(jnp.float32)
    return total.astype(parts.dtype)


def scatter_z(column):
    place_z = lax.axis_index("dp") // SIDE
    total = pick(column, place_z, 0).astype(jnp.float32)
    for step in range(1, SIDE):
        total = total + shift_dp(pick(column, place_z + step, 0), step, 0).astype(jnp.float32)
    return total


def sum_dp(part):
    for axis in range(2):
        total = part.astype(jnp.float32)
        for step in range(1, SIDE):
            total = total + shift_dp(part, step * axis, step * (1 - axis)).astype(jnp.float32)
        part = total.astype(part.dtype)
    return part


def gather_dp(own):
    ring = jnp.concatenate([own] + [shift_dp(own, 0, step) for step in range(1, SIDE)], axis=0)
    return [ring] + [shift_dp(ring, step, 0) for step in range(1, SIDE)]


def after(values, *earlier):
    return lax.optimization_barrier((values, *earlier))[0]


vmem_mib = {
    "attend": 18,
    "attend_back": 30,
    "ffn_near": 30,
    "ffn_far": 30,
    "ffn_grads": 20,
    "shared_ortho": 28,
}


def kernel_call(body, name, grid, prefetch, in_specs, out_specs, out_shape, scratch, flops, moved):
    return pl.pallas_call(
        body,
        grid_spec=pltpu.PrefetchScalarGridSpec(
            num_scalar_prefetch=prefetch,
            grid=grid,
            in_specs=in_specs,
            out_specs=out_specs,
            scratch_shapes=scratch,
        ),
        out_shape=out_shape,
        compiler_params=pltpu.CompilerParams(vmem_limit_bytes=vmem_mib.get(name, 16) * 1024 * 1024),
        cost_estimate=pl.CostEstimate(flops=flops, bytes_accessed=moved, transcendentals=0),
        name=name,
    )


def shaped(shape, kind):
    return jax.ShapeDtypeStruct(shape, kind)


def fixed(shape):
    return pl.BlockSpec(
        shape, lambda *grid: (0,) * len(shape), pipeline_mode=pl.Buffered(buffer_count=1)
    )


def visible(ids_q, ids_k, first_row, rows, cols):
    query_at = first_row + lax.broadcasted_iota(jnp.int32, (rows, cols), 0)
    key_at = lax.broadcasted_iota(jnp.int32, (rows, cols), 1)
    return (ids_q == ids_k) & (key_at <= query_at)


def block_at(index, piece):
    return pl.ds(pl.multiple_of(index * piece, piece), piece)


def store_by_distance(where, rows_ref, near_ref, far_ref, piece):
    core = where[SIDE * CORES]
    for step in range(SIDE):
        near = CORES * step + core
        far = CORES * step + 1 - core
        near_ref[block_at(where[near], piece), :] = rows_ref[block_at(near, piece), :].astype(
            near_ref.dtype
        )
        far_ref[block_at(where[far] - SIDE, piece), :] = rows_ref[block_at(far, piece), :].astype(
            far_ref.dtype
        )


def attend_kernel(
    where, packed, weight, cosine, sine, ids_q, ids_k, query_out, near_out, far_out, lse_out, mixed
):
    latent_width, head_dim = weight.shape
    piece = packed.shape[0] // (SIDE * CORES)
    block = CORES * piece
    scale = head_dim ** (-0.5)
    key_cols = slice(latent_width, latent_width + head_dim)
    value_cols = slice(latent_width + head_dim, latent_width + 2 * head_dim)
    for index in range(SIDE):
        first = index * block
        end = first + block
        rows = slice(first, end)
        query = matmul(packed[rows, :latent_width], weight[...])
        query = rotate(query, cosine[rows, :], sine[rows, :]).astype(low_type)
        query_out[rows, :] = query
        scores = matmul_nt(query, packed[:end, key_cols]) * scale
        allowed = visible(ids_q[rows, :], ids_k[:, :end], first, block, end)
        scores = jnp.where(allowed, scores, -1e30)
        row_max = jnp.max(scores, axis=-1, keepdims=True)
        exponent = jnp.exp(scores - row_max)
        row_total = jnp.sum(exponent, axis=-1, keepdims=True)
        probs = (exponent * (1.0 / row_total)).astype(low_type)
        lse_out[0, rows, :] = row_max + jnp.log(row_total)
        mixed[rows, :] = matmul(probs, packed[:end, value_cols]).astype(low_type)
    store_by_distance(where, mixed, near_out, far_out, piece)


def attend(where, packed, w_q_up, head_dim, cosine, sine, row_ids):
    row_len, packed_width = packed.shape
    latent_width, width = w_q_up.shape
    count = width // head_dim
    column = lambda head, where: (0, head)
    return kernel_call(
        attend_kernel,
        "attend",
        (count,),
        1,
        [
            fixed((row_len, packed_width)),
            pl.BlockSpec((latent_width, head_dim), column),
            fixed((row_len, head_dim // 2)),
            fixed((row_len, head_dim // 2)),
            fixed((row_len, 1)),
            fixed((1, row_len)),
        ],
        [
            pl.BlockSpec((row_len, head_dim), column),
            pl.BlockSpec((row_len // 2, head_dim), column),
            pl.BlockSpec((row_len // 2, head_dim), column),
            pl.BlockSpec((1, row_len, 1), lambda head, where: (head, 0, 0)),
        ],
        [
            shaped((row_len, width), low_type),
            shaped((row_len // 2, width), low_type),
            shaped((row_len // 2, width), low_type),
            shaped((count, row_len, 1), jnp.float32),
        ],
        [pltpu.VMEM((row_len, head_dim), low_type)],
        2 * width * row_len * (latent_width + 2 * row_len),
        8 * row_len * width,
    )(where, packed, w_q_up, cosine, sine, row_ids[:, None], row_ids[None, :])


def attend_back_kernel(where, *refs):
    pieces = refs[: SIDE * CORES]
    query_in, packed, w_out, weight, lse, cosine, sine, ids_q, ids_k = refs[
        SIDE * CORES : SIDE * CORES + 9
    ]
    weight_back, near_out, far_out, query_back, back_rows, totals = refs[SIDE * CORES + 9 :]
    row_len = packed.shape[0]
    latent_width, head_dim = weight.shape
    piece = row_len // (SIDE * CORES)
    block = CORES * piece
    scale = head_dim ** (-0.5)
    head = pl.program_id(0)
    key_cols = slice(latent_width, latent_width + head_dim)
    value_cols = slice(latent_width + head_dim, latent_width + 2 * head_dim)

    @pl.when(head == 0)
    def _():
        totals[...] = jnp.zeros_like(totals)

    for index in range(0, SIDE * CORES, 2):
        pair = jnp.concatenate([pieces[index][...], pieces[index + 1][...]], axis=0)
        back_rows[index * piece : (index + 2) * piece, :] = matmul(pair, w_out[...]).astype(
            low_type
        )
    for index in range(SIDE):
        first = index * block
        end = first + block
        rows = slice(first, end)
        query = query_in[rows, :]
        back = jnp.concatenate(
            [
                back_rows[block_at(where[CORES * index + side], piece), :]
                for side in range(CORES)
            ],
            axis=0,
        )
        keys = packed[:end, key_cols]
        scores = matmul_nt(query, keys) * scale
        allowed = visible(ids_q[rows, :], ids_k[:, :end], first, block, end)
        probs = jnp.where(allowed, jnp.exp(scores - lse[0, rows, :]), 0.0)
        probs_back = matmul_nt(back, packed[:end, value_cols])
        inner = jnp.sum(probs * probs_back, axis=-1, keepdims=True)
        score_back = (probs * (probs_back - inner)).astype(low_type)
        totals[:end, value_cols] += matmul_tn(probs.astype(low_type), back)
        totals[:end, key_cols] += matmul_tn(score_back, query) * scale
        query_grad = matmul(score_back, keys) * scale
        query_back[rows, :] = rotate_back(query_grad, cosine[rows, :], sine[rows, :]).astype(
            low_type
        )
        totals[rows, :latent_width] += matmul_nt(query_back[rows, :], weight[...])
    weight_back[...] = matmul_tn(packed[:, :latent_width], query_back[...]).astype(low_type)

    @pl.when(head == pl.num_programs(0) - 1)
    def _():
        store_by_distance(where, totals, near_out, far_out, piece)


def attend_back(where, pieces, query_rows, packed, w_out, w_q_up, lse, cosine, sine, row_ids):
    row_len, packed_width = packed.shape
    latent_width, width = w_q_up.shape
    model_width = w_out.shape[0]
    head_dim = (packed_width - latent_width) // 2
    count = width // head_dim
    column = lambda head, where: (0, head)
    return kernel_call(
        attend_back_kernel,
        "attend_back",
        (count,),
        1,
        [fixed(pieces[0].shape)] * len(pieces)
        + [
            pl.BlockSpec((row_len, head_dim), column),
            fixed((row_len, packed_width)),
            pl.BlockSpec((model_width, head_dim), column),
            pl.BlockSpec((latent_width, head_dim), column),
            pl.BlockSpec((1, row_len, 1), lambda head, where: (head, 0, 0)),
            fixed((row_len, head_dim // 2)),
            fixed((row_len, head_dim // 2)),
            fixed((row_len, 1)),
            fixed((1, row_len)),
        ],
        [
            pl.BlockSpec((latent_width, head_dim), column),
            fixed((row_len // 2, packed_width)),
            fixed((row_len // 2, packed_width)),
        ],
        [
            shaped((latent_width, width), low_type),
            shaped((row_len // 2, packed_width), low_type),
            shaped((row_len // 2, packed_width), low_type),
        ],
        [
            pltpu.VMEM((row_len, head_dim), low_type),
            pltpu.VMEM((row_len, head_dim), low_type),
            pltpu.VMEM((row_len, packed_width), jnp.float32),
        ],
        2 * width * row_len * (5 * row_len + model_width + 2 * latent_width),
        8 * row_len * width,
    )(
        where,
        *pieces,
        query_rows,
        packed,
        w_out,
        w_q_up,
        lse,
        cosine,
        sine,
        row_ids[:, None],
        row_ids[None, :],
    )


def ffn_kernel(owner, *refs):
    pieces = refs[:SIDE]
    grads = refs[SIDE : 2 * SIDE]
    w_gate, w_up, w_down = refs[2 * SIDE : 2 * SIDE + 3]
    gate_out, up_out, middle_out, features_back = refs[2 * SIDE + 3 :]
    piece = pieces[0].shape[0]
    for index in range(0, SIDE, 2):
        cols = slice(index * piece, (index + 2) * piece)
        pair = jnp.concatenate([pieces[index][...], pieces[index + 1][...]], axis=0)
        grad_pair = jnp.concatenate([grads[index][...], grads[index + 1][...]], axis=0)
        gate = matmul_nt(w_gate[...], pair)
        up = matmul_nt(w_up[...], pair)
        middle_back = matmul_nt(w_down[...], grad_pair)
        sigmoid = jax.nn.sigmoid(gate)
        activated = gate * sigmoid
        gate_back = (middle_back * up * sigmoid * (1.0 + gate * (1.0 - sigmoid))).astype(low_type)
        up_back = (middle_back * activated).astype(low_type)
        middle_out[:, cols] = (activated * up).astype(low_type)
        gate_out[:, cols] = gate_back
        up_out[:, cols] = up_back
        features_back[cols, :] = (
            matmul_tn(gate_back, w_gate[...]) + matmul_tn(up_back, w_up[...])
        ).astype(low_type)


def ffn_half(owner, pieces, grads, w_gate, w_up, w_down, far):
    piece, model_width = pieces[0].shape
    width = w_gate.shape[0]
    rows = SIDE * piece
    grad_specs = [
        pl.BlockSpec(
            (piece, model_width),
            lambda index, owner, place=SIDE * far + step: (owner[place], 0),
            pipeline_mode=pl.Buffered(buffer_count=1),
        )
        for step in range(SIDE)
    ]
    return kernel_call(
        ffn_kernel,
        "ffn_far" if far else "ffn_near",
        (1,),
        1,
        [fixed((piece, model_width))] * SIDE + grad_specs + [fixed((width, model_width))] * 3,
        [fixed((width, rows))] * 3 + [fixed((rows, model_width))],
        [shaped((width, rows), low_type)] * 3 + [shaped((rows, model_width), low_type)],
        [],
        10 * rows * model_width * width,
        6 * model_width * width + 6 * rows * model_width,
    )(owner, *pieces, *([grads] * SIDE), w_gate, w_up, w_down)


def ffn_grads_kernel(owner, *refs):
    count = SIDE * CORES
    pieces, grads, halves, target = refs[:count], refs[count : 2 * count], refs[-7:-1], refs[-1]
    width, half_rows = halves[0].shape
    share = target.shape[2]
    features = jnp.concatenate([source[...] for source in pieces], axis=0)
    grads = jnp.concatenate([source[...] for source in grads], axis=0)
    for index, right in enumerate((features, features, grads)):
        total = matmul(halves[index][...], right[:half_rows, :])
        total += matmul(halves[index + 3][...], right[half_rows:, :])
        total = total.astype(low_type)
        for place in range(target.shape[0]):
            target[place, index * width : (index + 1) * width, :] = total[
                :, place * share : (place + 1) * share
            ]


def ffn_grads(owner, pieces, grads, halves, dp_count):
    piece, model_width = pieces[0].shape
    row_len = grads.shape[0]
    width = halves[0].shape[0]
    block = model_width // 8
    share = model_width // dp_count
    return kernel_call(
        ffn_grads_kernel,
        "ffn_grads",
        (8,),
        1,
        [pl.BlockSpec((piece, block), lambda index, owner: (0, index))] * len(pieces)
        + [
            pl.BlockSpec((piece, block), lambda index, owner, place=place: (owner[place], index))
            for place in range(len(pieces))
        ]
        + [fixed(halves[0].shape)] * 6,
        pl.BlockSpec((block // share, 3 * width, share), lambda index, owner: (index, 0, 0)),
        shaped((dp_count, 3 * width, share), low_type),
        [],
        6 * row_len * model_width * width,
        4 * row_len * model_width + 6 * model_width * width,
    )(owner, *pieces, *([grads] * len(pieces)), *halves)


def joined_tn(left, right, steps, name):
    piece, width = left[0].shape
    block = width // steps
    count = len(left)
    cols = right[0].shape[1]
    rows = piece * count

    def body(*refs):
        left, right, target = refs[:count], refs[count:-1], refs[-1]
        left = jnp.concatenate([source[...] for source in left], axis=0)
        right = jnp.concatenate([source[...] for source in right], axis=0)
        target[...] = matmul_tn(left, right).astype(target.dtype)

    return kernel_call(
        body,
        name,
        (steps,),
        0,
        [pl.BlockSpec((piece, block), lambda index: (0, index))] * count
        + [fixed(source.shape) for source in right],
        pl.BlockSpec((block, cols), lambda index: (index, 0)),
        shaped((width, cols), low_type),
        [],
        2 * rows * width * cols,
        2 * rows * (width + cols) + 2 * width * cols,
    )(*left, *right)


def joined(owner, left, right, name):
    count = len(right)
    width = left.shape[0] // count
    piece, cols = right[0].shape

    def body(owner, *refs):
        left, right, target = refs[:count], refs[count:-1], refs[-1]
        left = jnp.concatenate([source[...] for source in left], axis=1)
        right = jnp.concatenate([source[...] for source in right], axis=0)
        target[...] = matmul(left, right).astype(target.dtype)

    return kernel_call(
        body,
        name,
        (1,),
        1,
        [
            pl.BlockSpec((width, piece), lambda index, owner, place=place: (owner[place], 0))
            for place in range(count)
        ]
        + [fixed(source.shape) for source in right],
        fixed((width, cols)),
        shaped((width, cols), low_type),
        [],
        2 * piece * count * width * cols,
        2 * piece * count * (width + cols) + 2 * width * cols,
    )(owner, *([left] * count), *right)


def panel_places(block):
    panel = min(block, LANES)
    count = -(-block // panel)
    return panel, count, upper_blocks(count)


def upper_blocks(count):
    return [(row, col) for row in range(count) for col in range(row, count)]


def momentum_kernel(spans, block, turned, *refs):
    count = len(spans)
    sums, moms = refs[0], refs[1 : 1 + count]
    grad_out, mom_out = refs[1 + count : 1 + 2 * count], refs[1 + 2 * count : 1 + 3 * count]
    gram_out = refs[-1]
    panel, tiles, places = panel_places(block)
    place = 0
    for index, (row_at, rows) in enumerate(spans):
        grad = sums[row_at : row_at + rows, :].astype(jnp.float32)
        new = decay_rate * moms[index][...] + grad
        grad_out[index][...] = grad
        mom_out[index][...] = new
        low = new.astype(low_type)
        for first in range(0, low.shape[0 if turned else 1], block):
            if turned:
                part = low[first : first + block, :]
                if tiles * panel > block:
                    blank = jnp.zeros((tiles * panel - block, part.shape[1]), low_type)
                    part = jnp.concatenate([part, blank], axis=0)
                gram = matmul_nt(part, part).astype(low_type)
            else:
                part = low[:, first : first + block]
                gram = matmul_tn(part, part).astype(low_type)
            for row, col in places:
                gram_out[place * panel : (place + 1) * panel, :] = gram[
                    row * panel : (row + 1) * panel, col * panel : (col + 1) * panel
                ]
                place += 1


def momenta(sums, moms, block, turned, name):
    axis = 0 if turned else 1
    blocks = sum(mom.shape[axis] // block for mom in moms)
    panel, tiles, places = panel_places(block)
    spans, row_at = [], 0
    for mom in moms:
        spans.append((row_at, mom.shape[0]))
        row_at += mom.shape[0]

    def body(*refs):
        momentum_kernel(spans, block, turned, *refs)

    shapes = [mom.shape for mom in moms]
    panels = (blocks * len(places) * panel, panel)
    results = kernel_call(
        body,
        name,
        (1,),
        0,
        [fixed(sums.shape)] + [fixed(shape) for shape in shapes],
        [fixed(shape) for shape in shapes + shapes] + [fixed(panels)],
        [shaped(shape, jnp.float32) for shape in shapes + shapes] + [shaped(panels, low_type)],
        [],
        2 * block * sum(shape[0] * shape[1] for shape in shapes),
        16 * sum(shape[0] * shape[1] for shape in shapes),
    )(sums, *moms)
    count = len(moms)
    return results[:count], results[count : 2 * count], results[-1]


def trace_of(gram):
    rows = lax.broadcasted_iota(jnp.int32, gram.shape, 0)
    cols = lax.broadcasted_iota(jnp.int32, gram.shape, 1)
    diagonal = jnp.where(rows == cols, gram, 0.0)
    return jnp.sum(jnp.sum(diagonal, axis=0, keepdims=True), axis=1, keepdims=True)


def polish_small(gram, block, turned=False):
    def apply(values, right):
        values = values.astype(low_type)
        return matmul(right, values) if turned else matmul(values, right)

    factor = 1.0 / (jnp.sqrt(trace_of(gram)) + 1e-07)
    iterate = block * factor
    gram = gram * (factor * factor)
    for step_index in range(NS_STEPS):
        gram_low = gram.astype(low_type)
        if step_index + 1 == NS_STEPS:
            first_term = apply(iterate, gram_low)
            second_term = apply(first_term, gram_low)
            return coef_first * iterate + coef_second * first_term + coef_third * second_term
        change = (coef_second * gram + coef_third * matmul(gram_low, gram_low)).astype(low_type)
        iterate = coef_first * iterate + apply(iterate, change)
        once = matmul(gram_low, change)
        twice = matmul(once.astype(low_type), change)
        gram = (coef_first * coef_first) * gram + (2.0 * coef_first) * once + twice


def update_kernel(block, turned, rates, origin, *refs):
    count = len(rates)
    flat = refs[-1]
    sources = refs[: -1 - 3 * count]
    moms, weights = refs[-1 - 3 * count : -1 - 2 * count], refs[-1 - 2 * count : -1 - count]
    targets = refs[-1 - count : -1]
    panel, tiles, places = panel_places(block)
    if len(sources) == 1:
        flat = sources[0]
    else:
        chunk = sources[0].shape[0] // SIDE
        for index, source in enumerate(sources):
            for part in range(SIDE):
                flat[block_at(origin[1 + SIDE * index + part], chunk), :] = source[
                    part * chunk : (part + 1) * chunk, :
                ]
    place = 0
    for index, rate in enumerate(rates):
        for first in range(0, moms[index].shape[0 if turned else 1], block):
            parts = {}
            for row, col in places:
                parts[row, col] = flat[place * panel : (place + 1) * panel, :].astype(jnp.float32)
                if row != col:
                    parts[col, row] = parts[row, col].T
                place += 1
            gram = jnp.concatenate(
                [
                    jnp.concatenate([parts[row, col] for col in range(tiles)], axis=1)
                    for row in range(tiles)
                ],
                axis=0,
            )
            part = slice(first, first + block)
            area = (part, slice(None)) if turned else (slice(None), part)
            start = moms[index][area]
            if turned and tiles * panel > block:
                blank = jnp.zeros((tiles * panel - block, start.shape[1]), jnp.float32)
                start = jnp.concatenate([start, blank], axis=0)
            ortho = polish_small(gram, start, turned)
            if turned:
                ortho = ortho[:block, :]
            targets[index][area] = weights[index][area].astype(jnp.float32) - rate * ortho


def updates(origin, panels, moms, weights, block, turned, name):
    axis = 1 if turned else 0
    rates = [muon_rate * math.sqrt(weight.shape[axis] / block) for weight in weights]

    def body(origin, *refs):
        update_kernel(block, turned, rates, origin, *refs)

    shapes = [mom.shape for mom in moms]
    where_own = (
        (lambda index, origin: (0, origin[0])) if turned else (lambda index, origin: (origin[0], 0))
    )
    rows = sum(source.shape[0] for source in panels)
    panel = panels[0].shape[1]
    return kernel_call(
        body,
        name,
        (1,),
        1,
        [fixed(source.shape) for source in panels]
        + [fixed(shape) for shape in shapes]
        + [pl.BlockSpec(shape, where_own) for shape in shapes],
        [fixed(shape) for shape in shapes],
        [shaped(shape, jnp.float32) for shape in shapes],
        [pltpu.VMEM((rows, panel), low_type)],
        14 * rows * panel * block,
        sum(12 * shape[0] * shape[1] for shape in shapes),
    )(origin, *panels, *moms, *weights)


def polish(gram, gram_low, change_low, once_low, iterate, size):
    block = min(size, 256)
    count = size // block
    for step_index in range(NS_STEPS):
        last = step_index + 1 == NS_STEPS
        if last:
            first_term = matmul(iterate.astype(low_type), gram_low[...])
            second_term = matmul(first_term.astype(low_type), gram_low[...])
            return coef_first * iterate + coef_second * first_term + coef_third * second_term

        def make_change(index, carry):
            rows = block_at(index, block)
            square = matmul(gram_low[rows, :], gram_low[...])
            change_low[rows, :] = (coef_second * gram[rows, :] + coef_third * square).astype(
                low_type
            )
            return carry

        def make_once(index, carry):
            rows = block_at(index, block)
            once = matmul(gram_low[rows, :], change_low[...])
            once_low[rows, :] = once.astype(low_type)
            gram[rows, :] = (coef_first * coef_first) * gram[rows, :] + (2.0 * coef_first) * once
            return carry

        def make_gram(index, carry):
            rows = block_at(index, block)
            total = gram[rows, :] + matmul(once_low[rows, :], change_low[...])
            gram[rows, :] = total
            gram_low[rows, :] = total.astype(low_type)
            return carry

        lax.fori_loop(0, count, make_change, 0)
        iterate = coef_first * iterate + matmul(iterate.astype(low_type), change_low[...])
        lax.fori_loop(0, count, make_once, 0)
        lax.fori_loop(0, count, make_gram, 0)


def gram_parts_kernel(where, *refs):
    pieces, gains, near_out, far_out, blocks = refs[:SIDE], refs[-4], refs[-3], refs[-2], refs[-1]
    narrow = blocks.shape[1]
    chunk = blocks.shape[0] // (SIDE * CORES)
    extra = gains.shape[0] // (SIDE * CORES)
    rows = jnp.concatenate([source[...] for source in pieces], axis=0)
    wide = rows.shape[1] // narrow
    places = upper_blocks(wide - 2) + [(wide - 2, wide - 2), (wide - 1, wide - 1)]
    for index, (left, right) in enumerate(places):
        blocks[index * narrow : (index + 1) * narrow, :] = matmul_tn(
            rows[:, left * narrow : (left + 1) * narrow],
            rows[:, right * narrow : (right + 1) * narrow],
        ).astype(low_type)
    core = where[SIDE * CORES]
    for step in range(SIDE):
        near = CORES * step + core
        far = CORES * step + 1 - core
        for target, source, place in ((near_out, near, 0), (far_out, far, SIDE)):
            start = pl.multiple_of((where[source] - place) * (chunk + extra), extra)
            target[pl.ds(start, chunk), :] = blocks[block_at(source, chunk), :]
            start = pl.multiple_of(start + chunk, extra)
            target[pl.ds(start, extra), :] = gains[block_at(source, extra), :]


def gram_parts(where, pieces, gains, narrow):
    wide = pieces[0].shape[1] // narrow - 2
    total = (wide * (wide + 1) // 2 + 2) * narrow
    out_rows = (total + gains.shape[0]) // CORES
    rows = SIDE * pieces[0].shape[0]
    return kernel_call(
        gram_parts_kernel,
        "gram_parts",
        (1,),
        1,
        [fixed(piece.shape) for piece in pieces] + [fixed(gains.shape)],
        [fixed((out_rows, narrow))] * 2,
        [shaped((out_rows, narrow), low_type)] * 2,
        [pltpu.VMEM((total, narrow), low_type)],
        2 * rows * total * narrow,
        4 * total * narrow,
    )(where, *pieces, gains)


def shared_kernel(owner, *refs):
    pieces = refs[: SIDE * CORES]
    own, target, blocks, gram, gram_low, change_low, once_low = refs[SIDE * CORES :]
    chunk, narrow = pieces[0].shape
    wide = gram.shape[0]
    for index, source in enumerate(pieces):
        blocks[block_at(owner[index], chunk), :] = source[...]
    places = upper_blocks(wide // narrow)
    trace = jnp.zeros((1, 1), jnp.float32)
    for index, (left, right) in enumerate(places):
        if left == right:
            trace += trace_of(blocks[index * narrow : (index + 1) * narrow, :].astype(jnp.float32))
    factor = 1.0 / (jnp.sqrt(trace) + 1e-07)
    for index, (left, right) in enumerate(places):
        block = blocks[index * narrow : (index + 1) * narrow, :].astype(jnp.float32)
        block = block * (factor * factor)
        rows = slice(left * narrow, (left + 1) * narrow)
        cols = slice(right * narrow, (right + 1) * narrow)
        gram[rows, cols] = block
        gram_low[rows, cols] = block.astype(low_type)
        if left != right:
            turned = block.T
            gram[cols, rows] = turned
            gram_low[cols, rows] = turned.astype(low_type)
    for index in range(2):
        cols = slice(wide + index * narrow, wide + (index + 1) * narrow)
        first = (len(places) + index) * narrow
        small = blocks[first : first + narrow, :].astype(jnp.float32)
        target[:, cols] = polish_small(small, own[:, cols])
    target[:, :wide] = polish(gram, gram_low, change_low, once_low, own[:, :wide] * factor, wide)


def shared_ortho(owner, pieces, own, wide):
    chunk, narrow = pieces[0].shape
    return kernel_call(
        shared_kernel,
        "shared_ortho",
        (1,),
        1,
        [fixed(piece.shape) for piece in pieces] + [fixed(own.shape)],
        fixed(own.shape),
        shaped(own.shape, jnp.float32),
        [pltpu.VMEM((SIDE * CORES * chunk, narrow), low_type), pltpu.VMEM((wide, wide), jnp.float32)]
        + [pltpu.VMEM((wide, wide), low_type)] * 3,
        20 * wide * wide * wide,
        8 * wide * wide,
    )(owner, *pieces, own)


def own_rows(weight, count, rank):
    share_rows = weight.shape[0] // count
    return lax.dynamic_slice_in_dim(weight, rank * share_rows, share_rows, 0).astype(jnp.float32)


def on_device(
    tokens_in,
    cotangent,
    seg_starts,
    gains,
    w_q_down,
    w_key,
    w_value,
    w_q_up,
    w_out,
    w_gate,
    w_up,
    w_down,
    mom_gains,
    mom_q_down,
    mom_key,
    mom_value,
    mom_q_up,
    mom_out,
    mom_gate,
    mom_up,
    mom_down,
):
    heads_count = lax.axis_size("heads")
    heads_rank = lax.axis_index("heads")
    dp_count = lax.axis_size("dp")
    dp_rank = lax.axis_index("dp")
    all_rank = lax.axis_index(("dp", "heads"))
    all_count = dp_count * heads_count
    local_rows = tokens_in.shape[0]
    row_len = local_rows * heads_count
    model_width = tokens_in.shape[1]
    latent_width = w_q_down.shape[1]
    head_dim = w_key.shape[1]
    local_q = w_q_up.shape[1]
    share_rows = model_width // all_count
    share_gains = gains.shape[0] // all_count
    starts = seg_starts[0]
    whole_index = jnp.arange(row_len, dtype=jnp.int32)
    own_index = heads_rank * local_rows + jnp.arange(local_rows, dtype=jnp.int32)
    own_core = heads_rank % CORES
    own_step = heads_rank // CORES
    ranks = jnp.arange(heads_count, dtype=jnp.int32)
    where = SIDE * ((ranks % CORES) ^ own_core) + (ranks // CORES - own_step) % SIDE
    where = jnp.concatenate([where, own_core[None]]).astype(jnp.int32)
    owner = CORES * ((ranks % SIDE + own_step) % SIDE) + ((ranks // SIDE) ^ own_core)
    owner = owner.astype(jnp.int32)
    shifts = jnp.arange(SIDE, dtype=jnp.int32)
    origin_z = (dp_rank // SIDE - shifts) % SIDE
    origin_x = (dp_rank % SIDE - shifts) % SIDE
    origin = (SIDE * origin_z[:, None] + origin_x[None, :]).reshape(dp_count)
    origin = jnp.concatenate([dp_rank[None], origin]).astype(jnp.int32)
    gain_one = gains[:model_width]
    gain_latent = gains[model_width : model_width + latent_width]
    gain_two = gains[model_width + latent_width :]

    inputs = tokens_in.astype(jnp.float32)
    scale_one = rms_scale(inputs)
    normed_one = (inputs * scale_one * gain_one).astype(low_type)
    latent_raw = matmul(normed_one, w_q_down)
    scale_latent = rms_scale(latent_raw)
    latent_normed = (latent_raw * scale_latent * gain_latent).astype(low_type)
    own_pos = segment_info(starts, own_index)[1]
    own_cos, own_sin = rotary_tables(own_pos, head_dim)
    key_local = rotate(matmul(normed_one, w_key), own_cos, own_sin).astype(low_type)
    value_local = matmul(normed_one, w_value).astype(low_type)
    packed = lax.all_gather(
        jnp.concatenate([latent_normed, key_local, value_local], axis=1), "heads", axis=0, tiled=True
    )
    grad_rows = lax.all_gather(after(cotangent, packed), "heads", axis=0, tiled=True)
    normed_parts = lax.all_to_all(
        normed_one.T.reshape(dp_count, heads_count, share_rows, local_rows)
        .transpose(1, 0, 2, 3)
        .reshape(model_width, local_rows),
        "heads",
        split_axis=0,
        concat_axis=0,
        tiled=True,
    )
    packed, normed_parts = lax.optimization_barrier((packed, normed_parts))
    row_ids, row_pos = segment_info(starts, whole_index)
    row_cos, row_sin = rotary_tables(row_pos, head_dim)
    query_rows, attended_near, attended_far, lse = attend(
        where, packed, w_q_up, head_dim, row_cos, row_sin, row_ids
    )
    attn_mixed = ring_sums(
        chip_sums(
            matmul_nt(attended_far, w_out).astype(low_type),
            matmul_nt(attended_near, w_out).astype(low_type),
        )
    )
    hidden_one = inputs + attn_mixed
    scale_two = rms_scale(hidden_one)
    normed_two = (hidden_one * scale_two * gain_two).astype(low_type)

    gate_turned, up_turned, down_turned = w_gate.T, w_up.T, w_down.T
    pieces_two = gather_heads(normed_two)
    gate_near, up_near, middle_near, back_near = ffn_half(
        owner, pieces_two[:SIDE], grad_rows, gate_turned, up_turned, down_turned, 0
    )
    gate_far, up_far, middle_far, back_far = ffn_half(
        owner, pieces_two[SIDE:], grad_rows, gate_turned, up_turned, down_turned, 1
    )
    chip_two = chip_sums(back_far, back_near)
    normed_two_back = ring_sums(chip_two)
    ffn_part = ffn_grads(
        owner,
        pieces_two,
        grad_rows,
        (after(gate_near, chip_two), up_near, middle_near, gate_far, up_far, middle_far),
        dp_count,
    )
    ffn_sums = lax.psum_scatter(ffn_part, "dp", scatter_dimension=0, tiled=True)[0]
    mixed_far = matmul_tn(after(middle_far, chip_two), down_turned).astype(low_type)
    mixed_near = matmul_tn(middle_near, down_turned).astype(low_type)
    hidden_part, gain_two_grad = norm_back(hidden_one, scale_two, gain_two, normed_two_back)
    hidden_back = cotangent.astype(jnp.float32) + hidden_part

    hidden_low = after(hidden_back.astype(low_type), ffn_part, mixed_far, mixed_near)
    pieces_hidden = gather_heads(hidden_low)
    q_up_part, sums_near, sums_far = attend_back(
        where, pieces_hidden, query_rows, packed, w_out, w_q_up, lse, row_cos, row_sin, row_ids
    )
    ffn_grad, ffn_mom, ffn_gram = momenta(
        ffn_sums, (mom_gate.T, mom_up.T, mom_down.T), FF_BLOCK, True, "ffn_momenta"
    )
    chip_back, ffn_gram = lax.optimization_barrier((chip_sums(sums_far, sums_near), ffn_gram))
    ffn_column = scatter_x(ffn_gram.reshape(dp_count, -1, ffn_gram.shape[1]))
    packed_sums = ring_sums(chip_back)
    out_w_part = joined_tn(pieces_hidden, (attended_near, attended_far), 8, "out_grads")
    out_w_part, packed_sums, ffn_column = lax.optimization_barrier(
        (out_w_part, packed_sums, ffn_column)
    )
    latent_back = packed_sums[:, :latent_width]
    key_sum = packed_sums[:, latent_width : latent_width + head_dim]
    value_sum = packed_sums[:, latent_width + head_dim :]
    latent_raw_grad, gain_latent_grad = norm_back(
        latent_raw, scale_latent, gain_latent, latent_back
    )
    latent_raw_back = latent_raw_grad.astype(low_type)
    key_pre_back = rotate_back(key_sum, own_cos, own_sin).astype(low_type)
    values_low = value_sum.astype(low_type)

    back_low = jnp.concatenate([latent_raw_back, key_pre_back, values_low], axis=1)
    pieces_back = gather_heads(back_low)
    head_column = scatter_x(
        jnp.concatenate(
            [
                after(q_up_part, packed_sums).reshape(dp_count, -1, local_q),
                out_w_part.reshape(dp_count, -1, local_q),
            ],
            axis=1,
        )
    )
    ffn_chunk = scatter_z(ffn_column).astype(low_type)
    pieces_back, head_column, ffn_chunk = lax.optimization_barrier(
        (pieces_back, head_column, ffn_chunk)
    )
    shared_part = joined(owner, normed_parts, pieces_back, "shared_grads")
    normed_one_back = (
        matmul_nt(latent_raw_back, w_q_down)
        + matmul_nt(key_pre_back, w_key)
        + matmul_nt(values_low, w_value)
    )
    input_part, gain_one_grad = norm_back(inputs, scale_one, gain_one, normed_one_back)
    input_grad = hidden_back + input_part
    gains_part = jnp.concatenate([gain_one_grad, gain_latent_grad, gain_two_grad])
    gains_part = gains_part.reshape(dp_count, heads_count, share_gains).astype(low_type)
    gains_part = jnp.pad(
        gains_part, ((0, 0), (0, share_rows - heads_count), (0, LANES - share_gains))
    )

    shared_part, gains_part = lax.optimization_barrier((shared_part, gains_part))
    packed_width = shared_part.shape[1]
    shared_grad = scatter_z(
        scatter_x(
            jnp.concatenate(
                [shared_part.reshape(dp_count, share_rows, packed_width), gains_part], axis=2
            )
        )
    )
    head_sums = scatter_z(head_column)
    ffn_panels = gather_dp(ffn_chunk)
    shared_grad, head_sums, ffn_panels = lax.optimization_barrier(
        (shared_grad, head_sums, ffn_panels)
    )
    q_down_grad = shared_grad[:, :latent_width]
    key_w_grad = shared_grad[:, latent_width : latent_width + head_dim]
    value_w_grad = shared_grad[:, latent_width + head_dim : packed_width]
    q_down_mom = decay_rate * mom_q_down + q_down_grad
    key_w_mom = decay_rate * mom_key + key_w_grad
    value_w_mom = decay_rate * mom_value + value_w_grad

    shared_mom = jnp.concatenate([q_down_mom, key_w_mom, value_w_mom], axis=1)
    gains_rows = shared_grad[:heads_count, packed_width : packed_width + share_gains]
    gains_rows = jnp.pad(
        gains_rows.astype(low_type)[:, None, :],
        ((0, 0), (0, share_rows - 1), (0, head_dim - share_gains)),
    ).reshape(heads_count * share_rows, head_dim)
    pieces_mom = gather_dp(shared_mom.astype(low_type))
    gram_near, gram_far = gram_parts(where, pieces_mom, gains_rows, head_dim)
    gram_sums = ring_sums(chip_sums(gram_far, gram_near))
    gram_chunk = gram_sums.shape[0] - share_rows
    pieces_gram = gather_heads(gram_sums[:gram_chunk].astype(low_type))
    chip_mixed = chip_sums(after(mixed_far, shared_grad), mixed_near)
    layer_out = (hidden_one + ring_sums(after(chip_mixed, *pieces_gram))).astype(low_type)
    gains_grad = gram_sums[gram_chunk, :share_gains]
    gains_mom = decay_rate * mom_gains + gains_grad
    gains_new = own_rows(gains, all_count, all_rank) - gain_rate * gains_mom

    head_grad, head_mom, head_gram = momenta(
        head_sums, (mom_q_up, mom_out), head_dim, False, "head_momenta"
    )
    head_gram = sum_dp(after(head_gram, *pieces_mom))
    ffn_new = updates(
        origin,
        ffn_panels,
        ffn_mom,
        (gate_turned, up_turned, down_turned),
        FF_BLOCK,
        True,
        "ffn_updates",
    )
    pieces_gram, ffn_new = lax.optimization_barrier((pieces_gram, ffn_new))
    shared_done = shared_ortho(owner, pieces_gram, shared_mom, latent_width)
    q_up_new, out_w_new = updates(
        origin,
        (after(head_gram, shared_done),),
        head_mom,
        (w_q_up, w_out),
        head_dim,
        False,
        "head_updates",
    )
    q_down_new = (
        own_rows(w_q_down, all_count, all_rank)
        - muon_rate * math.sqrt(model_width / latent_width) * shared_done[:, :latent_width]
    )
    pair_factor = muon_rate * math.sqrt(model_width / head_dim)
    key_w_new = (
        own_rows(w_key, all_count, all_rank)
        - pair_factor * shared_done[:, latent_width : latent_width + head_dim]
    )
    value_w_new = (
        own_rows(w_value, all_count, all_rank)
        - pair_factor * shared_done[:, latent_width + head_dim :]
    )
    ffn_grad, ffn_mom, ffn_new = [
        [array.T for array in arrays] for arrays in (ffn_grad, ffn_mom, ffn_new)
    ]
    return (
        layer_out,
        input_grad,
        gains_grad,
        q_down_grad,
        key_w_grad,
        value_w_grad,
        *head_grad,
        *ffn_grad,
        gains_mom,
        q_down_mom,
        key_w_mom,
        value_w_mom,
        *head_mom,
        *ffn_mom,
        gains_new,
        q_down_new,
        key_w_new,
        value_w_new,
        q_up_new,
        out_w_new,
        *ffn_new,
    )


def solution(mesh):
    placed = (
        P(("dp", "heads"), None),
        P(("dp", "heads"), None),
        P("dp", None),
        P(),
        P(),
        P(),
        P(),
        P(None, "heads"),
        P(None, "heads"),
        P(None, "heads"),
        P(None, "heads"),
        P(None, "heads"),
        P(("dp", "heads")),
        P(("dp", "heads"), None),
        P(("dp", "heads"), None),
        P(("dp", "heads"), None),
        P("dp", "heads"),
        P("dp", "heads"),
        P("dp", "heads"),
        P("dp", "heads"),
        P("dp", "heads"),
    )
    return jax.shard_map(
        on_device,
        mesh=mesh,
        in_specs=placed,
        out_specs=(
            P(("dp", "heads"), None),
            P(("dp", "heads"), None),
            P(("dp", "heads")),
            P(("dp", "heads"), None),
            P(("dp", "heads"), None),
            P(("dp", "heads"), None),
            P("dp", "heads"),
            P("dp", "heads"),
            P("dp", "heads"),
            P("dp", "heads"),
            P("dp", "heads"),
            P(("dp", "heads")),
            P(("dp", "heads"), None),
            P(("dp", "heads"), None),
            P(("dp", "heads"), None),
            P("dp", "heads"),
            P("dp", "heads"),
            P("dp", "heads"),
            P("dp", "heads"),
            P("dp", "heads"),
            P(("dp", "heads")),
            P(("dp", "heads"), None),
            P(("dp", "heads"), None),
            P(("dp", "heads"), None),
            P("dp", "heads"),
            P("dp", "heads"),
            P("dp", "heads"),
            P("dp", "heads"),
            P("dp", "heads"),
        ),
        check_vma=False,
    )
```

time: 731 us -> 549 us (0.75)
  waiting for transfers between devices: 262 us -> 177 us
  matrix products: 87.1 us -> 18.3 us
  Pallas kernels: 69.7 us -> 108 us
  local copies, waits for them, and re-layouts: 77.2 us -> 40 us
  between operations: 47.4 us -> 15.6 us
  starting transfers between devices: 120 us -> 148 us
  other arithmetic: 57.9 us -> 31.9 us
    ppermute x58 -> x48, waiting for transfers between devices: 159 us -> 93.5 us  [shift_heads(): return lax.ppermute(values, 'heads', pairs)]
    pallas_call x5 -> x13, Pallas kernels: 69.7 us -> 108 us  [the longest x1 22.2 us: shared_ortho(): kernel_call(shared_kernel, 'shared_ortho', (1,), 1, [fixed(piece.shape) f...]
    all_gather x1 -> x2, waiting for transfers between devices: 0.01 us -> 31.5 us  [the longest x1 31.5 us: on_device(): lax.all_gather(jnp.concatenate([latent_normed, key_local, value_local], a...]
    psum x1 -> x0, waiting for transfers between devices: 30.2 us -> none  [on_device(): ffn_gram = lax.psum(ffn_gram, 'dp').astype(jnp.float32)]
    dot_general x7 -> x3, matrix products: 32.3 us -> 4.05 us  [matmul(): return jnp.dot(left, right, preferred_element_type=jnp.float32)]
    ppermute x30 -> x36, waiting for transfers between devices: 71.8 us -> 46.6 us  [shift_dp(): return lax.ppermute(values, 'dp', pairs)]
    dot_general x39 -> x0, matrix products: 23.1 us -> none  [the longest x36 20.8 us: times(): jnp.einsum('brc,bcd->brd', left.astype(low_type), right.astype(low_type),...]
    dot_general x11 -> x5, matrix products: 26.3 us -> 6.72 us  [matmul_nt(): lax.dot_general(left, right, (((1,), (1,)), ((), ())), preferred_element_...]
  transfers between devices with their start and end apart: 91 -> 88, of which waited for: 42 -> 39; matrix products, arithmetic and copies ran while one was open for 20% -> 8% of each run, Pallas kernels for 6% -> 15%
where the time goes in v4:
time: 549 us; the launch traced here: 539 us
  waiting for transfers between devices  177 us (32%)
  starting transfers between devices  148 us (27%)
  Pallas kernels  108 us (20%)
  local copies, waits for them, and re-layouts  40 us (7%)
  other arithmetic  31.9 us (6%)
  matrix products  18.3 us (3%)
  between operations  15.6 us (3%)
    ppermute x48, starting transfers between devices, shift_heads(): return lax.ppermute(values, 'heads', pairs)  95.7 us
    ppermute x48, waiting for transfers between devices, shift_heads(): return lax.ppermute(values, 'heads', pairs)  93.5 us
    ppermute x36, starting transfers between devices, shift_dp(): return lax.ppermute(values, 'dp', pairs)  48.5 us
    ppermute x36, waiting for transfers between devices, shift_dp(): return lax.ppermute(values, 'dp', pairs)  46.6 us
    unnamed x228, local copies, waits for them, and re-layouts  32.7 us
    all_gather x1, waiting for transfers between devices, on_device(): lax.all_gather(jnp.concatenate([latent_normed, key_local, value_local], a...  31.5 us
    pallas_call x1, Pallas kernels, shared_ortho(): kernel_call(shared_kernel, 'shared_ortho', (1,), 1, [fixed(piece.shape) f...  22.2 us
    pallas_call x2, Pallas kernels, ffn_half(): kernel_call(ffn_kernel, 'ffn_far' if far else 'ffn_near', (1,), 1, [fixed...  21 us
  transfers between devices with their start and end apart: 88, of which 39 were waited for; matrix products, arithmetic and copies ran while one was open for 8% of the time, Pallas kernels for 15%

profile of v4, /device:TPU:1, one launch (start us, length us, event | category | flops | bytes accessed | tf_op | source)
XLA Modules:
  0.0 538.7 jit_solution(18276051436598656682)
XLA Ops:
  15.5 31.5 %all-gather.3.cloned.1.call-done.packed.refs_9_ = bf16[1024,1536]{1,0:T(8,128)(2,1)} async-done(((bf16[128,1536]{1,0:T(8,128)(2,1)}), bf16[1024,1536]{1,0:T(8,128)(2,1)}) %all-gather.3.cloned.1.call-update) | async-done | bytes 3145744 | tf_op jit(solution)/shard_map/all_gather | solution.py:920
  66.8 7.3 %attend.1 = (bf16[1024,512]{1,0:T(8,128)(2,1)S(1)}, bf16[512,512]{1,0:T(8,128)(2,1)S(1)}, bf16[512,512]{1,0:T(8,128)(2,1)S(1)}, f32[2,1024,1]{2,1,0:T(8,128)S(1)}) custom-call(s32[9]{0:T(128)S(1)} %pad_add_fusion.where, bf16[1024,1536]{1,0:T(8,128)(2,1)S(1)} %copy-done.58, bf16[1024,512]{1,0:T(8,128)(2,1)S(1)} %copy-done.33, ...), custom_call_target="tpu_custom_call" | custom-call | flops 3221225472 | bytes 4194304 | tf_op jit(solution)/shard_map/attend/pallas_call | solution.py:254
  85.8 11.5 %collective-permute-done.1 = bf16[128,2048]{1,0:T(8,128)(2,1)S(1)} collective-permute-done((bf16[128,2048]{1,0:T(8,128)(2,1)S(1)}, bf16[128,2048]{1,0:T(8,128)(2,1)S(1)}, u32[]{:S(2)}, u32[]{:S(2)}) %collective-permute-start.1) | collective-permute-done | bytes 524320 | tf_op jit(solution)/shard_map/ppermute | solution.py:92
  97.3 10.8 %collective-permute-done.2 = bf16[128,2048]{1,0:T(8,128)(2,1)S(1)} collective-permute-done((bf16[128,2048]{1,0:T(8,128)(2,1)S(1)}, bf16[128,2048]{1,0:T(8,128)(2,1)S(1)}, u32[]{:S(2)}, u32[]{:S(2)}) %collective-permute-start.2) | collective-permute-done | bytes 524320 | tf_op jit(solution)/shard_map/ppermute | solution.py:92
  115.8 8.1 %collective-permute-done.6.refs_3_ = bf16[128,2048]{1,0:T(8,128)(2,1)S(1)} collective-permute-done((bf16[128,2048]{1,0:T(8,128)(2,1)S(1)}, bf16[128,2048]{1,0:T(8,128)(2,1)S(1)}, u32[]{:S(2)}, u32[]{:S(2)}) %collective-permute-start.6) | collective-permute-done | bytes 524320 | tf_op jit(solution)/shard_map/ppermute | solution.py:92
  126.5 10.0 %collective-permute-start.8 = (bf16[128,2048]{1,0:T(8,128)(2,1)S(1)}, bf16[128,2048]{1,0:T(8,128)(2,1)S(1)}, u32[]{:S(2)}, u32[]{:S(2)}) collective-permute-start(bf16[128,2048]{1,0:T(8,128)(2,1)S(1)} %collective-permute-done.4.refs_1_), channel_id=1, source_target_pairs={{0,1},{1,0},{2,3},{3,2},{4,5},{5,4},{6,7},{7,6},{8,9},{9,8},{10,11... | collective-permute-start | bytes 1572872 | tf_op jit(solution)/shard_map/ppermute | solution.py:92
  152.2 10.5 %ffn_far.1 = (bf16[704,512]{1,0:T(8,128)(2,1)S(1)}, bf16[704,512]{1,0:T(8,128)(2,1)S(1)}, bf16[704,512]{1,0:T(8,128)(2,1)S(1)}, bf16[512,2048]{1,0:T(8,128)(2,1)S(1)}) custom-call(s32[8]{0:T(128)S(1)} %fusion.79.owner, bf16[128,2048]{1,0:T(8,128)(2,1)S(1)} %copy-done.22, bf16[128,2048]{1,0:T(8,128)(2,1)S(1)} %copy-done.26, bf16[128,2048]{1,0:T(8,128)(2,1)S(1)} %copy-done.28, ...), custom_call_target="tpu_custom_call" | custom-call | flops 7381975040 | bytes 14942208 | tf_op jit(solution)/shard_map/ffn_far/pallas_call | solution.py:435
  163.3 10.5 %ffn_near.1 = (bf16[704,512]{1,0:T(8,128)(2,1)S(1)}, bf16[704,512]{1,0:T(8,128)(2,1)S(1)}, bf16[704,512]{1,0:T(8,128)(2,1)S(1)}, bf16[512,2048]{1,0:T(8,128)(2,1)S(1)}) custom-call(s32[8]{0:T(128)S(1)} %fusion.79.owner, bf16[128,2048]{1,0:T(8,128)(2,1)S(1)} %copy-done.12, bf16[128,2048]{1,0:T(8,128)(2,1)S(1)} %copy-done.18, ...), custom_call_target="tpu_custom_call" | custom-call | flops 7381975040 | bytes 14942208 | tf_op jit(solution)/shard_map/ffn_near/pallas_call | solution.py:435
  176.0 12.9 %ffn_grads.1 = bf16[16,2112,128]{2,1,0:T(8,128)(2,1)S(1)} custom-call(s32[8]{0:T(128)S(1)} %fusion.79.owner, bf16[128,2048]{1,0:T(8,128)(2,1)S(1)} %copy-done.12, bf16[128,2048]{1,0:T(8,128)(2,1)S(1)} %copy-done.18, bf16[128,2048]{1,0:T(8,128)(2,1)S(1)} %copy-done.20, bf16[128,2048]{1,0:T(8,128)(2,1)S(1)} %copy-done.16, bf16[128,2048]{1,0:T(8,128)(2,1)S(1)} %copy-done.22, ...), custom_call_target="tpu_custom_call" | custom-call | flops 8858370048 | bytes 17039360 | tf_op jit(solution)/shard_map/ffn_grads/pallas_call | solution.py:472
  209.2 12.5 %collective-permute-done.13 = bf16[128,2048]{1,0:T(8,128)(2,1)S(1)} collective-permute-done((bf16[128,2048]{1,0:T(8,128)(2,1)S(1)}, bf16[128,2048]{1,0:T(8,128)(2,1)S(1)}, u32[]{:S(2)}, u32[]{:S(2)}) %collective-permute-start.13) | collective-permute-done | bytes 524320 | tf_op jit(solution)/shard_map/ppermute | solution.py:92
  227.6 10.2 %collective-permute-done.15.refs_1_ = bf16[128,2048]{1,0:T(8,128)(2,1)S(1)} collective-permute-done((bf16[128,2048]{1,0:T(8,128)(2,1)S(1)}, bf16[128,2048]{1,0:T(8,128)(2,1)S(1)}, u32[]{:S(2)}, u32[]{:S(2)}) %collective-permute-start.15) | collective-permute-done | bytes 524320 | tf_op jit(solution)/shard_map/ppermute | solution.py:92
  237.8 11.6 %collective-permute-start.19 = (bf16[128,2048]{1,0:T(8,128)(2,1)S(1)}, bf16[128,2048]{1,0:T(8,128)(2,1)S(1)}, u32[]{:S(2)}, u32[]{:S(2)}) collective-permute-start(bf16[128,2048]{1,0:T(8,128)(2,1)S(1)} %collective-permute-done.15.refs_1_), channel_id=1, source_target_pairs={{0,1},{1,0},{2,3},{3,2},{4,5},{5,4},{6,7},{7,6},{8,9},{9,8},{10,11... | collective-permute-start | bytes 1572872 | tf_op jit(solution)/shard_map/ppermute | solution.py:92
  254.6 14.0 %attend_back.1 = (bf16[1024,512]{1,0:T(8,128)(2,1)S(1)}, bf16[512,1536]{1,0:T(8,128)(2,1)S(1)}, bf16[512,1536]{1,0:T(8,128)(2,1)}) custom-call(s32[9]{0:T(128)S(1)} %pad_add_fusion.where, bf16[128,2048]{1,0:T(8,128)(2,1)S(1)} %get-tuple-element.123.refs_0_, bf16[128,2048]{1,0:T(8,128)(2,1)S(1)} %collective-permute-done.15.refs_1_, ...), custom_call_target="tpu_custom_call" | custom-call | flops 9663676416 | bytes 4194304 | tf_op jit(solution)/shard_map/attend_back/pallas_call | solution.py:349
  300.8 6.0 %collective-permute-done.24 = bf16[128,1536]{1,0:T(8,128)(2,1)S(1)} collective-permute-done((bf16[128,1536]{1,0:T(8,128)(2,1)S(1)}, bf16[128,1536]{1,0:T(8,128)(2,1)S(1)}, u32[]{:S(2)}, u32[]{:S(2)}) %collective-permute-start.24) | collective-permute-done | bytes 393248 | tf_op jit(solution)/shard_map/ppermute | solution.py:92
  335.5 8.2 %collective-permute-start.32 = (bf16[128,1536]{1,0:T(8,128)(2,1)}, bf16[128,1536]{1,0:T(8,128)(2,1)S(1)}, u32[]{:S(2)}, u32[]{:S(2)}) collective-permute-start(bf16[128,1536]{1,0:T(8,128)(2,1)} %pad_maximum_fusion.1.refs_8_), channel_id=1, source_target_pairs={{0,1},{1,0},{2,3},{3,2},{4,5},{5,4},{6,7},{7,6},{8,9},{9,8},{10,11... | collective-permute-start | bytes 1179656 | tf_op jit(solution)/shard_map/ppermute | solution.py:92
  346.7 15.0 %collective-permute-start.34 = (bf16[128,1536]{1,0:T(8,128)(2,1)}, bf16[128,1536]{1,0:T(8,128)(2,1)S(1)}, u32[]{:S(2)}, u32[]{:S(2)}) collective-permute-start(bf16[128,1536]{1,0:T(8,128)(2,1)} %collective-permute-done.30.refs_10_), channel_id=1, source_target_pairs={{0,1},{1,0},{2,3},{3,2},{4,5},{5,4},{6,7},{7,6},{8,9},{9,8},{10,11... | collective-permute-start | bytes 1179656 | tf_op jit(solution)/shard_map/ppermute | solution.py:92
  391.8 6.0 %collective-permute-start.56 = (bf16[1152,128]{1,0:T(8,128)(2,1)S(1)}, bf16[1152,128]{1,0:T(8,128)(2,1)S(1)}, u32[]{:S(2)}, u32[]{:S(2)}) collective-permute-start(bf16[1152,128]{1,0:T(8,128)(2,1)S(1)} %constant_dynamic-update-slice_fusion.refs_0_), channel_id=1, source_target_pairs={{0,96},{8,104},{16,112},{24,120},{32,0},{40,8},{48,16},{56,24},{64... | collective-permute-start | bytes 884744 | tf_op jit(solution)/shard_map/ppermute | solution.py:101
  419.5 9.1 %collective-permute-start.64 = (bf16[1600,256]{1,0:T(8,128)(2,1)S(1)}, bf16[1600,256]{1,0:T(8,128)(2,1)S(1)}, u32[]{:S(2)}, u32[]{:S(2)}) collective-permute-start(bf16[1600,256]{1,0:T(8,128)(2,1)S(1)} %get-tuple-element.151), channel_id=1, source_target_pairs={{0,1},{1,0},{2,3},{3,2},{4,5},{5,4},{6,7},{7,6},{8,9},{9,8},{10,11... | collective-permute-start | bytes 2457608 | tf_op jit(solution)/shard_map/ppermute | solution.py:92
  431.2 13.5 %ffn_updates.1 = (f32[704,128]{1,0:T(8,128)}, f32[704,128]{1,0:T(8,128)}, f32[704,128]{1,0:T(8,128)}) custom-call(s32[17]{0:T(128)S(1)} %pad_add_fusion.1.origin, bf16[1152,128]{1,0:T(8,128)(2,1)S(1)} %constant_dynamic-update-slice_fusion.refs_0_, bf16[1152,128]{1,0:T(8,128)(2,1)S(1)} %collective-permute-done.54.refs_1_, ...), custom_call_target="tpu_custom_call" | custom-call | flops 2906652672 | bytes 3244032 | tf_op jit(solution)/shard_map/ffn_updates/pallas_call | solution.py:703
  448.9 7.2 %collective-permute-done.78 = bf16[1536,128]{1,0:T(8,128)(2,1)S(1)} collective-permute-done((bf16[1536,128]{1,0:T(8,128)(2,1)S(1)}, bf16[1536,128]{1,0:T(8,128)(2,1)S(1)}, u32[]{:S(2)}, u32[]{:S(2)}) %collective-permute-start.78) | collective-permute-done | bytes 393248 | tf_op jit(solution)/shard_map/ppermute | solution.py:101
  456.2 9.0 %collective-permute-done.79 = bf16[1536,128]{1,0:T(8,128)(2,1)S(1)} collective-permute-done((bf16[1536,128]{1,0:T(8,128)(2,1)S(1)}, bf16[1536,128]{1,0:T(8,128)(2,1)S(1)}, u32[]{:S(2)}, u32[]{:S(2)}) %collective-permute-start.79) | collective-permute-done | bytes 393248 | tf_op jit(solution)/shard_map/ppermute | solution.py:101
  476.0 9.1 %collective-permute-done.82 = bf16[1536,128]{1,0:T(8,128)(2,1)S(1)} collective-permute-done((bf16[1536,128]{1,0:T(8,128)(2,1)S(1)}, bf16[1536,128]{1,0:T(8,128)(2,1)S(1)}, u32[]{:S(2)}, u32[]{:S(2)}) %collective-permute-start.82) | collective-permute-done | bytes 393248 | tf_op jit(solution)/shard_map/ppermute | solution.py:101
  499.6 22.2 %shared_ortho.1 = f32[16,1536]{1,0:T(8,128)S(1)} custom-call(s32[8]{0:T(128)S(1)} %fusion.79.owner, bf16[384,256]{1,0:T(8,128)(2,1)S(1)} %slice.234.refs_0_, bf16[384,256]{1,0:T(8,128)(2,1)S(1)} %collective-permute-done.68.refs_1_, bf16[384,256]{1,0:T(8,128)(2,1)S(1)} %collective-permute-done.69.refs_2_, ...), custom_call_target="tpu_custom_call" | custom-call | flops 21474836480 | bytes 8388608 | tf_op jit(solution)/shard_map/shared_ortho/pallas_call | solution.py:834
  521.8 6.0 %head_updates.1 = (f32[64,512]{1,0:T(8,128)}, f32[128,512]{1,0:T(8,128)}) custom-call(s32[17]{0:T(128)S(1)} %pad_add_fusion.1.origin, bf16[1536,128]{1,0:T(8,128)(2,1)S(1)} %add_convert_fusion.5.refs_0_, f32[64,512]{1,0:T(8,128)S(1)} %copy-done.56, f32[128,512]{1,0:T(8,128)S(1)} %copy-done.55, bf16[1024,512]{1,0:T(8,128)(2,1)S(1)} %copy-done.35, ...), custom_call_target="tpu_custom_call" | custom-call | flops 704643072 | bytes 1179648 | tf_op jit(solution)/shard_map/head_updates/pallas_call | solution.py:703
  (487 shorter events, 250.3 us)
Async XLA Ops:
  7.2 39.8 %all-gather.3.cloned.1.call-start = ((), (), s32[]{:S(2)}) async-start(), calls=%async_computation.2 | async-start | bytes 3538944 | tf_op jit(solution)/shard_map/all_gather | solution.py:920
  15.5 126.7 %all-gather.5.cloned.1.call-start = ((), (), s32[]{:S(2)}) async-start(), calls=%async_computation.3 | async-start | bytes 4718592 | tf_op jit(solution)/shard_map/all_gather | solution.py:923
  52.0 226.2 %reduce-scatter.4.cloned.1.call-start = ((), (), s32[]{:S(2)}) async-start(), calls=%async_computation.4 | async-start | bytes 9191424
  83.3 24.8 %collective-permute-start.2 = (bf16[128,2048]{1,0:T(8,128)(2,1)S(1)}, bf16[128,2048]{1,0:T(8,128)(2,1)S(1)}, u32[]{:S(2)}, u32[]{:S(2)}) collective-permute-start(bf16[128,2048]{1,0:T(8,128)(2,1)S(1)} %get-tuple-element.219), channel_id=1, source_target_pairs={{0,4},{1,5},{2,6},{3,7},{4,0},{5,1},{6,2},{7,3},{8,12},{9,13},{10,... | collective-permute-start | bytes 1572872 | tf_op jit(solution)/shard_map/ppermute | solution.py:92
  85.1 23.4 %collective-permute-start.3 = (bf16[128,2048]{1,0:T(8,128)(2,1)S(1)}, bf16[128,2048]{1,0:T(8,128)(2,1)S(1)}, u32[]{:S(2)}, u32[]{:S(2)}) collective-permute-start(bf16[128,2048]{1,0:T(8,128)(2,1)S(1)} %get-tuple-element.218), channel_id=1, source_target_pairs={{0,6},{1,7},{2,0},{3,1},{4,2},{5,3},{6,4},{7,5},{8,14},{9,15},{10,... | collective-permute-start | bytes 1572872 | tf_op jit(solution)/shard_map/ppermute | solution.py:92
  112.9 24.4 %collective-permute-start.5 = (bf16[128,2048]{1,0:T(8,128)(2,1)S(1)}, bf16[128,2048]{1,0:T(8,128)(2,1)S(1)}, u32[]{:S(2)}, u32[]{:S(2)}) collective-permute-start(bf16[128,2048]{1,0:T(8,128)(2,1)S(1)} %multiply_convert_fusion.refs_0_), channel_id=1, source_target_pairs={{0,4},{1,5},{2,6},{3,7},{4,0},{5,1},{6,2},{7,3},{8,12},{9,13},{10,... | collective-permute-start | bytes 1572872 | tf_op jit(solution)/shard_map/ppermute | solution.py:92
  114.0 25.0 %collective-permute-start.7 = (bf16[128,2048]{1,0:T(8,128)(2,1)S(1)}, bf16[128,2048]{1,0:T(8,128)(2,1)S(1)}, u32[]{:S(2)}, u32[]{:S(2)}) collective-permute-start(bf16[128,2048]{1,0:T(8,128)(2,1)S(1)} %multiply_convert_fusion.refs_0_), channel_id=1, source_target_pairs={{0,1},{1,0},{2,3},{3,2},{4,5},{5,4},{6,7},{7,6},{8,9},{9,8},{10,11... | collective-permute-start | bytes 1572872 | tf_op jit(solution)/shard_map/ppermute | solution.py:92
  195.0 26.6 %collective-permute-start.13 = (bf16[128,2048]{1,0:T(8,128)(2,1)S(1)}, bf16[128,2048]{1,0:T(8,128)(2,1)S(1)}, u32[]{:S(2)}, u32[]{:S(2)}) collective-permute-start(bf16[128,2048]{1,0:T(8,128)(2,1)S(1)} %get-tuple-element.216), channel_id=1, source_target_pairs={{0,4},{1,5},{2,6},{3,7},{4,0},{5,1},{6,2},{7,3},{8,12},{9,13},{10,... | collective-permute-start | bytes 1572872 | tf_op jit(solution)/shard_map/ppermute | solution.py:92
  198.4 23.3 %collective-permute-start.14 = (bf16[128,2048]{1,0:T(8,128)(2,1)S(1)}, bf16[128,2048]{1,0:T(8,128)(2,1)S(1)}, u32[]{:S(2)}, u32[]{:S(2)}) collective-permute-start(bf16[128,2048]{1,0:T(8,128)(2,1)S(1)} %get-tuple-element.215), channel_id=1, source_target_pairs={{0,6},{1,7},{2,0},{3,1},{4,2},{5,3},{6,4},{7,5},{8,14},{9,15},{10,... | collective-permute-start | bytes 1572872 | tf_op jit(solution)/shard_map/ppermute | solution.py:92
  226.0 23.4 %collective-permute-start.16 = (bf16[128,2048]{1,0:T(8,128)(2,1)S(1)}, bf16[128,2048]{1,0:T(8,128)(2,1)S(1)}, u32[]{:S(2)}, u32[]{:S(2)}) collective-permute-start(bf16[128,2048]{1,0:T(8,128)(2,1)S(1)} %get-tuple-element.123.refs_0_), channel_id=1, source_target_pairs={{0,4},{1,5},{2,6},{3,7},{4,0},{5,1},{6,2},{7,3},{8,12},{9,13},{10,... | collective-permute-start | bytes 1572872 | tf_op jit(solution)/shard_map/ppermute | solution.py:92
  226.0 26.0 %collective-permute-start.17 = (bf16[128,2048]{1,0:T(8,128)(2,1)S(1)}, bf16[128,2048]{1,0:T(8,128)(2,1)S(1)}, u32[]{:S(2)}, u32[]{:S(2)}) collective-permute-start(bf16[128,2048]{1,0:T(8,128)(2,1)S(1)} %get-tuple-element.123.refs_0_), channel_id=1, source_target_pairs={{0,2},{1,3},{2,4},{3,5},{4,6},{5,7},{6,0},{7,1},{8,10},{9,11},{10,... | collective-permute-start | bytes 1572872 | tf_op jit(solution)/shard_map/ppermute | solution.py:92
  226.6 26.4 %collective-permute-start.18 = (bf16[128,2048]{1,0:T(8,128)(2,1)S(1)}, bf16[128,2048]{1,0:T(8,128)(2,1)S(1)}, u32[]{:S(2)}, u32[]{:S(2)}) collective-permute-start(bf16[128,2048]{1,0:T(8,128)(2,1)S(1)} %get-tuple-element.123.refs_0_), channel_id=1, source_target_pairs={{0,1},{1,0},{2,3},{3,2},{4,5},{5,4},{6,7},{7,6},{8,9},{9,8},{10,11... | collective-permute-start | bytes 1572872 | tf_op jit(solution)/shard_map/ppermute | solution.py:92
  323.4 23.3 %collective-permute-start.36 = (bf16[4,192,512]{2,1,0:T(8,128)(2,1)}, bf16[4,192,512]{2,1,0:T(8,128)(2,1)}, u32[]{:S(2)}, u32[]{:S(2)}) collective-permute-start(bf16[4,192,512]{2,1,0:T(8,128)(2,1)} %get-tuple-element.208), channel_id=1, source_target_pairs={{0,8},{8,16},{16,24},{24,0},{32,40},{40,48},{48,56},{56,32},{64,72... | collective-permute-start | bytes 2359304 | tf_op jit(solution)/shard_map/ppermute | solution.py:101
  323.7 38.0 %collective-permute-start.37 = (bf16[4,192,512]{2,1,0:T(8,128)(2,1)}, bf16[4,192,512]{2,1,0:T(8,128)(2,1)}, u32[]{:S(2)}, u32[]{:S(2)}) collective-permute-start(bf16[4,192,512]{2,1,0:T(8,128)(2,1)} %get-tuple-element.209), channel_id=1, source_target_pairs={{0,16},{8,24},{16,0},{24,8},{32,48},{40,56},{48,32},{56,40},{64,80... | collective-permute-start | bytes 2359304 | tf_op jit(solution)/shard_map/ppermute | solution.py:101
  325.2 20.9 %collective-permute-start.31 = (bf16[128,1536]{1,0:T(8,128)(2,1)}, bf16[128,1536]{1,0:T(8,128)(2,1)}, u32[]{:S(2)}, u32[]{:S(2)}) collective-permute-start(bf16[128,1536]{1,0:T(8,128)(2,1)} %pad_maximum_fusion.1.refs_8_), channel_id=1, source_target_pairs={{0,2},{1,3},{2,4},{3,5},{4,6},{5,7},{6,0},{7,1},{8,10},{9,11},{10,... | collective-permute-start | bytes 1179656 | tf_op jit(solution)/shard_map/ppermute | solution.py:92
  331.7 31.0 %collective-permute-start.38 = (bf16[4,192,512]{2,1,0:T(8,128)(2,1)}, bf16[4,192,512]{2,1,0:T(8,128)(2,1)}, u32[]{:S(2)}, u32[]{:S(2)}) collective-permute-start(bf16[4,192,512]{2,1,0:T(8,128)(2,1)} %get-tuple-element.210), channel_id=1, source_target_pairs={{0,24},{8,0},{16,8},{24,16},{32,56},{40,32},{48,40},{56,48},{64,88... | collective-permute-start | bytes 2359304 | tf_op jit(solution)/shard_map/ppermute | solution.py:101
  335.5 29.5 %collective-permute-start.32 = (bf16[128,1536]{1,0:T(8,128)(2,1)}, bf16[128,1536]{1,0:T(8,128)(2,1)S(1)}, u32[]{:S(2)}, u32[]{:S(2)}) collective-permute-start(bf16[128,1536]{1,0:T(8,128)(2,1)} %pad_maximum_fusion.1.refs_8_), channel_id=1, source_target_pairs={{0,1},{1,0},{2,3},{3,2},{4,5},{5,4},{6,7},{7,6},{8,9},{9,8},{10,11... | collective-permute-start | bytes 1179656 | tf_op jit(solution)/shard_map/ppermute | solution.py:92
  419.5 28.8 %collective-permute-start.64 = (bf16[1600,256]{1,0:T(8,128)(2,1)S(1)}, bf16[1600,256]{1,0:T(8,128)(2,1)S(1)}, u32[]{:S(2)}, u32[]{:S(2)}) collective-permute-start(bf16[1600,256]{1,0:T(8,128)(2,1)S(1)} %get-tuple-element.151), channel_id=1, source_target_pairs={{0,1},{1,0},{2,3},{3,2},{4,5},{5,4},{6,7},{7,6},{8,9},{9,8},{10,11... | collective-permute-start | bytes 2457608 | tf_op jit(solution)/shard_map/ppermute | solution.py:92
  430.1 65.4 %collective-permute-start.57 = (bf16[512,2048]{1,0:T(8,128)(2,1)S(1)}, bf16[512,2048]{1,0:T(8,128)(2,1)S(1)}, u32[]{:S(2)}, u32[]{:S(2)}) collective-permute-start(bf16[512,2048]{1,0:T(8,128)(2,1)S(1)} %copy-done.111), channel_id=1, source_target_pairs={{0,1},{1,0},{2,3},{3,2},{4,5},{5,4},{6,7},{7,6},{8,9},{9,8},{10,11... | collective-permute-start | bytes 6291464 | tf_op jit(solution)/shard_map/ppermute | solution.py:92
  448.6 20.2 %collective-permute-start.65 = (bf16[400,256]{1,0:T(8,128)(2,1)S(1)}, bf16[400,256]{1,0:T(8,128)(2,1)S(1)}, u32[]{:S(2)}, u32[]{:S(2)}) collective-permute-start(bf16[400,256]{1,0:T(8,128)(2,1)S(1)} %get-tuple-element.229), channel_id=1, source_target_pairs={{0,2},{1,3},{2,4},{3,5},{4,6},{5,7},{6,0},{7,1},{8,10},{9,11},{10,... | collective-permute-start | bytes 614408 | tf_op jit(solution)/shard_map/ppermute | solution.py:92
  465.5 19.6 %collective-permute-start.82 = (bf16[1536,128]{1,0:T(8,128)(2,1)S(1)}, bf16[1536,128]{1,0:T(8,128)(2,1)S(1)}, u32[]{:S(2)}, u32[]{:S(2)}) collective-permute-start(bf16[1536,128]{1,0:T(8,128)(2,1)S(1)} %add_convert_fusion.6), channel_id=1, source_target_pairs={{0,64},{8,72},{16,80},{24,88},{32,96},{40,104},{48,112},{56,120},{... | collective-permute-start | bytes 1179656 | tf_op jit(solution)/shard_map/ppermute | solution.py:101
  496.5 34.1 %collective-permute-start.75 = (bf16[128,2048]{1,0:T(8,128)(2,1)S(1)}, bf16[128,2048]{1,0:T(8,128)(2,1)S(1)}, u32[]{:S(2)}, u32[]{:S(2)}) collective-permute-start(bf16[128,2048]{1,0:T(8,128)(2,1)S(1)} %get-tuple-element.211), channel_id=1, source_target_pairs={{0,2},{1,3},{2,4},{3,5},{4,6},{5,7},{6,0},{7,1},{8,10},{9,11},{10,... | collective-permute-start | bytes 1572872 | tf_op jit(solution)/shard_map/ppermute | solution.py:92
  496.6 34.0 %collective-permute-start.76 = (bf16[128,2048]{1,0:T(8,128)(2,1)S(1)}, bf16[128,2048]{1,0:T(8,128)(2,1)S(1)}, u32[]{:S(2)}, u32[]{:S(2)}) collective-permute-start(bf16[128,2048]{1,0:T(8,128)(2,1)S(1)} %get-tuple-element.213), channel_id=1, source_target_pairs={{0,4},{1,5},{2,6},{3,7},{4,0},{5,1},{6,2},{7,3},{8,12},{9,13},{10,... | collective-permute-start | bytes 1572872 | tf_op jit(solution)/shard_map/ppermute | solution.py:92
  497.0 33.5 %collective-permute-start.77 = (bf16[128,2048]{1,0:T(8,128)(2,1)S(1)}, bf16[128,2048]{1,0:T(8,128)(2,1)S(1)}, u32[]{:S(2)}, u32[]{:S(2)}) collective-permute-start(bf16[128,2048]{1,0:T(8,128)(2,1)S(1)} %get-tuple-element.212), channel_id=1, source_target_pairs={{0,6},{1,7},{2,0},{3,1},{4,2},{5,3},{6,4},{7,5},{8,14},{9,15},{10,... | collective-permute-start | bytes 1572872 | tf_op jit(solution)/shard_map/ppermute | solution.py:92
  (176 other events, 2511.3 us)
Sparse Core Ops, SparseCore 0:
  15.6 31.3 all-gather.2
  48.7 33.0 all-gather.4
  192.5 84.7 reduce-scatter.3

commit v5 on v4

v5 whole, which is shorter than its diff:
```python
import math

import jax
import jax.numpy as jnp
from jax import lax
from jax.experimental import pallas as pl
from jax.experimental.pallas import tpu as pltpu
from jax.sharding import PartitionSpec as P

NS_STEPS = 3
FF_BLOCK = 352
SIDE = 4
CORES = 2
LANES = 128

coef_first = 3.4445
coef_second = -4.775
coef_third = 2.0315
muon_rate = 0.5
gain_rate = 0.004
decay_rate = 0.5
low_type = jnp.bfloat16


def matmul(left, right):
    return jnp.dot(left, right, preferred_element_type=jnp.float32)


def matmul_nt(left, right):
    return lax.dot_general(
        left, right, (((1,), (1,)), ((), ())), preferred_element_type=jnp.float32
    )


def matmul_tn(left, right):
    return lax.dot_general(
        left, right, (((0,), (0,)), ((), ())), preferred_element_type=jnp.float32
    )


def rms_scale(values):
    return lax.rsqrt(jnp.mean(values * values, axis=-1, keepdims=True) + 1e-05)


def norm_back(values, scale, gain, grad_out):
    weighted = gain * grad_out
    inner = jnp.mean(values * weighted, axis=-1, keepdims=True)
    grad_in = scale * weighted - values * (scale * scale * scale) * inner
    gain_grad = jnp.sum(grad_out * values * scale, axis=0)
    return (grad_in, gain_grad)


def segment_info(starts, token_index):
    started = starts[None, :] <= token_index[:, None]
    seg_ids = jnp.sum(started.astype(jnp.int32), axis=1)
    seg_begin = jnp.max(jnp.where(started, starts[None, :], 0), axis=1)
    return (seg_ids, token_index - seg_begin)


def rotary_tables(positions, head_dim):
    half_dim = head_dim // 2
    frequency = jnp.exp(
        jnp.arange(half_dim, dtype=jnp.float32) * (-2.0 * math.log(10000.0) / head_dim)
    )
    angles = positions.astype(jnp.float32)[:, None] * frequency[None, :]
    return (jnp.cos(angles), jnp.sin(angles))


def rotate(values, cosine, sine_part):
    half_dim = values.shape[-1] // 2
    first_half = values[..., :half_dim]
    second_half = values[..., half_dim:]
    return jnp.concatenate(
        [
            first_half * cosine - second_half * sine_part,
            second_half * cosine + first_half * sine_part,
        ],
        axis=-1,
    )


def rotate_back(grads, cosine, sine_part):
    return rotate(grads, cosine, -sine_part)


def shift_heads(values, step, core):
    pairs = [
        (CORES * place + side, CORES * ((place + step) % SIDE) + (side ^ core))
        for place in range(SIDE)
        for side in range(CORES)
    ]
    return lax.ppermute(values, "heads", pairs)


def shift_dp(values, step_z, step_x):
    pairs = [
        (SIDE * z + x, SIDE * ((z + step_z) % SIDE) + (x + step_x) % SIDE)
        for z in range(SIDE)
        for x in range(SIDE)
    ]
    return lax.ppermute(values, "dp", pairs)


def gather_heads(own, beside=()):
    ring = [own] + [shift_heads(own, -step, 0) for step in range(1, SIDE)]
    ring, beside = lax.optimization_barrier((ring, beside))
    pieces = ring + [shift_heads(piece, 0, 1) for piece in ring]
    return (pieces, *beside) if beside else pieces


def chip_sums(far_half, near_half):
    rows = near_half.shape[0] // SIDE
    total = near_half.astype(jnp.float32) + shift_heads(far_half, 0, 1).astype(jnp.float32)
    return total.astype(far_half.dtype).reshape(SIDE, rows, *near_half.shape[1:])


def ring_operands(chip):
    return lax.optimization_barrier([chip[step] for step in range(SIDE)])


def ring_sums(operands):
    total = operands[0].astype(jnp.float32)
    for step in range(1, SIDE):
        total = total + shift_heads(operands[step], step, 0).astype(jnp.float32)
    return total


def pick(array, place, axis):
    return lax.dynamic_index_in_dim(array, place % SIDE, axis, keepdims=False)


def scatter_x(parts):
    place_x = lax.axis_index("dp") % SIDE
    grid = parts.reshape(SIDE, SIDE, *parts.shape[1:])
    total = pick(grid, place_x, 1).astype(jnp.float32)
    for step in range(1, SIDE):
        total = total + shift_dp(pick(grid, place_x + step, 1), 0, step).astype(jnp.float32)
    return total.astype(parts.dtype)


def scatter_z(column):
    place_z = lax.axis_index("dp") // SIDE
    total = pick(column, place_z, 0).astype(jnp.float32)
    for step in range(1, SIDE):
        total = total + shift_dp(pick(column, place_z + step, 0), step, 0).astype(jnp.float32)
    return total


def line_sum(part, axis):
    total = part.astype(jnp.float32)
    for step in range(1, SIDE):
        total = total + shift_dp(part, step * axis, step * (1 - axis)).astype(jnp.float32)
    return total.astype(part.dtype)


def exchange_dp(parts):
    return lax.all_to_all(parts, "dp", split_axis=0, concat_axis=0, tiled=True)


def after(values, *earlier):
    return lax.optimization_barrier((values, *earlier))[0]


vmem_mib = {
    "attend": 14,
    "attend_back": 20,
    "ffn_near": 26,
    "ffn_far": 26,
    "ffn_grads": 32,
    "head_grads": 16,
    "shared_updates": 24,
    "block_updates": 28,
}


def in_hbm(array):
    return pltpu.with_memory_space_constraint(array, pltpu.HBM)


def streamed_call(
    body, name, scalars, resident, arrays, out_shape, scratch, flops, moved, cuts, merged
):
    kinds, pieces = [], []
    for index, array in enumerate(arrays):
        rows = array.shape[0] if index not in cuts else cuts[index][0]
        if index < merged:
            rows = merged * array.shape[0] if index == 0 else 16
        kinds.append(pltpu.VMEM((rows, *array.shape[1:]), array.dtype))
        pieces.append(1 if index not in cuts else cuts[index][1])
    count, outs = len(arrays), len(out_shape)

    def wrapped(*refs):
        numbers, refs = refs[: len(scalars)], refs[len(scalars) :]
        still, refs = refs[: len(resident)], refs[len(resident) :]
        sources, refs = refs[:count], refs[count:]
        targets, refs = refs[:outs], refs[outs:]
        held, sems, rest = refs[:count], refs[count], refs[count + 1 :]
        copies, place = [], 0
        for index, source in enumerate(sources):
            parts = [(source, held[index])]
            if index < merged:
                rows = source.shape[0]
                parts = [(source, held[0].at[index * rows : (index + 1) * rows, :])]
            if index in cuts:
                parts = cuts[index][2](numbers, source, held[index])
            group = []
            for part_from, part_to in parts:
                group.append(pltpu.make_async_copy(part_from, part_to, sems.at[place]))
                place += 1
            copies.append(group)
        for group in copies:
            for copy in group:
                copy.start()
        done = [0]

        def ready(index):
            while done[0] <= index:
                for copy in copies[done[0]]:
                    copy.wait()
                done[0] += 1

        body(ready, numbers, still, held, targets, rest)
        ready(count - 1)

    return pl.pallas_call(
        wrapped,
        grid_spec=pltpu.PrefetchScalarGridSpec(
            num_scalar_prefetch=len(scalars),
            grid=(1,),
            in_specs=[pl.BlockSpec(memory_space=pltpu.VMEM)] * len(resident)
            + [pl.BlockSpec(memory_space=pltpu.HBM)] * count,
            out_specs=[pl.BlockSpec(memory_space=pltpu.VMEM)] * outs,
            scratch_shapes=[*kinds, pltpu.SemaphoreType.DMA((sum(pieces),)), *scratch],
        ),
        out_shape=out_shape,
        compiler_params=pltpu.CompilerParams(
            vmem_limit_bytes=vmem_mib.get(name, 12) * 1024 * 1024
        ),
        cost_estimate=pl.CostEstimate(flops=flops, bytes_accessed=moved, transcendentals=0),
        name=name,
    )(*scalars, *resident, *[in_hbm(array) for array in arrays])


def whole_call(body, name, scalars, arrays, out_shape, scratch, flops, moved):
    return pl.pallas_call(
        body,
        in_specs=[pl.BlockSpec(memory_space=pltpu.SMEM)] * len(scalars)
        + [pl.BlockSpec(memory_space=pltpu.VMEM)] * len(arrays),
        out_specs=jax.tree.map(lambda _: pl.BlockSpec(memory_space=pltpu.VMEM), out_shape),
        out_shape=out_shape,
        scratch_shapes=scratch,
        compiler_params=pltpu.CompilerParams(
            vmem_limit_bytes=vmem_mib.get(name, 12) * 1024 * 1024
        ),
        cost_estimate=pl.CostEstimate(flops=flops, bytes_accessed=moved, transcendentals=0),
        name=name,
    )(*scalars, *arrays)


def kernel_call(body, name, grid, prefetch, in_specs, out_specs, out_shape, scratch, flops, moved):
    return pl.pallas_call(
        body,
        grid_spec=pltpu.PrefetchScalarGridSpec(
            num_scalar_prefetch=prefetch,
            grid=grid,
            in_specs=in_specs,
            out_specs=out_specs,
            scratch_shapes=scratch,
        ),
        out_shape=out_shape,
        compiler_params=pltpu.CompilerParams(vmem_limit_bytes=vmem_mib.get(name, 12) * 1024 * 1024),
        cost_estimate=pl.CostEstimate(flops=flops, bytes_accessed=moved, transcendentals=0),
        name=name,
    )


def shaped(shape, kind):
    return jax.ShapeDtypeStruct(shape, kind)


def fixed(shape):
    return pl.BlockSpec(
        shape, lambda *grid: (0,) * len(shape), pipeline_mode=pl.Buffered(buffer_count=1)
    )


def visible(ids_q, ids_k, first_row, rows, cols):
    query_at = first_row + lax.broadcasted_iota(jnp.int32, (rows, cols), 0)
    key_at = lax.broadcasted_iota(jnp.int32, (rows, cols), 1)
    return (ids_q == ids_k) & (key_at <= query_at)


def block_at(index, piece):
    return pl.ds(pl.multiple_of(index * piece, piece), piece)


def store_by_distance(where, rows_ref, near_ref, far_ref, piece):
    core = where[SIDE * CORES]
    for step in range(SIDE):
        near = CORES * step + core
        far = CORES * step + 1 - core
        near_ref[block_at(where[near], piece), :] = rows_ref[block_at(near, piece), :].astype(
            near_ref.dtype
        )
        far_ref[block_at(where[far] - SIDE, piece), :] = rows_ref[block_at(far, piece), :].astype(
            far_ref.dtype
        )


def attend_kernel(
    where, packed, w_q_up, cosine, sine, ids_q, ids_k, query_out, near_out, far_out, lse_out, mixed
):
    row_len, packed_width = packed.shape
    latent_width, width = w_q_up.shape
    head_dim = (packed_width - latent_width) // 2
    piece = row_len // (SIDE * CORES)
    block = CORES * piece
    scale = head_dim ** (-0.5)
    key_cols = slice(latent_width, latent_width + head_dim)
    value_cols = slice(latent_width + head_dim, latent_width + 2 * head_dim)
    for head in range(width // head_dim):
        cols = slice(head * head_dim, (head + 1) * head_dim)
        for index in range(SIDE):
            first = index * block
            end = first + block
            rows = slice(first, end)
            query = matmul(packed[rows, :latent_width], w_q_up[:, cols])
            query = rotate(query, cosine[rows, :], sine[rows, :]).astype(low_type)
            query_out[rows, cols] = query
            scores = matmul_nt(query, packed[:end, key_cols]) * scale
            allowed = visible(ids_q[rows, :], ids_k[:, :end], first, block, end)
            scores = jnp.where(allowed, scores, -1e30)
            row_max = jnp.max(scores, axis=-1, keepdims=True)
            exponent = jnp.exp(scores - row_max)
            row_total = jnp.sum(exponent, axis=-1, keepdims=True)
            probs = (exponent * (1.0 / row_total)).astype(low_type)
            lse_out[head, rows, :] = row_max + jnp.log(row_total)
            mixed[rows, cols] = matmul(probs, packed[:end, value_cols]).astype(low_type)
    store_by_distance(where, mixed, near_out, far_out, piece)


def attend(where, packed, w_q_up, head_dim, cosine, sine, row_ids):
    row_len = packed.shape[0]
    latent_width, width = w_q_up.shape
    return whole_call(
        attend_kernel,
        "attend",
        [where],
        [packed, w_q_up, cosine, sine, row_ids[:, None], row_ids[None, :]],
        [
            shaped((row_len, width), low_type),
            shaped((row_len // 2, width), low_type),
            shaped((row_len // 2, width), low_type),
            shaped((width // head_dim, row_len, 1), jnp.float32),
        ],
        [pltpu.VMEM((row_len, width), low_type)],
        2 * width * row_len * (latent_width + 2 * row_len),
        8 * row_len * width,
    )


def attend_back_kernel(where, *refs):
    pieces = refs[: SIDE * CORES]
    query_in, packed, w_out, w_q_up, lse, cosine, sine, ids_q, ids_k = refs[
        SIDE * CORES : SIDE * CORES + 9
    ]
    weight_back, near_out, far_out, query_back, back_rows, totals = refs[SIDE * CORES + 9 :]
    row_len, packed_width = packed.shape
    latent_width, width = w_q_up.shape
    head_dim = (packed_width - latent_width) // 2
    piece = row_len // (SIDE * CORES)
    block = CORES * piece
    scale = head_dim ** (-0.5)
    key_cols = slice(latent_width, latent_width + head_dim)
    value_cols = slice(latent_width + head_dim, latent_width + 2 * head_dim)
    for index in range(0, SIDE * CORES, 2):
        pair = jnp.concatenate([pieces[index][...], pieces[index + 1][...]], axis=0)
        back_rows[index * piece : (index + 2) * piece, :] = matmul(pair, w_out[...]).astype(
            low_type
        )
    totals[:, latent_width:] = jnp.zeros((row_len, 2 * head_dim), jnp.float32)
    for head in range(width // head_dim):
        cols = slice(head * head_dim, (head + 1) * head_dim)
        for index in range(SIDE):
            first = index * block
            end = first + block
            rows = slice(first, end)
            query = query_in[rows, cols]
            back = jnp.concatenate(
                [
                    back_rows[block_at(where[CORES * index + side], piece), cols]
                    for side in range(CORES)
                ],
                axis=0,
            )
            keys = packed[:end, key_cols]
            scores = matmul_nt(query, keys) * scale
            allowed = visible(ids_q[rows, :], ids_k[:, :end], first, block, end)
            probs = jnp.where(allowed, jnp.exp(scores - lse[head, rows, :]), 0.0)
            probs_back = matmul_nt(back, packed[:end, value_cols])
            inner = jnp.sum(probs * probs_back, axis=-1, keepdims=True)
            score_back = (probs * (probs_back - inner)).astype(low_type)
            totals[:end, value_cols] += matmul_tn(probs.astype(low_type), back)
            totals[:end, key_cols] += matmul_tn(score_back, query) * scale
            query_grad = matmul(score_back, keys) * scale
            query_back[rows, cols] = rotate_back(
                query_grad, cosine[rows, :], sine[rows, :]
            ).astype(low_type)
    for index in range(SIDE):
        rows = slice(index * block, (index + 1) * block)
        totals[rows, :latent_width] = matmul_nt(query_back[rows, :], w_q_up[...])
    store_by_distance(where, totals, near_out, far_out, piece)
    weight_back[...] = matmul_tn(packed[:, :latent_width], query_back[...]).astype(low_type)


def attend_back(where, pieces, query_rows, packed, w_out, w_q_up, lse, cosine, sine, row_ids):
    row_len, packed_width = packed.shape
    latent_width, width = w_q_up.shape
    model_width = w_out.shape[0]
    return whole_call(
        attend_back_kernel,
        "attend_back",
        [where],
        [
            *pieces,
            query_rows,
            packed,
            w_out,
            w_q_up,
            lse,
            cosine,
            sine,
            row_ids[:, None],
            row_ids[None, :],
        ],
        [
            shaped((latent_width, width), low_type),
            shaped((row_len // 2, packed_width), low_type),
            shaped((row_len // 2, packed_width), low_type),
        ],
        [
            pltpu.VMEM((row_len, width), low_type),
            pltpu.VMEM((row_len, width), low_type),
            pltpu.VMEM((row_len, packed_width), jnp.float32),
        ],
        2 * width * row_len * (5 * row_len + model_width + 2 * latent_width),
        8 * row_len * width,
    )


def ffn_kernel(ready, numbers, still, held, targets, rest):
    w_gate = still[0]
    features, (w_up, grads, w_down) = held[0], held[SIDE:]
    gate_out, up_out, middle_out, features_back = targets
    gate_raw, up_raw = rest
    width = w_gate.shape[0]
    chunk = width // 2
    tile = features.shape[1] // 4

    def rows_of(part):
        return pl.ds(pl.multiple_of(part * chunk, chunk), chunk)

    def make_gate(part, carry):
        rows = rows_of(part)
        gate_raw[rows, :] = matmul_nt(w_gate[rows, :], features[...])
        return carry

    def make_up(part, carry):
        rows = rows_of(part)
        up_raw[rows, :] = matmul_nt(w_up[rows, :], features[...])
        return carry

    def make_backs(part, carry):
        rows = rows_of(part)
        middle_back = matmul_nt(w_down[rows, :], grads[...])
        gate, up = gate_raw[rows, :], up_raw[rows, :]
        sigmoid = jax.nn.sigmoid(gate)
        activated = gate * sigmoid
        middle_out[rows, :] = (activated * up).astype(low_type)
        gate_out[rows, :] = (
            middle_back * up * sigmoid * (1.0 + gate * (1.0 - sigmoid))
        ).astype(low_type)
        up_out[rows, :] = (middle_back * activated).astype(low_type)
        return carry

    def make_features(part, carry):
        area = pl.ds(pl.multiple_of(part * tile, tile), tile)
        features_back[:, area] = (
            matmul_tn(gate_out[...], w_gate[:, area]) + matmul_tn(up_out[...], w_up[:, area])
        ).astype(low_type)
        return carry

    ready(SIDE - 1)
    lax.fori_loop(0, 2, make_gate, 0)
    ready(SIDE)
    lax.fori_loop(0, 2, make_up, 0)
    ready(SIDE + 2)
    lax.fori_loop(0, 2, make_backs, 0)
    lax.fori_loop(0, 4, make_features, 0)


def ffn_half(owner, pieces, grads, w_gate, w_up, w_down, far):
    piece, model_width = pieces[0].shape
    width = w_gate.shape[0]
    rows = SIDE * piece

    def own_blocks(numbers, source, target):
        return [
            (
                source.at[block_at(numbers[0][SIDE * far + step], piece), :],
                target.at[step * piece : (step + 1) * piece, :],
            )
            for step in range(SIDE)
        ]

    return streamed_call(
        ffn_kernel,
        "ffn_far" if far else "ffn_near",
        [owner],
        [w_gate],
        [*pieces, w_up, grads, w_down],
        [shaped((width, rows), low_type)] * 3 + [shaped((rows, model_width), low_type)],
        [pltpu.VMEM((width, rows), jnp.float32)] * 2,
        10 * rows * model_width * width,
        6 * model_width * width + 6 * rows * model_width,
        {SIDE + 1: (rows, SIDE, own_blocks)},
        SIDE,
    )


def ffn_grads_kernel(owner, *refs):
    count = SIDE * CORES
    pieces, grads, halves, target = refs[:count], refs[count], refs[count + 1 : -1], refs[-1]
    width, half_rows = halves[0].shape
    piece = pieces[0].shape[0]
    places, share = target.shape[0], target.shape[2]
    block = places * share
    cols = pl.ds(pl.multiple_of(pl.program_id(0) * block, block), block)
    features = jnp.concatenate([source[:, cols] for source in pieces], axis=0)
    grads = jnp.concatenate(
        [grads[block_at(owner[index], piece), cols] for index in range(count)], axis=0
    )
    for index, right in enumerate((features, features, grads)):
        total = matmul(halves[index][...], right[:half_rows, :])
        total += matmul(halves[index + 3][...], right[half_rows:, :])
        total = total.astype(low_type)
        for place in range(places):
            target[place, index * width : (index + 1) * width, :] = total[
                :, place * share : (place + 1) * share
            ]


def ffn_grads(owner, pieces, grads, halves, dp_count):
    piece, model_width = pieces[0].shape
    row_len = grads.shape[0]
    width = halves[0].shape[0]
    block = model_width // 4
    share = model_width // dp_count
    return kernel_call(
        ffn_grads_kernel,
        "ffn_grads",
        (4,),
        1,
        [fixed((piece, model_width))] * len(pieces)
        + [fixed((row_len, model_width))]
        + [fixed(halves[0].shape)] * 6,
        pl.BlockSpec((block // share, 3 * width, share), lambda index, owner: (index, 0, 0)),
        pltpu.HBM((dp_count, 3 * width, share), low_type),
        [],
        6 * row_len * model_width * width,
        4 * row_len * model_width + 6 * model_width * width,
    )(owner, *map(in_hbm, pieces), in_hbm(grads), *halves)


def head_grads(pieces, halves, q_up_part, dp_count):
    piece, model_width = pieces[0].shape
    count = len(pieces)
    width = halves[0].shape[1]
    steps = 4
    block = model_width // steps
    each = dp_count // steps
    q_up_rows = q_up_part.shape[0] // dp_count
    out_rows = model_width // dp_count
    rows = piece * count

    def body(*refs):
        sources, (near, far, above, target) = refs[:count], refs[count:]
        cols = pl.ds(pl.multiple_of(pl.program_id(0) * block, block), block)
        left = jnp.concatenate([source[:, cols] for source in sources], axis=0)
        right = jnp.concatenate([near[...], far[...]], axis=0)
        total = matmul_tn(left, right)
        for index in range(each):
            first = index * q_up_rows
            target[index, :q_up_rows, :] = above[first : first + q_up_rows, :]
            first = index * out_rows
            target[index, q_up_rows:, :] = total[first : first + out_rows, :].astype(low_type)

    return kernel_call(
        body,
        "head_grads",
        (steps,),
        0,
        [fixed((piece, model_width))] * count
        + [fixed(source.shape) for source in halves]
        + [pl.BlockSpec((each * q_up_rows, width), lambda index: (index, 0))],
        pl.BlockSpec((each, q_up_rows + out_rows, width), lambda index: (index, 0, 0)),
        pltpu.HBM((dp_count, q_up_rows + out_rows, width), low_type),
        [],
        2 * rows * model_width * width,
        2 * rows * (model_width + width) + 4 * model_width * width,
    )(*map(in_hbm, pieces), *map(in_hbm, halves), q_up_part)


def shared_parts_kernel(count, owner, *refs):
    left, right, gains, target = refs[:count], refs[count:-2], refs[-2], refs[-1]
    left = jnp.concatenate([source[...] for source in left], axis=1)
    right = jnp.concatenate([source[...] for source in right], axis=0)
    total = matmul(left, right).astype(low_type)
    places, extra = gains.shape[0], gains.shape[1]
    rows = total.shape[0] // places
    tiles = total.shape[1] // LANES
    for place in range(places):
        for tile in range(tiles):
            target[place, tile * rows : (tile + 1) * rows, :] = total[
                place * rows : (place + 1) * rows, tile * LANES : (tile + 1) * LANES
            ]
        first = tiles * rows
        target[place, first : first + extra, :] = gains[place, :, :]


def shared_parts_of(owner, left, right, gains):
    count = len(right)
    width = left.shape[0] // count
    piece, cols = right[0].shape
    places = gains.shape[0]
    rows = width // places * (cols // LANES) + gains.shape[1]

    def body(owner, *refs):
        shared_parts_kernel(count, owner, *refs)

    return kernel_call(
        body,
        "shared_parts",
        (1,),
        1,
        [
            pl.BlockSpec((width, piece), lambda index, owner, place=place: (owner[place], 0))
            for place in range(count)
        ]
        + [fixed(source.shape) for source in right]
        + [fixed(gains.shape)],
        fixed((places, rows, LANES)),
        shaped((places, rows, LANES), low_type),
        [],
        2 * piece * count * width * cols,
        2 * piece * count * (width + cols) + 2 * width * cols,
    )(owner, *([in_hbm(left)] * count), *right, gains)


def shared_momenta_kernel(parts, q_down, key, value, *refs):
    grads, moms, gains_out, own, target = refs[:3], refs[3:6], refs[6], refs[7], refs[8]
    total = parts[0].astype(jnp.float32)
    for place in range(1, parts.shape[0]):
        total += parts[place].astype(jnp.float32)
    rows = q_down.shape[0]
    tiles = own.shape[1] // LANES
    first = 0
    for tile in range(tiles):
        own[:, tile * LANES : (tile + 1) * LANES] = total[tile * rows : (tile + 1) * rows, :]
    for old, grad_out, mom_out in zip((q_down, key, value), grads, moms):
        cols = slice(first, first + old.shape[1])
        grad = own[:, cols]
        new = decay_rate * old[...] + grad
        grad_out[...] = grad
        mom_out[...] = new
        own[:, cols] = new
        first += old.shape[1]
    head = tiles * rows
    extra = gains_out.shape[0]
    gains_out[...] = total[head : head + extra, :]
    for place in range(target.shape[0]):
        for tile in range(tiles):
            target[place, tile * rows : (tile + 1) * rows, :] = own[
                :, tile * LANES : (tile + 1) * LANES
            ].astype(low_type)


def shared_momenta(parts, old, extra):
    places, rows, _ = parts.shape
    shapes = [array.shape for array in old]
    width = sum(shape[1] for shape in shapes)
    return whole_call(
        shared_momenta_kernel,
        "shared_momenta",
        [],
        [parts, *old],
        [shaped(shape, jnp.float32) for shape in shapes + shapes]
        + [
            shaped((extra, LANES), jnp.float32),
            shaped((shapes[0][0], width), jnp.float32),
            shaped((places, rows - extra, LANES), low_type),
        ],
        [],
        places * rows * LANES,
        4 * places * rows * LANES,
    )


def panel_places(block):
    panel = min(block, LANES)
    count = -(-block // panel)
    return panel, count, upper_blocks(count)


def upper_blocks(count):
    return [(row, col) for row in range(count) for col in range(row, count)]


def momentum_kernel(spans, block, turned, *refs):
    count = len(spans)
    sums, moms = refs[0], refs[1 : 1 + count]
    grad_out, mom_out = refs[1 + count : 1 + 2 * count], refs[1 + 2 * count : 1 + 3 * count]
    gram_out = refs[-1]
    kind = gram_out.dtype
    panel, tiles, places = panel_places(block)
    place = 0
    for index, (row_at, rows) in enumerate(spans):
        grad = sums[row_at : row_at + rows, :].astype(jnp.float32)
        new = decay_rate * moms[index][...] + grad
        grad_out[index][...] = grad
        mom_out[index][...] = new
        low = new.astype(low_type)
        for first in range(0, low.shape[0 if turned else 1], block):
            if turned:
                part = low[first : first + block, :]
                if tiles * panel > block:
                    blank = jnp.zeros((tiles * panel - block, part.shape[1]), low_type)
                    part = jnp.concatenate([part, blank], axis=0)
                gram = matmul_nt(part, part).astype(kind)
            else:
                part = low[:, first : first + block]
                gram = matmul_tn(part, part).astype(kind)
            for row, col in places:
                gram_out[place * panel : (place + 1) * panel, :] = gram[
                    row * panel : (row + 1) * panel, col * panel : (col + 1) * panel
                ]
                place += 1


def momenta(sums, moms, block, turned, name):
    axis = 0 if turned else 1
    blocks = sum(mom.shape[axis] // block for mom in moms)
    panel, tiles, places = panel_places(block)
    spans, row_at = [], 0
    for mom in moms:
        spans.append((row_at, mom.shape[0]))
        row_at += mom.shape[0]

    def body(*refs):
        momentum_kernel(spans, block, turned, *refs)

    shapes = [mom.shape for mom in moms]
    panels = (blocks * len(places) * panel, panel)
    results = whole_call(
        body,
        name,
        [],
        [sums, *moms],
        [shaped(shape, jnp.float32) for shape in shapes + shapes]
        + [shaped(panels, low_type)],
        [],
        2 * block * sum(shape[0] * shape[1] for shape in shapes),
        16 * sum(shape[0] * shape[1] for shape in shapes),
    )
    count = len(moms)
    return results[:count], results[count : 2 * count], results[-1]


def trace_of(gram):
    rows = lax.broadcasted_iota(jnp.int32, gram.shape, 0)
    cols = lax.broadcasted_iota(jnp.int32, gram.shape, 1)
    diagonal = jnp.where(rows == cols, gram, 0.0)
    return jnp.sum(jnp.sum(diagonal, axis=0, keepdims=True), axis=1, keepdims=True)


def polish_small(grams, blocks, turned):
    def apply(values, right, turn):
        values = values.astype(low_type)
        return matmul(right, values) if turn else matmul(values, right)

    factors = [1.0 / (jnp.sqrt(trace_of(gram)) + 1e-07) for gram in grams]
    iterates = [block * factor for block, factor in zip(blocks, factors)]
    grams = [gram * (factor * factor) for gram, factor in zip(grams, factors)]
    for step_index in range(NS_STEPS):
        lows = [gram.astype(low_type) for gram in grams]
        if step_index + 1 == NS_STEPS:
            first = [apply(*args) for args in zip(iterates, lows, turned)]
            second = [apply(*args) for args in zip(first, lows, turned)]
            return [
                coef_first * iterate + coef_second * one + coef_third * two
                for iterate, one, two in zip(iterates, first, second)
            ]
        squares = [matmul(low, low) for low in lows]
        changes = [
            (coef_second * gram + coef_third * square).astype(low_type)
            for gram, square in zip(grams, squares)
        ]
        moves = [apply(*args) for args in zip(iterates, changes, turned)]
        iterates = [coef_first * iterate + move for iterate, move in zip(iterates, moves)]
        once = [matmul(low, change) for low, change in zip(lows, changes)]
        twice = [matmul(one.astype(low_type), change) for one, change in zip(once, changes)]
        grams = [
            (coef_first * coef_first) * gram + (2.0 * coef_first) * one + two
            for gram, one, two in zip(grams, once, twice)
        ]


def gram_from_panels(panels, first, block):
    panel, tiles, places = panel_places(block)
    parts = {}
    for index, (row, col) in enumerate(places):
        start = (first + index) * panel
        parts[row, col] = panels[start : start + panel, :].astype(jnp.float32)
        if row != col:
            parts[col, row] = parts[row, col].T
    return jnp.concatenate(
        [
            jnp.concatenate([parts[row, col] for col in range(tiles)], axis=1)
            for row in range(tiles)
        ],
        axis=0,
    )


def updates(rank, panels, groups, name):
    groups = [(None, *group) for group in groups]
    counts = [len(group[1]) for group in groups]
    total = sum(counts)
    moms = [mom for group in groups for mom in group[1]]
    weights = [weight for group in groups for weight in group[2]]
    flags = [group[4] for group in groups for _ in group[1]]
    shapes = [mom.shape for mom in moms]

    places = panels.shape[0]
    chunks, starts = [], []
    for _, group_moms, _, block, turned in groups:
        panel, _, tile_places = panel_places(block)
        count = sum(mom.shape[0 if turned else 1] // block for mom in group_moms)
        starts.append(sum(chunks))
        chunks.append(count * len(tile_places) * panel // places)

    def body(rank, *refs):
        parts, refs, flats = refs[0], refs[1 : 1 + 3 * total], refs[1 + 3 * total :]
        mom_refs, weight_refs, targets = refs[:total], refs[total : 2 * total], refs[2 * total :]
        for flat, chunk, at in zip(flats, chunks, starts):
            for place in range(places):
                flat[place * chunk : (place + 1) * chunk, :] = parts[place, at : at + chunk, :]
        grams, blocks, turns, targets_at = [], [], [], []
        index = 0
        for group, source in zip(groups, flats):
            block, turned = group[3], group[4]
            panel, tiles, tile_places = panel_places(block)
            first = 0
            for weight in group[2]:
                rate = muon_rate * math.sqrt(weight.shape[1 if turned else 0] / block)
                for start in range(0, shapes[index][0 if turned else 1], block):
                    grams.append(gram_from_panels(source, first, block))
                    first += len(tile_places)
                    part = slice(start, start + block)
                    area = (part, slice(None)) if turned else (slice(None), part)
                    values = mom_refs[index][area]
                    if turned and tiles * panel > block:
                        blank = jnp.zeros((tiles * panel - block, values.shape[1]), jnp.float32)
                        values = jnp.concatenate([values, blank], axis=0)
                    blocks.append(values)
                    turns.append(turned)
                    targets_at.append((index, area, rate, block))
                index += 1
        for ortho, turn, (index, area, rate, block) in zip(
            polish_small(grams, blocks, turns), turns, targets_at
        ):
            if turn:
                ortho = ortho[:block, :]
            targets[index][area] = weight_refs[index][area].astype(jnp.float32) - rate * ortho

    def own_block(shape, turned):
        if turned:
            return pl.BlockSpec(shape, lambda index, rank: (0, rank[0]))
        return pl.BlockSpec(shape, lambda index, rank: (rank[0], 0))

    results = kernel_call(
        body,
        name,
        (1,),
        1,
        [fixed(panels.shape)]
        + [fixed(shape) for shape in shapes]
        + [own_block(shape, flag) for shape, flag in zip(shapes, flags)],
        [fixed(shape) for shape in shapes],
        [shaped(shape, jnp.float32) for shape in shapes],
        [pltpu.VMEM((places * chunk, panels.shape[2]), low_type) for chunk in chunks],
        14 * panels.size * groups[-1][3],
        sum(12 * shape[0] * shape[1] for shape in shapes),
    )(rank, panels, *map(in_hbm, moms), *map(in_hbm, weights))
    split, place = [], 0
    for count in counts:
        split.append(results[place : place + count])
        place += count
    return split


def panel_sums_kernel(parts, target):
    total = parts[0].astype(jnp.float32)
    for place in range(1, parts.shape[0]):
        total += parts[place].astype(jnp.float32)
    total = total.astype(low_type)
    for place in range(target.shape[0]):
        target[place, :, :] = total


def panel_sums(parts):
    return whole_call(
        panel_sums_kernel,
        "panel_sums",
        [],
        [parts],
        [shaped(parts.shape, low_type)],
        [],
        parts.size,
        4 * parts.size,
    )[0]


def polish(gram, gram_low, change_low, once_low, iterate, size):
    block = min(size, 512)
    count = size // block
    for step_index in range(NS_STEPS):
        last = step_index + 1 == NS_STEPS
        if last:
            first_term = matmul(iterate.astype(low_type), gram_low[...])
            second_term = matmul(first_term.astype(low_type), gram_low[...])
            return coef_first * iterate + coef_second * first_term + coef_third * second_term

        def make_change(index, carry):
            rows = block_at(index, block)
            square = matmul(gram_low[rows, :], gram_low[...])
            change_low[rows, :] = (coef_second * gram[rows, :] + coef_third * square).astype(
                low_type
            )
            return carry

        def make_once(index, carry):
            rows = block_at(index, block)
            once = matmul(gram_low[rows, :], change_low[...])
            once_low[rows, :] = once.astype(low_type)
            gram[rows, :] = (coef_first * coef_first) * gram[rows, :] + (2.0 * coef_first) * once
            return carry

        def make_gram(index, carry):
            rows = block_at(index, block)
            total = gram[rows, :] + matmul(once_low[rows, :], change_low[...])
            gram[rows, :] = total
            gram_low[rows, :] = total.astype(low_type)
            return carry

        lax.fori_loop(0, count, make_change, 0)
        iterate = coef_first * iterate + matmul(iterate.astype(low_type), change_low[...])
        lax.fori_loop(0, count, make_once, 0)
        lax.fori_loop(0, count, make_gram, 0)


def gram_parts_kernel(where, *refs):
    parts, gains, near_out, far_out, blocks = refs
    narrow = blocks.shape[1]
    chunk = blocks.shape[0] // (SIDE * CORES)
    extra = gains.shape[0] // (SIDE * CORES)
    places = parts.shape[0]
    tiles = parts.shape[1] // extra
    rows = jnp.concatenate(
        [
            jnp.concatenate(
                [parts[place, tile * extra : (tile + 1) * extra, :] for place in range(places)],
                axis=0,
            )
            for tile in range(tiles)
        ],
        axis=1,
    )
    wide = rows.shape[1] // narrow
    places = upper_blocks(wide - 2) + [(wide - 2, wide - 2), (wide - 1, wide - 1)]
    for index, (left, right) in enumerate(places):
        blocks[index * narrow : (index + 1) * narrow, :] = matmul_tn(
            rows[:, left * narrow : (left + 1) * narrow],
            rows[:, right * narrow : (right + 1) * narrow],
        ).astype(low_type)
    core = where[SIDE * CORES]
    for step in range(SIDE):
        near = CORES * step + core
        far = CORES * step + 1 - core
        for target, source, place in ((near_out, near, 0), (far_out, far, SIDE)):
            start = pl.multiple_of((where[source] - place) * (chunk + extra), extra)
            target[pl.ds(start, chunk), :] = blocks[block_at(source, chunk), :]
            start = pl.multiple_of(start + chunk, extra)
            target[pl.ds(start, extra), :] = gains[block_at(source, extra), :]


def gram_parts(where, parts, gains, narrow):
    places = parts.shape[0]
    extra = gains.shape[0] // (SIDE * CORES)
    width = parts.shape[1] // extra * LANES
    wide = width // narrow - 2
    total = (wide * (wide + 1) // 2 + 2) * narrow
    out_rows = (total + gains.shape[0]) // CORES
    return whole_call(
        gram_parts_kernel,
        "gram_parts",
        [where],
        [parts, gains],
        [shaped((out_rows, narrow), low_type)] * 2,
        [pltpu.VMEM((total, narrow), low_type)],
        2 * places * extra * total * narrow,
        4 * total * narrow,
    )


def shared_kernel(rows_all, owner, *refs):
    pieces = refs[: SIDE * CORES]
    own, *refs = refs[SIDE * CORES :]
    weights, targets, refs = refs[:3], refs[3:6], refs[6:]
    blocks, gram, gram_low, change_low, once_low = refs
    chunk, narrow = pieces[0].shape
    wide = gram.shape[0]
    for index, source in enumerate(pieces):
        blocks[block_at(owner[index], chunk), :] = source[...]
    places = upper_blocks(wide // narrow)
    trace = jnp.zeros((1, 1), jnp.float32)
    for index, (left, right) in enumerate(places):
        if left == right:
            trace += trace_of(blocks[index * narrow : (index + 1) * narrow, :].astype(jnp.float32))
    factor = 1.0 / (jnp.sqrt(trace) + 1e-07)
    for index, (left, right) in enumerate(places):
        block = blocks[index * narrow : (index + 1) * narrow, :].astype(jnp.float32)
        block = block * (factor * factor)
        rows = slice(left * narrow, (left + 1) * narrow)
        cols = slice(right * narrow, (right + 1) * narrow)
        gram[rows, cols] = block
        gram_low[rows, cols] = block.astype(low_type)
        if left != right:
            turned = block.T
            gram[cols, rows] = turned
            gram_low[cols, rows] = turned.astype(low_type)
    grams, starts = [], []
    for index in range(2):
        first = (len(places) + index) * narrow
        grams.append(blocks[first : first + narrow, :].astype(jnp.float32))
        starts.append(own[:, wide + index * narrow : wide + (index + 1) * narrow])
    for index, ortho in enumerate(polish_small(grams, starts, [False, False])):
        rate = muon_rate * math.sqrt(rows_all / narrow)
        targets[1 + index][...] = weights[1 + index][...].astype(jnp.float32) - rate * ortho
    ortho = polish(gram, gram_low, change_low, once_low, own[:, :wide] * factor, wide)
    rate = muon_rate * math.sqrt(rows_all / wide)
    targets[0][...] = weights[0][...].astype(jnp.float32) - rate * ortho


def shared_updates(owner, pieces, own, weights, rows_all):
    chunk, narrow = pieces[0].shape
    wide = weights[0].shape[1]

    def body(owner, *refs):
        shared_kernel(rows_all, owner, *refs)

    return whole_call(
        body,
        "shared_updates",
        [owner],
        [*map(in_hbm, pieces), in_hbm(own), *map(in_hbm, weights)],
        [shaped(weight.shape, jnp.float32) for weight in weights],
        [pltpu.VMEM((SIDE * CORES * chunk, narrow), low_type), pltpu.VMEM((wide, wide), jnp.float32)]
        + [pltpu.VMEM((wide, wide), low_type)] * 3,
        20 * wide * wide * wide,
        8 * wide * wide,
    )


def own_rows(weight, count, rank):
    share_rows = weight.shape[0] // count
    return lax.dynamic_slice_in_dim(weight, rank * share_rows, share_rows, 0)


def on_device(
    tokens_in,
    cotangent,
    seg_starts,
    gains,
    w_q_down,
    w_key,
    w_value,
    w_q_up,
    w_out,
    w_gate,
    w_up,
    w_down,
    mom_gains,
    mom_q_down,
    mom_key,
    mom_value,
    mom_q_up,
    mom_out,
    mom_gate,
    mom_up,
    mom_down,
):
    heads_count = lax.axis_size("heads")
    heads_rank = lax.axis_index("heads")
    dp_count = lax.axis_size("dp")
    dp_rank = lax.axis_index("dp")
    all_rank = lax.axis_index(("dp", "heads"))
    all_count = dp_count * heads_count
    local_rows = tokens_in.shape[0]
    row_len = local_rows * heads_count
    model_width = tokens_in.shape[1]
    latent_width = w_q_down.shape[1]
    head_dim = w_key.shape[1]
    local_q = w_q_up.shape[1]
    share_rows = model_width // all_count
    share_gains = gains.shape[0] // all_count
    starts = seg_starts[0]
    whole_index = jnp.arange(row_len, dtype=jnp.int32)
    own_index = heads_rank * local_rows + jnp.arange(local_rows, dtype=jnp.int32)
    own_core = heads_rank % CORES
    own_step = heads_rank // CORES
    ranks = jnp.arange(heads_count, dtype=jnp.int32)
    where = SIDE * ((ranks % CORES) ^ own_core) + (ranks // CORES - own_step) % SIDE
    where = jnp.concatenate([where, own_core[None]]).astype(jnp.int32)
    owner = CORES * ((ranks % SIDE + own_step) % SIDE) + ((ranks // SIDE) ^ own_core)
    owner = owner.astype(jnp.int32)
    dp_place = dp_rank[None].astype(jnp.int32)
    gain_one = gains[:model_width]
    gain_latent = gains[model_width : model_width + latent_width]
    gain_two = gains[model_width + latent_width :]

    inputs = tokens_in.astype(jnp.float32)
    scale_one = rms_scale(inputs)
    normed_one = (inputs * scale_one * gain_one).astype(low_type)
    latent_raw = matmul(normed_one, w_q_down)
    scale_latent = rms_scale(latent_raw)
    latent_normed = (latent_raw * scale_latent * gain_latent).astype(low_type)
    own_pos = segment_info(starts, own_index)[1]
    own_cos, own_sin = rotary_tables(own_pos, head_dim)
    key_local = rotate(matmul(normed_one, w_key), own_cos, own_sin).astype(low_type)
    value_local = matmul(normed_one, w_value).astype(low_type)
    packed = lax.all_gather(
        jnp.concatenate([latent_normed, key_local, value_local], axis=1), "heads", axis=0, tiled=True
    )
    grad_rows = lax.all_gather(after(cotangent, packed), "heads", axis=0, tiled=True)
    normed_parts = lax.all_to_all(
        normed_one.T.reshape(dp_count, heads_count, share_rows, local_rows)
        .transpose(1, 0, 2, 3)
        .reshape(model_width, local_rows),
        "heads",
        split_axis=0,
        concat_axis=0,
        tiled=True,
    )
    shared_rows = [own_rows(weight, all_count, all_rank) for weight in (w_q_down, w_key, w_value)]
    packed, normed_parts, shared_rows = lax.optimization_barrier(
        (packed, normed_parts, shared_rows)
    )
    row_ids, row_pos = segment_info(starts, whole_index)
    row_cos, row_sin = rotary_tables(row_pos, head_dim)
    query_rows, attended_near, attended_far, lse = attend(
        where, packed, w_q_up, head_dim, row_cos, row_sin, row_ids
    )
    attn_mixed = ring_sums(
        ring_operands(
            chip_sums(
                matmul_nt(attended_far, w_out).astype(low_type),
                matmul_nt(attended_near, w_out).astype(low_type),
            )
        )
    )
    hidden_one = inputs + attn_mixed
    scale_two = rms_scale(hidden_one)
    normed_two = (hidden_one * scale_two * gain_two).astype(low_type)

    gate_turned, up_turned, down_turned = w_gate.T, w_up.T, w_down.T
    pieces_two = gather_heads(normed_two)
    gate_near, up_near, middle_near, back_near = ffn_half(
        owner, pieces_two[:SIDE], grad_rows, gate_turned, up_turned, down_turned, 0
    )
    gate_far, up_far, middle_far, back_far = ffn_half(
        owner, pieces_two[SIDE:], grad_rows, gate_turned, up_turned, down_turned, 1
    )
    chip_two = ring_operands(chip_sums(back_far, back_near))
    normed_two_back = ring_sums(chip_two)
    ffn_part = ffn_grads(
        owner,
        pieces_two,
        grad_rows,
        (after(gate_near, *chip_two), up_near, middle_near, gate_far, up_far, middle_far),
        dp_count,
    )
    ffn_sums = lax.psum_scatter(ffn_part, "dp", scatter_dimension=0, tiled=True)[0]
    mixed_far = matmul_tn(after(middle_far, *chip_two), down_turned).astype(low_type)
    mixed_near = matmul_tn(after(middle_near, *chip_two), down_turned).astype(low_type)
    hidden_part, gain_two_grad = norm_back(hidden_one, scale_two, gain_two, normed_two_back)
    hidden_back = cotangent.astype(jnp.float32) + hidden_part

    hidden_low = after(hidden_back.astype(low_type), ffn_part, mixed_far, mixed_near)
    pieces_hidden, *chip_mixed = gather_heads(
        hidden_low, tuple(ring_operands(chip_sums(mixed_far, mixed_near)))
    )
    q_up_part, sums_near, sums_far = attend_back(
        where, pieces_hidden, query_rows, packed, w_out, w_q_up, lse, row_cos, row_sin, row_ids
    )
    chip_back = ring_operands(chip_sums(sums_far, sums_near))
    packed_sums = ring_sums(chip_back)
    head_parts = head_grads(
        pieces_hidden, (after(attended_near, *chip_back), attended_far), q_up_part, dp_count
    )
    packed_sums, head_parts = lax.optimization_barrier((packed_sums, head_parts))
    head_sums = lax.psum_scatter(head_parts, "dp", scatter_dimension=0, tiled=True)[0]
    latent_back = packed_sums[:, :latent_width]
    key_sum = packed_sums[:, latent_width : latent_width + head_dim]
    value_sum = packed_sums[:, latent_width + head_dim :]
    latent_raw_grad, gain_latent_grad = norm_back(
        latent_raw, scale_latent, gain_latent, latent_back
    )
    latent_raw_back = latent_raw_grad.astype(low_type)
    key_pre_back = rotate_back(key_sum, own_cos, own_sin).astype(low_type)
    values_low = value_sum.astype(low_type)

    back_low = jnp.concatenate([latent_raw_back, key_pre_back, values_low], axis=1)
    latent_out = matmul_nt(latent_raw_back, w_q_down)
    pieces_back, latent_out = gather_heads(back_low, (latent_out,))
    normed_one_back = (
        latent_out
        + matmul_nt(key_pre_back, w_key)
        + matmul_nt(values_low, w_value)
    )
    input_part, gain_one_grad = norm_back(inputs, scale_one, gain_one, normed_one_back)
    input_grad = hidden_back + input_part
    gains_part = jnp.concatenate([gain_one_grad, gain_latent_grad, gain_two_grad])
    gains_part = gains_part.reshape(dp_count, heads_count, share_gains).astype(low_type)
    gains_part = jnp.pad(
        gains_part, ((0, 0), (0, share_rows - heads_count), (0, LANES - share_gains))
    )

    shared_part = shared_parts_of(owner, normed_parts, pieces_back, gains_part)
    *shared_grads, gains_dp, shared_mom, next_parts = shared_momenta(
        exchange_dp(shared_part), (mom_q_down, mom_key, mom_value), share_rows
    )
    q_down_grad, key_w_grad, value_w_grad, q_down_mom, key_w_mom, value_w_mom = shared_grads

    gains_rows = jnp.pad(
        gains_dp[:heads_count, None, :share_gains].astype(low_type),
        ((0, 0), (0, share_rows - 1), (0, head_dim - share_gains)),
    ).reshape(heads_count * share_rows, head_dim)
    ffn_grad, ffn_mom, ffn_gram = momenta(
        after(ffn_sums, shared_mom),
        (mom_gate.T, mom_up.T, mom_down.T),
        FF_BLOCK,
        True,
        "ffn_momenta",
    )
    parts_mom, ffn_gram = lax.optimization_barrier((exchange_dp(next_parts), ffn_gram))
    gram_near, gram_far = gram_parts(where, parts_mom, gains_rows, head_dim)
    chip_gram = ring_operands(chip_sums(gram_far, gram_near))
    gram_sums = ring_sums(chip_gram)
    head_grad, head_mom, head_gram = momenta(
        head_sums, (mom_q_up, mom_out), head_dim, False, "head_momenta"
    )
    gram_chunk = gram_sums.shape[0] - share_rows
    panels = jnp.concatenate(
        [
            after(panel, gram_sums).reshape(dp_count, -1, panel.shape[1])
            for panel in (ffn_gram, head_gram)
        ],
        axis=1,
    )
    pieces_gram, panels = gather_heads(
        gram_sums[:gram_chunk].astype(low_type), (exchange_dp(panels),)
    )
    panels = panel_sums(panels)
    pieces_gram, panels, chip_mixed = lax.optimization_barrier((pieces_gram, panels, chip_mixed))
    panels = exchange_dp(panels)
    layer_out = (hidden_one + ring_sums(chip_mixed)).astype(low_type)
    gains_grad = gram_sums[gram_chunk, :share_gains]
    gains_mom = decay_rate * mom_gains + gains_grad
    gains_new = own_rows(gains, all_count, all_rank) - gain_rate * gains_mom

    shared_new = shared_updates(
        owner,
        pieces_gram,
        shared_mom,
        shared_rows,
        model_width,
    )
    shared_new, panels, layer_out = lax.optimization_barrier((shared_new, panels, layer_out))
    ffn_new, (q_up_new, out_w_new) = updates(
        dp_place,
        panels,
        (
            (ffn_mom, (gate_turned, up_turned, down_turned), FF_BLOCK, True),
            (head_mom, (w_q_up, w_out), head_dim, False),
        ),
        "block_updates",
    )
    ffn_grad, ffn_mom, ffn_new = [
        [array.T for array in arrays] for arrays in (ffn_grad, ffn_mom, ffn_new)
    ]
    return (
        layer_out,
        input_grad,
        gains_grad,
        q_down_grad,
        key_w_grad,
        value_w_grad,
        *head_grad,
        *ffn_grad,
        gains_mom,
        q_down_mom,
        key_w_mom,
        value_w_mom,
        *head_mom,
        *ffn_mom,
        gains_new,
        *shared_new,
        q_up_new,
        out_w_new,
        *ffn_new,
    )


def solution(mesh):
    placed = (
        P(("dp", "heads"), None),
        P(("dp", "heads"), None),
        P("dp", None),
        P(),
        P(),
        P(),
        P(),
        P(None, "heads"),
        P(None, "heads"),
        P(None, "heads"),
        P(None, "heads"),
        P(None, "heads"),
        P(("dp", "heads")),
        P(("dp", "heads"), None),
        P(("dp", "heads"), None),
        P(("dp", "heads"), None),
        P("dp", "heads"),
        P("dp", "heads"),
        P("dp", "heads"),
        P("dp", "heads"),
        P("dp", "heads"),
    )
    return jax.shard_map(
        on_device,
        mesh=mesh,
        in_specs=placed,
        out_specs=(
            P(("dp", "heads"), None),
            P(("dp", "heads"), None),
            P(("dp", "heads")),
            P(("dp", "heads"), None),
            P(("dp", "heads"), None),
            P(("dp", "heads"), None),
            P("dp", "heads"),
            P("dp", "heads"),
            P("dp", "heads"),
            P("dp", "heads"),
            P("dp", "heads"),
            P(("dp", "heads")),
            P(("dp", "heads"), None),
            P(("dp", "heads"), None),
            P(("dp", "heads"), None),
            P("dp", "heads"),
            P("dp", "heads"),
            P("dp", "heads"),
            P("dp", "heads"),
            P("dp", "heads"),
            P(("dp", "heads")),
            P(("dp", "heads"), None),
            P(("dp", "heads"), None),
            P(("dp", "heads"), None),
            P("dp", "heads"),
            P("dp", "heads"),
            P("dp", "heads"),
            P("dp", "heads"),
            P("dp", "heads"),
        ),
        check_vma=False,
    )
```

time: 549 us -> 478 us (0.87)
  starting transfers between devices: 148 us -> 65.5 us
  blocking collectives: 0 us -> 22.4 us
  waiting for transfers between devices: 177 us -> 199 us
  local copies, waits for them, and re-layouts: 40 us -> 23.5 us
  other arithmetic: 31.9 us -> 18.1 us
    ppermute x48, waiting for transfers between devices: 93.5 us -> 146 us  [shift_heads(): return lax.ppermute(values, 'heads', pairs)]
    ppermute x36 -> x0, starting transfers between devices: 48.5 us -> none  [shift_dp(): return lax.ppermute(values, 'dp', pairs)]
    ppermute x36 -> x0, waiting for transfers between devices: 46.6 us -> none  [shift_dp(): return lax.ppermute(values, 'dp', pairs)]
    ppermute x48, starting transfers between devices: 95.7 us -> 50.6 us  [shift_heads(): return lax.ppermute(values, 'heads', pairs)]
    all_to_all x0 -> x1, blocking collectives: none -> 22.4 us  [exchange_dp(): return lax.all_to_all(parts, 'dp', split_axis=0, concat_axis=0, tiled=True)]
    unnamed x228 -> x161, local copies, waits for them, and re-layouts: 32.7 us -> 14.1 us
    all_to_all x0 -> x3, waiting for transfers between devices: none -> 17.1 us  [exchange_dp(): return lax.all_to_all(parts, 'dp', split_axis=0, concat_axis=0, tiled=True)]
    all_to_all x0 -> x3, starting transfers between devices: none -> 11.2 us  [exchange_dp(): return lax.all_to_all(parts, 'dp', split_axis=0, concat_axis=0, tiled=True)]
  transfers between devices with their start and end apart: 88 -> 56, of which waited for: 39 -> 32; matrix products, arithmetic and copies ran while one was open for 8% -> 7% of each run, Pallas kernels for 15% -> 14%
where the time goes in v5:
time: 478 us; the launch traced here: 469 us
  waiting for transfers between devices  199 us (42%)
  Pallas kernels  108 us (23%)
  starting transfers between devices  65.5 us (14%)
  local copies, waits for them, and re-layouts  23.5 us (5%)
  blocking collectives  22.4 us (5%)
  other arithmetic  18.1 us (4%)
  matrix products  17.8 us (4%)
  between operations  15.4 us (3%)
    ppermute x48, waiting for transfers between devices, shift_heads(): return lax.ppermute(values, 'heads', pairs)  146 us
    ppermute x48, starting transfers between devices, shift_heads(): return lax.ppermute(values, 'heads', pairs)  50.6 us
    pallas_call x8, Pallas kernels, whole_call(): pl.pallas_call(body, in_specs=[pl.BlockSpec(memory_space=pltpu.SMEM)] * l...  45.5 us
    all_gather x1, waiting for transfers between devices, on_device(): lax.all_gather(jnp.concatenate([latent_normed, key_local, value_local], a...  31.5 us
    pallas_call x2, Pallas kernels, streamed_call(): pl.pallas_call(wrapped, grid_spec=pltpu.PrefetchScalarGridSpec(num_scalar...  24.6 us
    all_to_all x1, blocking collectives, exchange_dp(): return lax.all_to_all(parts, 'dp', split_axis=0, concat_axis=0, tiled=True)  22.4 us
    all_to_all x3, waiting for transfers between devices, exchange_dp(): return lax.all_to_all(parts, 'dp', split_axis=0, concat_axis=0, tiled=True)  17.1 us
    pallas_call x1, Pallas kernels, ffn_grads(): kernel_call(ffn_grads_kernel, 'ffn_grads', (4,), 1, [fixed((piece, model_...  15.1 us
  transfers between devices with their start and end apart: 56, of which 32 were waited for; matrix products, arithmetic and copies ran while one was open for 7% of the time, Pallas kernels for 14%

profile of v5, /device:TPU:1, one launch (start us, length us, event | category | flops | bytes accessed | tf_op | source)
XLA Modules:
  0.0 469.4 jit_solution(7245921466943217535)
XLA Ops:
  17.8 31.5 %all-gather.3.cloned.1.call-done.packed.refs_9_ = bf16[1024,1536]{1,0:T(8,128)(2,1)} async-done(((bf16[128,1536]{1,0:T(8,128)(2,1)}), bf16[1024,1536]{1,0:T(8,128)(2,1)}) %all-gather.3.cloned.1.call-update) | async-done | bytes 3145744 | tf_op jit(solution)/shard_map/all_gather | solution.py:1152
  66.5 6.4 %attend.1 = (bf16[1024,512]{1,0:T(8,128)(2,1)S(1)}, bf16[512,512]{1,0:T(8,128)(2,1)S(1)}, bf16[512,512]{1,0:T(8,128)(2,1)S(1)}, f32[2,1024,1]{2,1,0:T(8,128)S(1)}) custom-call(s32[9]{0:T(128)S(1)} %pad_add_fusion.where, bf16[1024,1536]{1,0:T(8,128)(2,1)S(1)} %copy-done.31, bf16[1024,512]{1,0:T(8,128)(2,1)S(1)} %copy-done.4, ...), custom_call_target="tpu_custom_call" | custom-call | flops 3221225472 | bytes 4194304 | tf_op jit(solution)/shard_map/attend/pallas_call | solution.py:245
  84.5 12.0 %collective-permute-done.1 = bf16[128,2048]{1,0:T(8,128)(2,1)S(1)} collective-permute-done((bf16[128,2048]{1,0:T(8,128)(2,1)S(1)}, bf16[128,2048]{1,0:T(8,128)(2,1)S(1)}, u32[]{:S(2)}, u32[]{:S(2)}) %collective-permute-start.1) | collective-permute-done | bytes 524320 | tf_op jit(solution)/shard_map/ppermute | solution.py:92
  96.5 10.4 %collective-permute-done.2 = bf16[128,2048]{1,0:T(8,128)(2,1)S(1)} collective-permute-done((bf16[128,2048]{1,0:T(8,128)(2,1)S(1)}, bf16[128,2048]{1,0:T(8,128)(2,1)S(1)}, u32[]{:S(2)}, u32[]{:S(2)}) %collective-permute-start.2) | collective-permute-done | bytes 524320 | tf_op jit(solution)/shard_map/ppermute | solution.py:92
  112.7 9.7 %collective-permute-done.6.refs_5_.refs_3_ = bf16[128,2048]{1,0:T(8,128)(2,1)S(1)} collective-permute-done((bf16[128,2048]{1,0:T(8,128)(2,1)S(1)}, bf16[128,2048]{1,0:T(8,128)(2,1)S(1)}, u32[]{:S(2)}, u32[]{:S(2)}) %collective-permute-start.6) | collective-permute-done | bytes 524320 | tf_op jit(solution)/shard_map/ppermute | solution.py:92
  122.4 12.9 %collective-permute-done.5.refs_4_.refs_2_ = bf16[128,2048]{1,0:T(8,128)(2,1)S(1)} collective-permute-done((bf16[128,2048]{1,0:T(8,128)(2,1)S(1)}, bf16[128,2048]{1,0:T(8,128)(2,1)S(1)}, u32[]{:S(2)}, u32[]{:S(2)}) %collective-permute-start.5) | collective-permute-done | bytes 524320 | tf_op jit(solution)/shard_map/ppermute | solution.py:92
  141.5 12.3 %ffn_far.1 = (bf16[704,512]{1,0:T(8,128)(2,1)S(1)}, bf16[704,512]{1,0:T(8,128)(2,1)S(1)}, bf16[704,512]{1,0:T(8,128)(2,1)S(1)}, bf16[512,2048]{1,0:T(8,128)(2,1)S(1)}) custom-call(s32[8]{0:T(128)S(1)} %fusion.34.refs_0_.owner, bf16[704,2048]{1,0:T(8,128)(2,1)S(1)} %bitcast.54, bf16[128,2048]{1,0:T(8,128)(2,1)} %copy-done.72, bf16[128,2048]{1,0:T(8,128)(2,1)} %copy-done.73, ...), custom_call_target="tpu_custom_call" | custom-call | flops 7381975040 | bytes 14942208 | tf_op jit(solution)/shard_map/ffn_far/pallas_call | solution.py:225
  154.5 12.3 %ffn_near.1 = (bf16[704,512]{1,0:T(8,128)(2,1)S(1)}, bf16[704,512]{1,0:T(8,128)(2,1)S(1)}, bf16[704,512]{1,0:T(8,128)(2,1)S(1)}, bf16[512,2048]{1,0:T(8,128)(2,1)S(1)}) custom-call(s32[8]{0:T(128)S(1)} %fusion.34.refs_0_.owner, bf16[704,2048]{1,0:T(8,128)(2,1)S(1)} %bitcast.55, bf16[128,2048]{1,0:T(8,128)(2,1)} %copy-done.61, bf16[128,2048]{1,0:T(8,128)(2,1)} %copy-done.71, ...), custom_call_target="tpu_custom_call" | custom-call | flops 7381975040 | bytes 14942208 | tf_op jit(solution)/shard_map/ffn_near/pallas_call | solution.py:225
  168.8 15.1 %ffn_grads.1 = bf16[16,2112,128]{2,1,0:T(8,128)(2,1)} custom-call(s32[8]{0:T(128)S(1)} %fusion.34.refs_0_.owner, bf16[128,2048]{1,0:T(8,128)(2,1)} %copy-done.61, bf16[128,2048]{1,0:T(8,128)(2,1)} %copy-done.71, bf16[128,2048]{1,0:T(8,128)(2,1)} %copy-done.70, bf16[128,2048]{1,0:T(8,128)(2,1)} %copy-done.69, bf16[128,2048]{1,0:T(8,128)(2,1)} %copy-done.72, ...), custom_call_target="tpu_custom_call" | custom-call | flops 8858370048 | bytes 17039360 | tf_op jit(solution)/shard_map/ffn_grads/pallas_call | solution.py:559
  192.0 11.5 %collective-permute-done.12 = bf16[128,2048]{1,0:T(8,128)(2,1)S(1)} collective-permute-done((bf16[128,2048]{1,0:T(8,128)(2,1)S(1)}, bf16[128,2048]{1,0:T(8,128)(2,1)S(1)}, u32[]{:S(2)}, u32[]{:S(2)}) %collective-permute-start.12) | collective-permute-done | bytes 524320 | tf_op jit(solution)/shard_map/ppermute | solution.py:92
  203.5 11.4 %collective-permute-done.13 = bf16[128,2048]{1,0:T(8,128)(2,1)S(1)} collective-permute-done((bf16[128,2048]{1,0:T(8,128)(2,1)S(1)}, bf16[128,2048]{1,0:T(8,128)(2,1)S(1)}, u32[]{:S(2)}, u32[]{:S(2)}) %collective-permute-start.13) | collective-permute-done | bytes 524320 | tf_op jit(solution)/shard_map/ppermute | solution.py:92
  226.9 8.8 %collective-permute-done.17.refs_3_ = bf16[128,2048]{1,0:T(8,128)(2,1)S(1)} collective-permute-done((bf16[128,2048]{1,0:T(8,128)(2,1)S(1)}, bf16[128,2048]{1,0:T(8,128)(2,1)S(1)}, u32[]{:S(2)}, u32[]{:S(2)}) %collective-permute-start.17) | collective-permute-done | bytes 524320 | tf_op jit(solution)/shard_map/ppermute | solution.py:92
  235.7 12.8 %collective-permute-done.16.refs_2_ = bf16[128,2048]{1,0:T(8,128)(2,1)S(1)} collective-permute-done((bf16[128,2048]{1,0:T(8,128)(2,1)S(1)}, bf16[128,2048]{1,0:T(8,128)(2,1)S(1)}, u32[]{:S(2)}, u32[]{:S(2)}) %collective-permute-start.16) | collective-permute-done | bytes 524320 | tf_op jit(solution)/shard_map/ppermute | solution.py:92
  253.1 11.5 %attend_back.1 = (bf16[1024,512]{1,0:T(8,128)(2,1)S(1)}, bf16[512,1536]{1,0:T(8,128)(2,1)S(1)}, bf16[512,1536]{1,0:T(8,128)(2,1)S(1)}) custom-call(s32[9]{0:T(128)S(1)} %pad_add_fusion.where, bf16[128,2048]{1,0:T(8,128)(2,1)S(1)} %get-tuple-element.186.refs_0_, bf16[128,2048]{1,0:T(8,128)(2,1)S(1)} %collective-permute-done.15.refs_1_, ...), custom_call_target="tpu_custom_call" | custom-call | flops 9663676416 | bytes 4194304 | tf_op jit(solution)/shard_map/attend_back/pallas_call | solution.py:245
  271.9 6.6 %head_grads.1 = bf16[16,192,512]{2,1,0:T(8,128)(2,1)} custom-call(bf16[128,2048]{1,0:T(8,128)(2,1)} %copy-done.1, bf16[128,2048]{1,0:T(8,128)(2,1)} %copy-done.11, bf16[128,2048]{1,0:T(8,128)(2,1)} %copy-done.10, bf16[128,2048]{1,0:T(8,128)(2,1)} %copy-done.9, bf16[128,2048]{1,0:T(8,128)(2,1)} %copy-done.12, bf16[128,2048]{1,0:T(8,128)(2,1)} %copy-done.13, ...), custom_call_target="tpu_custom_call" | custom-call | flops 2147483648 | bytes 9437184 | tf_op jit(solution)/shard_map/head_grads/pallas_call | solution.py:598
  280.3 8.7 %collective-permute-done.25 = bf16[128,1536]{1,0:T(8,128)(2,1)S(1)} collective-permute-done((bf16[128,1536]{1,0:T(8,128)(2,1)S(1)}, bf16[128,1536]{1,0:T(8,128)(2,1)S(1)}, u32[]{:S(2)}, u32[]{:S(2)}) %collective-permute-start.25) | collective-permute-done | bytes 393248 | tf_op jit(solution)/shard_map/ppermute | solution.py:92
  298.0 5.1 %collective-permute-done.29.refs_11_ = bf16[128,1536]{1,0:T(8,128)(2,1)S(1)} collective-permute-done((bf16[128,1536]{1,0:T(8,128)(2,1)S(1)}, bf16[128,1536]{1,0:T(8,128)(2,1)S(1)}, u32[]{:S(2)}, u32[]{:S(2)}) %collective-permute-start.29) | collective-permute-done | bytes 393248 | tf_op jit(solution)/shard_map/ppermute | solution.py:92
  303.1 10.0 %collective-permute-done.28.refs_10_ = bf16[128,1536]{1,0:T(8,128)(2,1)S(1)} collective-permute-done((bf16[128,1536]{1,0:T(8,128)(2,1)S(1)}, bf16[128,1536]{1,0:T(8,128)(2,1)S(1)}, u32[]{:S(2)}, u32[]{:S(2)}) %collective-permute-start.28) | collective-permute-done | bytes 393248 | tf_op jit(solution)/shard_map/ppermute | solution.py:92
  320.3 22.4 %all_to_all.32.parts = bf16[16,208,128]{2,1,0:T(8,128)(2,1)S(1)} all-to-all(bf16[16,208,128]{2,1,0:T(8,128)(2,1)S(1)} %shared_parts.1), channel_id=1, replica_groups=mesh['dp'=16,'heads'=8] {'dp'}, dimensions={0} | all-to-all | bytes 1703936 | tf_op jit(solution)/shard_map/all_to_all | solution.py:157
  350.7 9.9 %all-to-all-done.2.refs_0_ = bf16[16,192,128]{2,1,0:T(8,128)(2,1)S(1)} async-done(((bf16[16,192,128]{2,1,0:T(8,128)(2,1)}), bf16[16,192,128]{2,1,0:T(8,128)(2,1)S(1)}, u32[]{:S(2)}, u32[]{:S(2)}) %all-to-all-start.2) | async-done | bytes 786464 | tf_op jit(solution)/shard_map/all_to_all | solution.py:157
  394.1 5.8 %collective-permute-done.39.refs_2_ = bf16[384,256]{1,0:T(8,128)(2,1)S(1)} collective-permute-done((bf16[384,256]{1,0:T(8,128)(2,1)S(1)}, bf16[384,256]{1,0:T(8,128)(2,1)S(1)}, u32[]{:S(2)}, u32[]{:S(2)}) %collective-permute-start.39) | collective-permute-done | bytes 196640 | tf_op jit(solution)/shard_map/ppermute | solution.py:92
  400.5 7.3 %all-to-all-done.3.parts = bf16[16,384,128]{2,1,0:T(8,128)(2,1)S(1)} async-done(((bf16[16,384,128]{2,1,0:T(8,128)(2,1)}), bf16[16,384,128]{2,1,0:T(8,128)(2,1)S(1)}, u32[]{:S(2)}, u32[]{:S(2)}) %all-to-all-start.3) | async-done | bytes 1572896 | tf_op jit(solution)/shard_map/all_to_all | solution.py:157
  425.1 21.4 %shared_updates.1 = (f32[16,1024]{1,0:T(8,128)}, f32[16,256]{1,0:T(8,128)}, f32[16,256]{1,0:T(8,128)}) custom-call(s32[8]{0:T(128)S(1)} %fusion.34.refs_0_.owner, bf16[384,256]{1,0:T(8,128)(2,1)} %copy-done.66, bf16[384,256]{1,0:T(8,128)(2,1)} %collective-permute-done.38.refs_1_, bf16[384,256]{1,0:T(8,128)(2,1)} %copy-done.76, bf16[384,256]{1,0:T(8,128)(2,1)} %copy-done.75, ...), custom_call_target="tpu_custom_call" | custom-call | flops 21474836480 | bytes 8388608 | tf_op jit(solution)/shard_map/shared_updates/pallas_call | solution.py:245
  449.1 13.4 %block_updates.1 = (f32[704,128]{1,0:T(8,128)}, f32[704,128]{1,0:T(8,128)}, f32[704,128]{1,0:T(8,128)}, f32[64,512]{1,0:T(8,128)}, f32[128,512]{1,0:T(8,128)}) custom-call(s32[1]{0:T(128)} %bitcast.28.rank, bf16[16,384,128]{2,1,0:T(8,128)(2,1)S(1)} %all-to-all-done.4.refs_0_, f32[704,128]{1,0:T(8,128)} %get-tuple-element.265.refs_1_, ...), custom_call_target="tpu_custom_call" | custom-call | flops 2818572288 | bytes 4423680 | tf_op jit(solution)/shard_map/block_updates/pallas_call | solution.py:891
  (335 shorter events, 164.8 us)
Async XLA Ops:
  7.2 42.0 %all-gather.3.cloned.1.call-start = ((), (), s32[]{:S(2)}) async-start(), calls=%async_computation.7 | async-start | bytes 3538944 | tf_op jit(solution)/shard_map/all_gather | solution.py:1152
  17.7 123.8 %all-gather.5.cloned.1.call-start = ((), (), s32[]{:S(2)}) async-start(), calls=%async_computation.8 | async-start | bytes 4718592 | tf_op jit(solution)/shard_map/all_gather | solution.py:1155
  54.3 293.9 %reduce-scatter.7.cloned.1.call-start = ((), (), s32[]{:S(2)}) async-start(), calls=%async_computation.9 | async-start | bytes 9191424
  82.0 24.8 %collective-permute-start.2 = (bf16[128,2048]{1,0:T(8,128)(2,1)S(1)}, bf16[128,2048]{1,0:T(8,128)(2,1)S(1)}, u32[]{:S(2)}, u32[]{:S(2)}) collective-permute-start(bf16[128,2048]{1,0:T(8,128)(2,1)S(1)} %get-tuple-element.159), channel_id=1, source_target_pairs={{0,4},{1,5},{2,6},{3,7},{4,0},{5,1},{6,2},{7,3},{8,12},{9,13},{10,... | collective-permute-start | bytes 1572872 | tf_op jit(solution)/shard_map/ppermute | solution.py:92
  83.8 23.8 %collective-permute-start.3 = (bf16[128,2048]{1,0:T(8,128)(2,1)S(1)}, bf16[128,2048]{1,0:T(8,128)(2,1)S(1)}, u32[]{:S(2)}, u32[]{:S(2)}) collective-permute-start(bf16[128,2048]{1,0:T(8,128)(2,1)S(1)} %get-tuple-element.160), channel_id=1, source_target_pairs={{0,6},{1,7},{2,0},{3,1},{4,2},{5,3},{6,4},{7,5},{8,14},{9,15},{10,... | collective-permute-start | bytes 1572872 | tf_op jit(solution)/shard_map/ppermute | solution.py:92
  109.5 25.8 %collective-permute-start.5 = (bf16[128,2048]{1,0:T(8,128)(2,1)S(1)}, bf16[128,2048]{1,0:T(8,128)(2,1)S(1)}, u32[]{:S(2)}, u32[]{:S(2)}) collective-permute-start(bf16[128,2048]{1,0:T(8,128)(2,1)S(1)} %multiply_convert_fusion.refs_2_.refs_0_), channel_id=1, source_target_pairs={{0,4},{1,5},{2,6},{3,7},{4,0},{5,1},{6,2},{7,3},{8,12},{9,13},{10,... | collective-permute-start | bytes 1572872 | tf_op jit(solution)/shard_map/ppermute | solution.py:92
  112.7 22.6 %collective-permute-start.4 = (bf16[128,2048]{1,0:T(8,128)(2,1)S(1)}, bf16[128,2048]{1,0:T(8,128)(2,1)S(1)}, u32[]{:S(2)}, u32[]{:S(2)}) collective-permute-start(bf16[128,2048]{1,0:T(8,128)(2,1)S(1)} %multiply_convert_fusion.refs_2_.refs_0_), channel_id=1, source_target_pairs={{0,6},{1,7},{2,0},{3,1},{4,2},{5,3},{6,4},{7,5},{8,14},{9,15},{10,... | collective-permute-start | bytes 1572872 | tf_op jit(solution)/shard_map/ppermute | solution.py:92
  184.0 186.5 %reduce-scatter.9.cloned.1.call-start = ((), (), s32[]{:S(2)}) async-start(), calls=%async_computation.10 | async-start | bytes 3342336
  188.8 28.4 %collective-permute-start.18 = (bf16[512,2048]{1,0:T(8,128)(2,1)S(1)}, bf16[512,2048]{1,0:T(8,128)(2,1)S(1)}, u32[]{:S(2)}, u32[]{:S(2)}) collective-permute-start(bf16[512,2048]{1,0:T(8,128)(2,1)S(1)} %convolution_convert_fusion.1), channel_id=1, source_target_pairs={{0,1},{1,0},{2,3},{3,2},{4,5},{5,4},{6,7},{7,6},{8,9},{9,8},{10,11... | collective-permute-start | bytes 6291464 | tf_op jit(solution)/shard_map/ppermute | solution.py:92
  189.0 25.9 %collective-permute-start.13 = (bf16[128,2048]{1,0:T(8,128)(2,1)S(1)}, bf16[128,2048]{1,0:T(8,128)(2,1)S(1)}, u32[]{:S(2)}, u32[]{:S(2)}) collective-permute-start(bf16[128,2048]{1,0:T(8,128)(2,1)S(1)} %get-tuple-element.170), channel_id=1, source_target_pairs={{0,4},{1,5},{2,6},{3,7},{4,0},{5,1},{6,2},{7,3},{8,12},{9,13},{10,... | collective-permute-start | bytes 1572872 | tf_op jit(solution)/shard_map/ppermute | solution.py:92
  192.0 23.0 %collective-permute-start.14 = (bf16[128,2048]{1,0:T(8,128)(2,1)S(1)}, bf16[128,2048]{1,0:T(8,128)(2,1)S(1)}, u32[]{:S(2)}, u32[]{:S(2)}) collective-permute-start(bf16[128,2048]{1,0:T(8,128)(2,1)S(1)} %get-tuple-element.171), channel_id=1, source_target_pairs={{0,6},{1,7},{2,0},{3,1},{4,2},{5,3},{6,4},{7,5},{8,14},{9,15},{10,... | collective-permute-start | bytes 1572872 | tf_op jit(solution)/shard_map/ppermute | solution.py:92
  220.4 15.3 %collective-permute-start.17 = (bf16[128,2048]{1,0:T(8,128)(2,1)S(1)}, bf16[128,2048]{1,0:T(8,128)(2,1)S(1)}, u32[]{:S(2)}, u32[]{:S(2)}) collective-permute-start(bf16[128,2048]{1,0:T(8,128)(2,1)S(1)} %get-tuple-element.186.refs_0_), channel_id=1, source_target_pairs={{0,2},{1,3},{2,4},{3,5},{4,6},{5,7},{6,0},{7,1},{8,10},{9,11},{10,... | collective-permute-start | bytes 1572872 | tf_op jit(solution)/shard_map/ppermute | solution.py:92
  221.5 27.0 %collective-permute-start.16 = (bf16[128,2048]{1,0:T(8,128)(2,1)S(1)}, bf16[128,2048]{1,0:T(8,128)(2,1)S(1)}, u32[]{:S(2)}, u32[]{:S(2)}) collective-permute-start(bf16[128,2048]{1,0:T(8,128)(2,1)S(1)} %get-tuple-element.186.refs_0_), channel_id=1, source_target_pairs={{0,4},{1,5},{2,6},{3,7},{4,0},{5,1},{6,2},{7,3},{8,12},{9,13},{10,... | collective-permute-start | bytes 1572872 | tf_op jit(solution)/shard_map/ppermute | solution.py:92
  225.1 23.4 %collective-permute-start.15 = (bf16[128,2048]{1,0:T(8,128)(2,1)S(1)}, bf16[128,2048]{1,0:T(8,128)(2,1)S(1)}, u32[]{:S(2)}, u32[]{:S(2)}) collective-permute-start(bf16[128,2048]{1,0:T(8,128)(2,1)S(1)} %get-tuple-element.186.refs_0_), channel_id=1, source_target_pairs={{0,6},{1,7},{2,0},{3,1},{4,2},{5,3},{6,4},{7,5},{8,14},{9,15},{10,... | collective-permute-start | bytes 1572872 | tf_op jit(solution)/shard_map/ppermute | solution.py:92
  268.8 20.2 %collective-permute-start.25 = (bf16[128,1536]{1,0:T(8,128)(2,1)S(1)}, bf16[128,1536]{1,0:T(8,128)(2,1)S(1)}, u32[]{:S(2)}, u32[]{:S(2)}) collective-permute-start(bf16[128,1536]{1,0:T(8,128)(2,1)S(1)} %get-tuple-element.196), channel_id=1, source_target_pairs={{0,4},{1,5},{2,6},{3,7},{4,0},{5,1},{6,2},{7,3},{8,12},{9,13},{10,... | collective-permute-start | bytes 1179656 | tf_op jit(solution)/shard_map/ppermute | solution.py:92
  271.8 17.3 %collective-permute-start.26 = (bf16[128,1536]{1,0:T(8,128)(2,1)S(1)}, bf16[128,1536]{1,0:T(8,128)(2,1)S(1)}, u32[]{:S(2)}, u32[]{:S(2)}) collective-permute-start(bf16[128,1536]{1,0:T(8,128)(2,1)S(1)} %get-tuple-element.197), channel_id=1, source_target_pairs={{0,6},{1,7},{2,0},{3,1},{4,2},{5,3},{6,4},{7,5},{8,14},{9,15},{10,... | collective-permute-start | bytes 1179656 | tf_op jit(solution)/shard_map/ppermute | solution.py:92
  292.4 20.7 %collective-permute-start.28 = (bf16[128,1536]{1,0:T(8,128)(2,1)S(1)}, bf16[128,1536]{1,0:T(8,128)(2,1)S(1)}, u32[]{:S(2)}, u32[]{:S(2)}) collective-permute-start(bf16[128,1536]{1,0:T(8,128)(2,1)S(1)} %pad_maximum_fusion.2.refs_8_), channel_id=1, source_target_pairs={{0,4},{1,5},{2,6},{3,7},{4,0},{5,1},{6,2},{7,3},{8,12},{9,13},{10,... | collective-permute-start | bytes 1179656 | tf_op jit(solution)/shard_map/ppermute | solution.py:92
  296.0 17.2 %collective-permute-start.27 = (bf16[128,1536]{1,0:T(8,128)(2,1)S(1)}, bf16[128,1536]{1,0:T(8,128)(2,1)S(1)}, u32[]{:S(2)}, u32[]{:S(2)}) collective-permute-start(bf16[128,1536]{1,0:T(8,128)(2,1)S(1)} %pad_maximum_fusion.2.refs_8_), channel_id=1, source_target_pairs={{0,6},{1,7},{2,0},{3,1},{4,2},{5,3},{6,4},{7,5},{8,14},{9,15},{10,... | collective-permute-start | bytes 1179656 | tf_op jit(solution)/shard_map/ppermute | solution.py:92
  344.5 16.1 %all-to-all-start.2 = ((bf16[16,192,128]{2,1,0:T(8,128)(2,1)}), bf16[16,192,128]{2,1,0:T(8,128)(2,1)S(1)}, u32[]{:S(2)}, u32[]{:S(2)}) async-start(bf16[16,192,128]{2,1,0:T(8,128)(2,1)} %get-tuple-element.206), calls=%async_computation.2 | async-start | bytes 1572864 | tf_op jit(solution)/shard_map/all_to_all | solution.py:157
  381.9 25.9 %all-to-all-start.3 = ((bf16[16,384,128]{2,1,0:T(8,128)(2,1)}), bf16[16,384,128]{2,1,0:T(8,128)(2,1)S(1)}, u32[]{:S(2)}, u32[]{:S(2)}) async-start(bf16[16,384,128]{2,1,0:T(8,128)(2,1)} %pad_maximum_fusion), calls=%async_computation.3 | async-start | bytes 3145728 | tf_op jit(solution)/shard_map/all_to_all | solution.py:157
  416.3 32.7 %all-to-all-start.4 = ((bf16[16,384,128]{2,1,0:T(8,128)(2,1)}), bf16[16,384,128]{2,1,0:T(8,128)(2,1)S(1)}, u32[]{:S(2)}, u32[]{:S(2)}) async-start(bf16[16,384,128]{2,1,0:T(8,128)(2,1)} %panel_sums.1), calls=%async_computation.4 | async-start | bytes 3145728 | tf_op jit(solution)/shard_map/all_to_all | solution.py:157
  420.1 26.5 %collective-permute-start.45 = (bf16[128,2048]{1,0:T(8,128)(2,1)S(1)}, bf16[128,2048]{1,0:T(8,128)(2,1)S(1)}, u32[]{:S(2)}, u32[]{:S(2)}) collective-permute-start(bf16[128,2048]{1,0:T(8,128)(2,1)S(1)} %copy-done.64), channel_id=1, source_target_pairs={{0,2},{1,3},{2,4},{3,5},{4,6},{5,7},{6,0},{7,1},{8,10},{9,11},{10,... | collective-permute-start | bytes 1572872 | tf_op jit(solution)/shard_map/ppermute | solution.py:92
  421.6 26.3 %collective-permute-start.46 = (bf16[128,2048]{1,0:T(8,128)(2,1)S(1)}, bf16[128,2048]{1,0:T(8,128)(2,1)S(1)}, u32[]{:S(2)}, u32[]{:S(2)}) collective-permute-start(bf16[128,2048]{1,0:T(8,128)(2,1)S(1)} %copy-done.63), channel_id=1, source_target_pairs={{0,4},{1,5},{2,6},{3,7},{4,0},{5,1},{6,2},{7,3},{8,12},{9,13},{10,... | collective-permute-start | bytes 1572872 | tf_op jit(solution)/shard_map/ppermute | solution.py:92
  425.1 22.7 %collective-permute-start.47 = (bf16[128,2048]{1,0:T(8,128)(2,1)S(1)}, bf16[128,2048]{1,0:T(8,128)(2,1)S(1)}, u32[]{:S(2)}, u32[]{:S(2)}) collective-permute-start(bf16[128,2048]{1,0:T(8,128)(2,1)S(1)} %copy-done.62), channel_id=1, source_target_pairs={{0,6},{1,7},{2,0},{3,1},{4,2},{5,3},{6,4},{7,5},{8,14},{9,15},{10,... | collective-permute-start | bytes 1572872 | tf_op jit(solution)/shard_map/ppermute | solution.py:92
  (112 other events, 1403.4 us)
Sparse Core Ops, SparseCore 0:
  17.9 31.3 all-gather.2
  51.0 32.1 all-gather.4
  184.1 84.6 reduce-scatter.6
  289.4 80.1 reduce-scatter.8

commit v6 on v5

--- a/solution.py
+++ b/solution.py
@@ -1163,9 +1163,7 @@
         tiled=True,
     )
     shared_rows = [own_rows(weight, all_count, all_rank) for weight in (w_q_down, w_key, w_value)]
-    packed, normed_parts, shared_rows = lax.optimization_barrier(
-        (packed, normed_parts, shared_rows)
-    )
+    packed, normed_parts = lax.optimization_barrier((packed, normed_parts))
     row_ids, row_pos = segment_info(starts, whole_index)
     row_cos, row_sin = rotary_tables(row_pos, head_dim)
     query_rows, attended_near, attended_far, lse = attend(
@@ -1179,6 +1177,7 @@
             )
         )
     )
+    attn_mixed, shared_rows = lax.optimization_barrier((attn_mixed, shared_rows))
     hidden_one = inputs + attn_mixed
     scale_two = rms_scale(hidden_one)
     normed_two = (hidden_one * scale_two * gain_two).astype(low_type)
@@ -1201,15 +1200,13 @@
         dp_count,
     )
     ffn_sums = lax.psum_scatter(ffn_part, "dp", scatter_dimension=0, tiled=True)[0]
-    mixed_far = matmul_tn(after(middle_far, *chip_two), down_turned).astype(low_type)
-    mixed_near = matmul_tn(after(middle_near, *chip_two), down_turned).astype(low_type)
     hidden_part, gain_two_grad = norm_back(hidden_one, scale_two, gain_two, normed_two_back)
     hidden_back = cotangent.astype(jnp.float32) + hidden_part
 
-    hidden_low = after(hidden_back.astype(low_type), ffn_part, mixed_far, mixed_near)
-    pieces_hidden, *chip_mixed = gather_heads(
-        hidden_low, tuple(ring_operands(chip_sums(mixed_far, mixed_near)))
-    )
+    hidden_low = after(hidden_back.astype(low_type), ffn_part)
+    mixed_far = matmul_tn(after(middle_far, hidden_low), down_turned).astype(low_type)
+    mixed_near = matmul_tn(after(middle_near, hidden_low), down_turned).astype(low_type)
+    pieces_hidden, mixed_far, mixed_near = gather_heads(hidden_low, (mixed_far, mixed_near))
     q_up_part, sums_near, sums_far = attend_back(
         where, pieces_hidden, query_rows, packed, w_out, w_q_up, lse, row_cos, row_sin, row_ids
     )
@@ -1218,7 +1215,7 @@
     head_parts = head_grads(
         pieces_hidden, (after(attended_near, *chip_back), attended_far), q_up_part, dp_count
     )
-    packed_sums, head_parts = lax.optimization_barrier((packed_sums, head_parts))
+    packed_sums = after(packed_sums, head_parts)
     head_sums = lax.psum_scatter(head_parts, "dp", scatter_dimension=0, tiled=True)[0]
     latent_back = packed_sums[:, :latent_width]
     key_sum = packed_sums[:, latent_width : latent_width + head_dim]
@@ -1232,7 +1229,9 @@
 
     back_low = jnp.concatenate([latent_raw_back, key_pre_back, values_low], axis=1)
     latent_out = matmul_nt(latent_raw_back, w_q_down)
-    pieces_back, latent_out = gather_heads(back_low, (latent_out,))
+    pieces_back, latent_out, *chip_mixed = gather_heads(
+        back_low, (latent_out, *ring_operands(chip_sums(mixed_far, mixed_near)))
+    )
     normed_one_back = (
         latent_out
         + matmul_nt(key_pre_back, w_key)
@@ -1278,9 +1277,8 @@
         ],
         axis=1,
     )
-    pieces_gram, panels = gather_heads(
-        gram_sums[:gram_chunk].astype(low_type), (exchange_dp(panels),)
-    )
+    panels = exchange_dp(panels)
+    pieces_gram = gather_heads(gram_sums[:gram_chunk].astype(low_type))
     panels = panel_sums(panels)
     pieces_gram, panels, chip_mixed = lax.optimization_barrier((pieces_gram, panels, chip_mixed))
     panels = exchange_dp(panels)

time: 478 us -> 473 us (0.990)
  starting transfers between devices: 65.5 us -> 44.7 us
  other arithmetic: 18.1 us -> 26.6 us
  local copies, waits for them, and re-layouts: 23.5 us -> 32 us
    ppermute x48, starting transfers between devices: 50.6 us -> 26.9 us  [shift_heads(): return lax.ppermute(values, 'heads', pairs)]
    ppermute x48, waiting for transfers between devices: 146 us -> 160 us  [shift_heads(): return lax.ppermute(values, 'heads', pairs)]
    all_gather x1, waiting for transfers between devices: 31.5 us -> 23.2 us  [on_device(): lax.all_gather(jnp.concatenate([latent_normed, key_local, value_local], a...]
    unnamed x161 -> x169, local copies, waits for them, and re-layouts: 14.1 us -> 17.8 us
  transfers between devices with their start and end apart: 56 -> 56, of which waited for: 32 -> 41; matrix products, arithmetic and copies ran while one was open for 7% -> 9% of each run, Pallas kernels for 14% -> 14%
where the time goes in v6:
time: 473 us; the launch traced here: 464 us
  waiting for transfers between devices  201 us (42%)
  Pallas kernels  107 us (23%)
  starting transfers between devices  44.7 us (9%)
  local copies, waits for them, and re-layouts  32 us (7%)
  other arithmetic  26.6 us (6%)
  blocking collectives  22.2 us (5%)
  between operations  15.3 us (3%)
  matrix products  14.6 us (3%)
    ppermute x48, waiting for transfers between devices, shift_heads(): return lax.ppermute(values, 'heads', pairs)  160 us
    pallas_call x8, Pallas kernels, whole_call(): pl.pallas_call(body, in_specs=[pl.BlockSpec(memory_space=pltpu.SMEM)] * l...  44.1 us
    ppermute x48, starting transfers between devices, shift_heads(): return lax.ppermute(values, 'heads', pairs)  26.9 us
    pallas_call x2, Pallas kernels, streamed_call(): pl.pallas_call(wrapped, grid_spec=pltpu.PrefetchScalarGridSpec(num_scalar...  24.6 us
    all_gather x1, waiting for transfers between devices, on_device(): lax.all_gather(jnp.concatenate([latent_normed, key_local, value_local], a...  23.2 us
    all_to_all x1, blocking collectives, exchange_dp(): return lax.all_to_all(parts, 'dp', split_axis=0, concat_axis=0, tiled=True)  22.2 us
    all_to_all x3, waiting for transfers between devices, exchange_dp(): return lax.all_to_all(parts, 'dp', split_axis=0, concat_axis=0, tiled=True)  18 us
    unnamed x169, local copies, waits for them, and re-layouts  17.8 us
  transfers between devices with their start and end apart: 56, of which 41 were waited for; matrix products, arithmetic and copies ran while one was open for 9% of the time, Pallas kernels for 14%

profile of v6, /device:TPU:1, one launch (start us, length us, event | category | flops | bytes accessed | tf_op | source)
XLA Modules:
  0.0 463.5 jit_solution(10567347898732094556)
XLA Ops:
  25.9 23.2 %all-gather.3.cloned.1.call-done.packed.refs_9_ = bf16[1024,1536]{1,0:T(8,128)(2,1)} async-done(((bf16[128,1536]{1,0:T(8,128)(2,1)}), bf16[1024,1536]{1,0:T(8,128)(2,1)}) %all-gather.3.cloned.1.call-update) | async-done | bytes 3145744 | tf_op jit(solution)/shard_map/all_gather | solution.py:1152
  59.4 6.4 %attend.1 = (bf16[1024,512]{1,0:T(8,128)(2,1)S(1)}, bf16[512,512]{1,0:T(8,128)(2,1)S(1)}, bf16[512,512]{1,0:T(8,128)(2,1)S(1)}, f32[2,1024,1]{2,1,0:T(8,128)S(1)}) custom-call(s32[9]{0:T(128)S(1)} %pad_add_fusion.where, bf16[1024,1536]{1,0:T(8,128)(2,1)S(1)} %copy-done.32, bf16[1024,512]{1,0:T(8,128)(2,1)S(1)} %copy-done.5, f32[1024,128]{1,0:T(8,128)S(1)} %copy-done.21, ...), custom_call_target="tpu_custom_call" | custom-call | flops 3221225472 | bytes 4194304 | tf_op jit(solution)/shard_map/attend/pallas_call | solution.py:245
  81.7 10.2 %collective-permute-done.3 = bf16[128,2048]{1,0:T(8,128)(2,1)} collective-permute-done((bf16[128,2048]{1,0:T(8,128)(2,1)}, bf16[128,2048]{1,0:T(8,128)(2,1)}, u32[]{:S(2)}, u32[]{:S(2)}) %collective-permute-start.3) | collective-permute-done | bytes 524320 | tf_op jit(solution)/shard_map/ppermute | solution.py:92
  92.7 11.7 %collective-permute-done.1 = bf16[128,2048]{1,0:T(8,128)(2,1)} collective-permute-done((bf16[128,2048]{1,0:T(8,128)(2,1)}, bf16[128,2048]{1,0:T(8,128)(2,1)}, u32[]{:S(2)}, u32[]{:S(2)}) %collective-permute-start.1) | collective-permute-done | bytes 524320 | tf_op jit(solution)/shard_map/ppermute | solution.py:92
  109.1 10.8 %collective-permute-done.4.refs_3_.refs_1_ = bf16[128,2048]{1,0:T(8,128)(2,1)S(1)} collective-permute-done((bf16[128,2048]{1,0:T(8,128)(2,1)S(1)}, bf16[128,2048]{1,0:T(8,128)(2,1)S(1)}, u32[]{:S(2)}, u32[]{:S(2)}) %collective-permute-start.4) | collective-permute-done | bytes 524320 | tf_op jit(solution)/shard_map/ppermute | solution.py:92
  121.9 12.5 %collective-permute-done.6.refs_5_.refs_3_ = bf16[128,2048]{1,0:T(8,128)(2,1)S(1)} collective-permute-done((bf16[128,2048]{1,0:T(8,128)(2,1)S(1)}, bf16[128,2048]{1,0:T(8,128)(2,1)S(1)}, u32[]{:S(2)}, u32[]{:S(2)}) %collective-permute-start.6) | collective-permute-done | bytes 524320 | tf_op jit(solution)/shard_map/ppermute | solution.py:92
  141.4 12.3 %ffn_far.1 = (bf16[704,512]{1,0:T(8,128)(2,1)S(1)}, bf16[704,512]{1,0:T(8,128)(2,1)S(1)}, bf16[704,512]{1,0:T(8,128)(2,1)S(1)}, bf16[512,2048]{1,0:T(8,128)(2,1)S(1)}) custom-call(s32[8]{0:T(128)S(1)} %fusion.34.refs_0_.owner, bf16[704,2048]{1,0:T(8,128)(2,1)S(1)} %bitcast.54, bf16[128,2048]{1,0:T(8,128)(2,1)} %copy-done.81, bf16[128,2048]{1,0:T(8,128)(2,1)} %copy-done.82, ...), custom_call_target="tpu_custom_call" | custom-call | flops 7381975040 | bytes 14942208 | tf_op jit(solution)/shard_map/ffn_far/pallas_call | solution.py:225
  154.1 12.3 %ffn_near.1 = (bf16[704,512]{1,0:T(8,128)(2,1)S(1)}, bf16[704,512]{1,0:T(8,128)(2,1)S(1)}, bf16[704,512]{1,0:T(8,128)(2,1)S(1)}, bf16[512,2048]{1,0:T(8,128)(2,1)S(1)}) custom-call(s32[8]{0:T(128)S(1)} %fusion.34.refs_0_.owner, bf16[704,2048]{1,0:T(8,128)(2,1)S(1)} %bitcast.55, bf16[128,2048]{1,0:T(8,128)(2,1)} %copy-done.60, bf16[128,2048]{1,0:T(8,128)(2,1)} %copy-done.78, ...), custom_call_target="tpu_custom_call" | custom-call | flops 7381975040 | bytes 14942208 | tf_op jit(solution)/shard_map/ffn_near/pallas_call | solution.py:225
  168.7 15.2 %ffn_grads.1 = bf16[16,2112,128]{2,1,0:T(8,128)(2,1)} custom-call(s32[8]{0:T(128)S(1)} %fusion.34.refs_0_.owner, bf16[128,2048]{1,0:T(8,128)(2,1)} %copy-done.60, bf16[128,2048]{1,0:T(8,128)(2,1)} %copy-done.78, bf16[128,2048]{1,0:T(8,128)(2,1)} %copy-done.79, bf16[128,2048]{1,0:T(8,128)(2,1)} %copy-done.80, bf16[128,2048]{1,0:T(8,128)(2,1)} %copy-done.81, ...), custom_call_target="tpu_custom_call" | custom-call | flops 8858370048 | bytes 17039360 | tf_op jit(solution)/shard_map/ffn_grads/pallas_call | solution.py:559
  186.3 11.4 %collective-permute-done.14 = bf16[128,2048]{1,0:T(8,128)(2,1)S(1)} collective-permute-done((bf16[128,2048]{1,0:T(8,128)(2,1)}, bf16[128,2048]{1,0:T(8,128)(2,1)S(1)}, u32[]{:S(2)}, u32[]{:S(2)}) %collective-permute-start.14) | collective-permute-done | bytes 524320 | tf_op jit(solution)/shard_map/ppermute | solution.py:92
  199.4 12.1 %collective-permute-done.12 = bf16[128,2048]{1,0:T(8,128)(2,1)S(1)} collective-permute-done((bf16[128,2048]{1,0:T(8,128)(2,1)}, bf16[128,2048]{1,0:T(8,128)(2,1)S(1)}, u32[]{:S(2)}, u32[]{:S(2)}) %collective-permute-start.12) | collective-permute-done | bytes 524320 | tf_op jit(solution)/shard_map/ppermute | solution.py:92
  221.4 7.4 %collective-permute-done.15.refs_1_ = bf16[128,2048]{1,0:T(8,128)(2,1)S(1)} collective-permute-done((bf16[128,2048]{1,0:T(8,128)(2,1)S(1)}, bf16[128,2048]{1,0:T(8,128)(2,1)S(1)}, u32[]{:S(2)}, u32[]{:S(2)}) %collective-permute-start.15) | collective-permute-done | bytes 524320 | tf_op jit(solution)/shard_map/ppermute | solution.py:92
  229.5 12.6 %collective-permute-done.17.refs_3_ = bf16[128,2048]{1,0:T(8,128)(2,1)S(1)} collective-permute-done((bf16[128,2048]{1,0:T(8,128)(2,1)S(1)}, bf16[128,2048]{1,0:T(8,128)(2,1)S(1)}, u32[]{:S(2)}, u32[]{:S(2)}) %collective-permute-start.17) | collective-permute-done | bytes 524320 | tf_op jit(solution)/shard_map/ppermute | solution.py:92
  246.5 11.3 %attend_back.1 = (bf16[1024,512]{1,0:T(8,128)(2,1)S(1)}, bf16[512,1536]{1,0:T(8,128)(2,1)S(1)}, bf16[512,1536]{1,0:T(8,128)(2,1)S(1)}) custom-call(s32[9]{0:T(128)S(1)} %pad_add_fusion.where, bf16[128,2048]{1,0:T(8,128)(2,1)S(1)} %get-tuple-element.184.refs_0_, bf16[128,2048]{1,0:T(8,128)(2,1)S(1)} %collective-permute-done.15.refs_1_, ...), custom_call_target="tpu_custom_call" | custom-call | flops 9663676416 | bytes 4194304 | tf_op jit(solution)/shard_map/attend_back/pallas_call | solution.py:245
  265.0 6.7 %head_grads.1 = bf16[16,192,512]{2,1,0:T(8,128)(2,1)} custom-call(bf16[128,2048]{1,0:T(8,128)(2,1)} %copy-done.3, bf16[128,2048]{1,0:T(8,128)(2,1)} %copy-done.10, bf16[128,2048]{1,0:T(8,128)(2,1)} %copy-done.11, bf16[128,2048]{1,0:T(8,128)(2,1)} %copy-done.12, bf16[128,2048]{1,0:T(8,128)(2,1)} %copy-done.13, bf16[128,2048]{1,0:T(8,128)(2,1)} %copy-done.14, ...), custom_call_target="tpu_custom_call" | custom-call | flops 2147483648 | bytes 9437184 | tf_op jit(solution)/shard_map/head_grads/pallas_call | solution.py:598
  275.7 9.4 %collective-permute-done.23 = bf16[128,1536]{1,0:T(8,128)(2,1)} collective-permute-done((bf16[128,1536]{1,0:T(8,128)(2,1)}, bf16[128,1536]{1,0:T(8,128)(2,1)}, u32[]{:S(2)}, u32[]{:S(2)}) %collective-permute-start.23) | collective-permute-done | bytes 393248 | tf_op jit(solution)/shard_map/ppermute | solution.py:92
  291.0 6.6 %collective-permute-done.26.refs_9_ = bf16[128,1536]{1,0:T(8,128)(2,1)S(1)} collective-permute-done((bf16[128,1536]{1,0:T(8,128)(2,1)S(1)}, bf16[128,1536]{1,0:T(8,128)(2,1)S(1)}, u32[]{:S(2)}, u32[]{:S(2)}) %collective-permute-start.26) | collective-permute-done | bytes 393248 | tf_op jit(solution)/shard_map/ppermute | solution.py:92
  298.6 9.9 %collective-permute-done.28.refs_11_ = bf16[128,1536]{1,0:T(8,128)(2,1)S(1)} collective-permute-done((bf16[128,1536]{1,0:T(8,128)(2,1)S(1)}, bf16[128,1536]{1,0:T(8,128)(2,1)S(1)}, u32[]{:S(2)}, u32[]{:S(2)}) %collective-permute-start.28) | collective-permute-done | bytes 393248 | tf_op jit(solution)/shard_map/ppermute | solution.py:92
  315.1 22.2 %all_to_all.32.parts = bf16[16,208,128]{2,1,0:T(8,128)(2,1)S(1)} all-to-all(bf16[16,208,128]{2,1,0:T(8,128)(2,1)S(1)} %shared_parts.1), channel_id=1, replica_groups=mesh['dp'=16,'heads'=8] {'dp'}, dimensions={0} | all-to-all | bytes 1703936 | tf_op jit(solution)/shard_map/all_to_all | solution.py:157
  347.2 10.4 %all-to-all-done.2.refs_0_ = bf16[16,192,128]{2,1,0:T(8,128)(2,1)S(1)} async-done(((bf16[16,192,128]{2,1,0:T(8,128)(2,1)}), bf16[16,192,128]{2,1,0:T(8,128)(2,1)S(1)}, u32[]{:S(2)}, u32[]{:S(2)}) %all-to-all-start.2) | async-done | bytes 786464 | tf_op jit(solution)/shard_map/all_to_all | solution.py:157
  393.3 6.0 %collective-permute-done.40.refs_3_ = bf16[384,256]{1,0:T(8,128)(2,1)} collective-permute-done((bf16[384,256]{1,0:T(8,128)(2,1)S(1)}, bf16[384,256]{1,0:T(8,128)(2,1)}, u32[]{:S(2)}, u32[]{:S(2)}) %collective-permute-start.40) | collective-permute-done | bytes 196640 | tf_op jit(solution)/shard_map/ppermute | solution.py:92
  401.6 7.7 %all-to-all-done.3.parts = bf16[16,384,128]{2,1,0:T(8,128)(2,1)S(1)} async-done(((bf16[16,384,128]{2,1,0:T(8,128)(2,1)}), bf16[16,384,128]{2,1,0:T(8,128)(2,1)S(1)}, u32[]{:S(2)}, u32[]{:S(2)}) %all-to-all-start.3) | async-done | bytes 1572896 | tf_op jit(solution)/shard_map/all_to_all | solution.py:157
  416.8 21.4 %shared_updates.1 = (f32[16,1024]{1,0:T(8,128)}, f32[16,256]{1,0:T(8,128)}, f32[16,256]{1,0:T(8,128)}) custom-call(s32[8]{0:T(128)S(1)} %fusion.34.refs_0_.owner, bf16[384,256]{1,0:T(8,128)(2,1)} %copy-done.62, bf16[384,256]{1,0:T(8,128)(2,1)} %collective-permute-done.38.refs_1_, bf16[384,256]{1,0:T(8,128)(2,1)} %collective-permute-done.39.refs_2_, ...), custom_call_target="tpu_custom_call" | custom-call | flops 21474836480 | bytes 8388608 | tf_op jit(solution)/shard_map/shared_updates/pallas_call | solution.py:245
  443.2 13.4 %block_updates.1 = (f32[704,128]{1,0:T(8,128)}, f32[704,128]{1,0:T(8,128)}, f32[704,128]{1,0:T(8,128)}, f32[64,512]{1,0:T(8,128)}, f32[128,512]{1,0:T(8,128)}) custom-call(s32[1]{0:T(128)} %bitcast.28.rank, bf16[16,384,128]{2,1,0:T(8,128)(2,1)S(1)} %all-to-all-done.4.refs_0_, f32[704,128]{1,0:T(8,128)} %get-tuple-element.267.refs_1_, ...), custom_call_target="tpu_custom_call" | custom-call | flops 2818572288 | bytes 4423680 | tf_op jit(solution)/shard_map/block_updates/pallas_call | solution.py:891
  (346 shorter events, 165.2 us)
Async XLA Ops:
  7.2 41.9 %all-gather.3.cloned.1.call-start = ((), (), s32[]{:S(2)}) async-start(), calls=%async_computation.7 | async-start | bytes 3538944 | tf_op jit(solution)/shard_map/all_gather | solution.py:1152
  18.8 33.5 %all-to-all-start = ((bf16[8,256,128]{2,1,0:T(8,128)(2,1)}), bf16[8,256,128]{2,1,0:T(8,128)(2,1)S(1)}, u32[]{:S(2)}, u32[]{:S(2)}) async-start(bf16[8,256,128]{2,1,0:T(8,128)(2,1)} %bitcast.5), calls=%async_computation | async-start | bytes 1048576 | tf_op jit(solution)/shard_map/all_to_all | solution.py:1156
  24.8 114.8 %all-gather.5.cloned.1.call-start = ((), (), s32[]{:S(2)}) async-start(), calls=%async_computation.8 | async-start | bytes 4718592 | tf_op jit(solution)/shard_map/all_gather | solution.py:1155
  49.1 293.6 %reduce-scatter.7.cloned.1.call-start = ((), (), s32[]{:S(2)}) async-start(), calls=%async_computation.9 | async-start | bytes 9191424
  76.0 15.9 %collective-permute-start.3 = (bf16[128,2048]{1,0:T(8,128)(2,1)}, bf16[128,2048]{1,0:T(8,128)(2,1)}, u32[]{:S(2)}, u32[]{:S(2)}) collective-permute-start(bf16[128,2048]{1,0:T(8,128)(2,1)} %get-tuple-element.161), channel_id=1, source_target_pairs={{0,6},{1,7},{2,0},{3,1},{4,2},{5,3},{6,4},{7,5},{8,14},{9,15},{10,... | collective-permute-start | bytes 1572872 | tf_op jit(solution)/shard_map/ppermute | solution.py:92
  77.2 15.5 %collective-permute-start.2 = (bf16[128,2048]{1,0:T(8,128)(2,1)}, bf16[128,2048]{1,0:T(8,128)(2,1)}, u32[]{:S(2)}, u32[]{:S(2)}) collective-permute-start(bf16[128,2048]{1,0:T(8,128)(2,1)} %get-tuple-element.160), channel_id=1, source_target_pairs={{0,4},{1,5},{2,6},{3,7},{4,0},{5,1},{6,2},{7,3},{8,12},{9,13},{10,... | collective-permute-start | bytes 1572872 | tf_op jit(solution)/shard_map/ppermute | solution.py:92
  78.0 26.5 %collective-permute-start.1 = (bf16[128,2048]{1,0:T(8,128)(2,1)}, bf16[128,2048]{1,0:T(8,128)(2,1)}, u32[]{:S(2)}, u32[]{:S(2)}) collective-permute-start(bf16[128,2048]{1,0:T(8,128)(2,1)} %get-tuple-element.159), channel_id=1, source_target_pairs={{0,2},{1,3},{2,4},{3,5},{4,6},{5,7},{6,0},{7,1},{8,10},{9,11},{10,... | collective-permute-start | bytes 1572872 | tf_op jit(solution)/shard_map/ppermute | solution.py:92
  107.8 14.1 %collective-permute-start.5 = (bf16[128,2048]{1,0:T(8,128)(2,1)S(1)}, bf16[128,2048]{1,0:T(8,128)(2,1)S(1)}, u32[]{:S(2)}, u32[]{:S(2)}) collective-permute-start(bf16[128,2048]{1,0:T(8,128)(2,1)S(1)} %multiply_convert_fusion.refs_2_.refs_0_), channel_id=1, source_target_pairs={{0,4},{1,5},{2,6},{3,7},{4,0},{5,1},{6,2},{7,3},{8,12},{9,13},{10,... | collective-permute-start | bytes 1572872 | tf_op jit(solution)/shard_map/ppermute | solution.py:92
  109.1 25.4 %collective-permute-start.6 = (bf16[128,2048]{1,0:T(8,128)(2,1)S(1)}, bf16[128,2048]{1,0:T(8,128)(2,1)S(1)}, u32[]{:S(2)}, u32[]{:S(2)}) collective-permute-start(bf16[128,2048]{1,0:T(8,128)(2,1)S(1)} %multiply_convert_fusion.refs_2_.refs_0_), channel_id=1, source_target_pairs={{0,2},{1,3},{2,4},{3,5},{4,6},{5,7},{6,0},{7,1},{8,10},{9,11},{10,... | collective-permute-start | bytes 1572872 | tf_op jit(solution)/shard_map/ppermute | solution.py:92
  183.9 182.4 %reduce-scatter.9.cloned.1.call-start = ((), (), s32[]{:S(2)}) async-start(), calls=%async_computation.10 | async-start | bytes 3342336
  184.0 13.8 %collective-permute-start.14 = (bf16[128,2048]{1,0:T(8,128)(2,1)}, bf16[128,2048]{1,0:T(8,128)(2,1)S(1)}, u32[]{:S(2)}, u32[]{:S(2)}) collective-permute-start(bf16[128,2048]{1,0:T(8,128)(2,1)} %get-tuple-element.173), channel_id=1, source_target_pairs={{0,6},{1,7},{2,0},{3,1},{4,2},{5,3},{6,4},{7,5},{8,14},{9,15},{10,... | collective-permute-start | bytes 1572872 | tf_op jit(solution)/shard_map/ppermute | solution.py:92
  184.4 15.0 %collective-permute-start.13 = (bf16[128,2048]{1,0:T(8,128)(2,1)}, bf16[128,2048]{1,0:T(8,128)(2,1)S(1)}, u32[]{:S(2)}, u32[]{:S(2)}) collective-permute-start(bf16[128,2048]{1,0:T(8,128)(2,1)} %get-tuple-element.172), channel_id=1, source_target_pairs={{0,4},{1,5},{2,6},{3,7},{4,0},{5,1},{6,2},{7,3},{8,12},{9,13},{10,... | collective-permute-start | bytes 1572872 | tf_op jit(solution)/shard_map/ppermute | solution.py:92
  185.8 25.7 %collective-permute-start.12 = (bf16[128,2048]{1,0:T(8,128)(2,1)}, bf16[128,2048]{1,0:T(8,128)(2,1)S(1)}, u32[]{:S(2)}, u32[]{:S(2)}) collective-permute-start(bf16[128,2048]{1,0:T(8,128)(2,1)} %get-tuple-element.171), channel_id=1, source_target_pairs={{0,2},{1,3},{2,4},{3,5},{4,6},{5,7},{6,0},{7,1},{8,10},{9,11},{10,... | collective-permute-start | bytes 1572872 | tf_op jit(solution)/shard_map/ppermute | solution.py:92
  215.6 13.9 %collective-permute-start.16 = (bf16[128,2048]{1,0:T(8,128)(2,1)S(1)}, bf16[128,2048]{1,0:T(8,128)(2,1)S(1)}, u32[]{:S(2)}, u32[]{:S(2)}) collective-permute-start(bf16[128,2048]{1,0:T(8,128)(2,1)S(1)} %get-tuple-element.184.refs_0_), channel_id=1, source_target_pairs={{0,4},{1,5},{2,6},{3,7},{4,0},{5,1},{6,2},{7,3},{8,12},{9,13},{10,... | collective-permute-start | bytes 1572872 | tf_op jit(solution)/shard_map/ppermute | solution.py:92
  216.8 25.4 %collective-permute-start.17 = (bf16[128,2048]{1,0:T(8,128)(2,1)S(1)}, bf16[128,2048]{1,0:T(8,128)(2,1)S(1)}, u32[]{:S(2)}, u32[]{:S(2)}) collective-permute-start(bf16[128,2048]{1,0:T(8,128)(2,1)S(1)} %get-tuple-element.184.refs_0_), channel_id=1, source_target_pairs={{0,2},{1,3},{2,4},{3,5},{4,6},{5,7},{6,0},{7,1},{8,10},{9,11},{10,... | collective-permute-start | bytes 1572872 | tf_op jit(solution)/shard_map/ppermute | solution.py:92
  243.2 15.1 %collective-permute-start.29 = (bf16[512,2048]{1,0:T(8,128)(2,1)S(1)}, bf16[512,2048]{1,0:T(8,128)(2,1)S(1)}, u32[]{:S(2)}, u32[]{:S(2)}) collective-permute-start(bf16[512,2048]{1,0:T(8,128)(2,1)S(1)} %convolution_convert_fusion.1), channel_id=1, source_target_pairs={{0,1},{1,0},{2,3},{3,2},{4,5},{5,4},{6,7},{7,6},{8,9},{9,8},{10,11... | collective-permute-start | bytes 6291464 | tf_op jit(solution)/shard_map/ppermute | solution.py:92
  264.3 20.7 %collective-permute-start.23 = (bf16[128,1536]{1,0:T(8,128)(2,1)}, bf16[128,1536]{1,0:T(8,128)(2,1)}, u32[]{:S(2)}, u32[]{:S(2)}) collective-permute-start(bf16[128,1536]{1,0:T(8,128)(2,1)} %get-tuple-element.193), channel_id=1, source_target_pairs={{0,2},{1,3},{2,4},{3,5},{4,6},{5,7},{6,0},{7,1},{8,10},{9,11},{10,... | collective-permute-start | bytes 1179656 | tf_op jit(solution)/shard_map/ppermute | solution.py:92
  288.1 20.4 %collective-permute-start.28 = (bf16[128,1536]{1,0:T(8,128)(2,1)S(1)}, bf16[128,1536]{1,0:T(8,128)(2,1)S(1)}, u32[]{:S(2)}, u32[]{:S(2)}) collective-permute-start(bf16[128,1536]{1,0:T(8,128)(2,1)S(1)} %pad_maximum_fusion.2.refs_8_), channel_id=1, source_target_pairs={{0,2},{1,3},{2,4},{3,5},{4,6},{5,7},{6,0},{7,1},{8,10},{9,11},{10,... | collective-permute-start | bytes 1179656 | tf_op jit(solution)/shard_map/ppermute | solution.py:92
  339.0 18.6 %all-to-all-start.2 = ((bf16[16,192,128]{2,1,0:T(8,128)(2,1)}), bf16[16,192,128]{2,1,0:T(8,128)(2,1)S(1)}, u32[]{:S(2)}, u32[]{:S(2)}) async-start(bf16[16,192,128]{2,1,0:T(8,128)(2,1)} %get-tuple-element.210), calls=%async_computation.2 | async-start | bytes 1572864 | tf_op jit(solution)/shard_map/all_to_all | solution.py:157
  381.6 27.7 %all-to-all-start.3 = ((bf16[16,384,128]{2,1,0:T(8,128)(2,1)}), bf16[16,384,128]{2,1,0:T(8,128)(2,1)S(1)}, u32[]{:S(2)}, u32[]{:S(2)}) async-start(bf16[16,384,128]{2,1,0:T(8,128)(2,1)} %pad_maximum_fusion), calls=%async_computation.3 | async-start | bytes 3145728 | tf_op jit(solution)/shard_map/all_to_all | solution.py:157
  410.7 32.5 %all-to-all-start.4 = ((bf16[16,384,128]{2,1,0:T(8,128)(2,1)}), bf16[16,384,128]{2,1,0:T(8,128)(2,1)S(1)}, u32[]{:S(2)}, u32[]{:S(2)}) async-start(bf16[16,384,128]{2,1,0:T(8,128)(2,1)} %copy-done.1), calls=%async_computation.4 | async-start | bytes 3145728 | tf_op jit(solution)/shard_map/all_to_all | solution.py:157
  415.0 23.2 %collective-permute-start.47 = (bf16[128,2048]{1,0:T(8,128)(2,1)}, bf16[128,2048]{1,0:T(8,128)(2,1)S(1)}, u32[]{:S(2)}, u32[]{:S(2)}) collective-permute-start(bf16[128,2048]{1,0:T(8,128)(2,1)} %get-tuple-element.252), channel_id=1, source_target_pairs={{0,6},{1,7},{2,0},{3,1},{4,2},{5,3},{6,4},{7,5},{8,14},{9,15},{10,... | collective-permute-start | bytes 1572872 | tf_op jit(solution)/shard_map/ppermute | solution.py:92
  415.1 23.1 %collective-permute-start.46 = (bf16[128,2048]{1,0:T(8,128)(2,1)}, bf16[128,2048]{1,0:T(8,128)(2,1)S(1)}, u32[]{:S(2)}, u32[]{:S(2)}) collective-permute-start(bf16[128,2048]{1,0:T(8,128)(2,1)} %get-tuple-element.251), channel_id=1, source_target_pairs={{0,4},{1,5},{2,6},{3,7},{4,0},{5,1},{6,2},{7,3},{8,12},{9,13},{10,... | collective-permute-start | bytes 1572872 | tf_op jit(solution)/shard_map/ppermute | solution.py:92
  416.0 26.0 %collective-permute-start.45 = (bf16[128,2048]{1,0:T(8,128)(2,1)S(1)}, bf16[128,2048]{1,0:T(8,128)(2,1)S(1)}, u32[]{:S(2)}, u32[]{:S(2)}) collective-permute-start(bf16[128,2048]{1,0:T(8,128)(2,1)S(1)} %copy-done.61), channel_id=1, source_target_pairs={{0,2},{1,3},{2,4},{3,5},{4,6},{5,7},{6,0},{7,1},{8,10},{9,11},{10,... | collective-permute-start | bytes 1572872 | tf_op jit(solution)/shard_map/ppermute | solution.py:92
  (116 other events, 1304.6 us)
Sparse Core Ops, SparseCore 0:
  17.6 31.4 all-gather.2
  50.8 33.5 all-gather.4
  184.0 83.9 reduce-scatter.6
  271.8 86.5 reduce-scatter.8
